TPU v7x, 32 devices: a whole 2x2x4 slice. The times are simulated.
32 devices in a mesh: groups: 2 (over y), cluster: 4 (over x, core), station: 4 (over z).
Axes of the slice: x: 2, y: 2, z: 4, core: 2. Of those that a mesh axis runs over, the one named last changes fastest.
Arguments:
- waveforms: float32 [256, 16, 3, 256], P(('groups', 'cluster'), 'station'), parts along dimension 0, may hold values from -120 to 120
- event_mask: int32 [256, 16], P(('groups', 'cluster'), 'station'), parts along dimension 0, may hold values 0 or 1
- station_weight: float32 [32], P('groups'), parts along dimension 0, may hold values from 0.01 to 10
- partners: int32 [4, 8], P(None, 'groups'), parts along dimension 1, may hold values from 0 to 3, as said below
- pair_list: int32 [4, 8, 256, 2], P(None, ('groups', 'cluster')), parts along dimension 1, may hold values from 0 to 31
- counts: int32 [8], P('groups'), parts along dimension 0, may hold values from 16 to 32, as said below
Outputs:
- stacked: float32 [4, 8, 256, 512], P(None, ('groups', 'cluster'), 'station'), parts along dimension 1
There are 2 independent parts, one for each index of `groups`. A program takes and returns all parts, laid end to end along the dimension named above; each array names one. Nothing has to cross between parts.
Inputs may be any that keep to these rules, and one draw needn't show every extreme that they name: `partners`: in every round each cluster is paired with itself or with one of its two neighbours on the cluster cycle (index plus or minus one, modulo 4), and the pairing is mutual. `counts`: event slots of a cluster at or above its count are padding. Every draw has a cluster holding 32 events and another holding 32 // 2.
All inputs are finite; a program needn't handle non-finite values. No bound on the sum of `event_mask` on one device may be relied on, other than what follows from the above.
Results may differ from a plain program's by a relative error of at most 0.0003.
Values sent between devices are 32-bit elements; how exact they have to be, the bound alone decides.
No kernel may reach another device: no remote copies, remote signals or barrier semaphores. Data moves between devices by JAX's collectives and lax.ppermute only.
A program may use at most 64 MiB of HBM per device.

v0:
```python
import math

import jax
import jax.numpy as jnp
from jax import lax
from jax.sharding import PartitionSpec as P

epsilon = 1e-06
HIGHEST = lax.Precision.HIGHEST


def passed_along(array, axis, by):
    length = lax.axis_size(axis)
    return lax.ppermute(array, axis, [(i, (i + by) % length) for i in range(length)])


def make_tables(seismogram_readings):
    record_duration = 2 * seismogram_readings
    time_points = jnp.arange(seismogram_readings, dtype=jnp.int32)
    rotation_radians = time_points[:, None] * time_points[None, :] % record_duration
    angles = rotation_radians.astype(jnp.float32) * (math.pi / seismogram_readings)
    forward = jnp.concatenate([jnp.cos(angles), -jnp.sin(angles)], axis=1)
    column = jnp.arange(record_duration, dtype=jnp.int32)
    delayed_seismograms = (column + seismogram_readings) % record_duration
    backward_rotation_radians = (
        time_points[:, None] * delayed_seismograms[None, :] % record_duration
    )
    angles_back = backward_rotation_radians.astype(jnp.float32) * (math.pi / seismogram_readings)
    normalizing_multiplier = (
        jnp.where(time_points == 0, 1.0, 2.0).astype(jnp.float32)[:, None] / record_duration
    )
    inverse = jnp.concatenate(
        [
            normalizing_multiplier * jnp.cos(angles_back),
            -normalizing_multiplier * jnp.sin(angles_back),
        ],
        axis=0,
    )
    return (forward, inverse)


def normalized(waveforms, event_mask):
    energy = jnp.sum(waveforms * waveforms, axis=-1, keepdims=True)
    scaled = waveforms * lax.rsqrt(energy + epsilon)
    return scaled * event_mask[:, :, None, None].astype(jnp.float32)


def transform(traces, forward):
    events, stations, channels, seismogram_readings = traces.shape
    flattened = traces.reshape(events * stations * channels, seismogram_readings)
    spectra = jnp.dot(flattened, forward, precision=HIGHEST, preferred_element_type=jnp.float32)
    return spectra.reshape(events, stations * channels, 2 * seismogram_readings)


def cross_block(own_side, other_side, first_index, second):
    half_width = own_side.shape[-1] // 2
    left_rows = jnp.take(own_side, first_index, axis=0)
    right_rows = jnp.take(other_side, second, axis=0)
    real_part = jnp.sum(
        left_rows[..., :half_width] * right_rows[..., :half_width]
        + left_rows[..., half_width:] * right_rows[..., half_width:],
        axis=1,
    )
    imag_part = jnp.sum(
        left_rows[..., half_width:] * right_rows[..., :half_width]
        - left_rows[..., :half_width] * right_rows[..., half_width:],
        axis=1,
    )
    return jnp.concatenate([real_part, imag_part], axis=-1)


def pair_spectra(own_side, other_side, pairs_now, valid_pairs):
    pair_count = pairs_now.shape[0]
    block_rows = math.gcd(pair_count, 64)
    firsts = pairs_now[:, 0].reshape(pair_count // block_rows, block_rows)
    seconds = pairs_now[:, 1].reshape(pair_count // block_rows, block_rows)

    def one_block(indices):
        return cross_block(own_side, other_side, indices[0], indices[1])

    stacked_rows = lax.map(one_block, (firsts, seconds)).reshape(pair_count, own_side.shape[-1])
    return stacked_rows * valid_pairs[:, None]


def on_device(waveforms, event_mask, station_weight, partners, pair_list, counts):
    events, stations, channels, seismogram_readings = waveforms.shape
    rounds_total = partners.shape[0]
    forward, inverse = make_tables(seismogram_readings)
    cluster_here = lax.axis_index("cluster")
    cluster_width = lax.axis_size("cluster")
    station_here = lax.axis_index("station")
    local_weight = lax.dynamic_slice_in_dim(station_weight, station_here * stations, stations)
    network_scale = 1.0 / (channels * jnp.sum(station_weight))
    unit_traces = normalized(waveforms, event_mask)
    own_spectra = transform(unit_traces, forward)
    weight_rows = jnp.repeat(local_weight, channels)
    weighted = own_spectra * weight_rows[None, :, None]
    partner_ids = partners[:, cluster_here]
    right_neighbour = (cluster_here + 1) % cluster_width
    traces_from_left = passed_along(unit_traces, "cluster", 1)
    traces_from_right = passed_along(unit_traces, "cluster", -1)
    both_sides = transform(jnp.concatenate([traces_from_left, traces_from_right], axis=0), forward)
    from_left = both_sides[:events]
    from_right = both_sides[events:]
    shares = []
    for turn_index in range(rounds_total):
        partner_now = partner_ids[turn_index]
        other_side = jnp.where(
            partner_now == cluster_here,
            own_spectra,
            jnp.where(partner_now == right_neighbour, from_right, from_left),
        )
        pairs_now = pair_list[turn_index, 0]
        own_count = counts[cluster_here]
        other_count = counts[partner_now]
        valid_pairs = ((pairs_now[:, 0] < own_count) & (pairs_now[:, 1] < other_count)).astype(
            jnp.float32
        )
        partial_value = pair_spectra(weighted, other_side, pairs_now, valid_pairs)
        shares.append(lax.psum_scatter(partial_value, "station", scatter_dimension=0, tiled=True))
    summed = jnp.stack(shares)
    share_rows = summed.shape[1]
    result = jnp.dot(
        summed.reshape(rounds_total * share_rows, 2 * seismogram_readings),
        inverse,
        precision=HIGHEST,
        preferred_element_type=jnp.float32,
    )
    return (result * network_scale).reshape(rounds_total, 1, share_rows, 2 * seismogram_readings)


def solution(mesh):
    return jax.shard_map(
        on_device,
        mesh=mesh,
        in_specs=(
            P(("groups", "cluster"), "station", None, None),
            P(("groups", "cluster"), "station"),
            P("groups"),
            P(None, "groups"),
            P(None, ("groups", "cluster"), None, None),
            P("groups"),
        ),
        out_specs=P(None, ("groups", "cluster"), "station", None),
        check_vma=False,
    )
```

profile of v0, /device:TPU:0, one launch (start us, length us, event | category | flops | bytes accessed | tf_op | source)
XLA Modules:
  0.0 267.3 jit_solution(18406320838458610675)
XLA Ops:
  10.2 2.0 collective-permute-start.1
  22.6 1.9 and_convert_fusion.2
  39.6 2.2 select_n.164
  41.8 5.9 %copy_select_fusion.3 = (f32[32,12,512]{2,0,1:T(8,128)S(1)}, f32[32,12,512]{2,0,1:T(8,128)}, f32[32,12,512]{2,0,1:T(8,128)}, f32[32,12,512]{2,0,1:T(8,128)}, f32[32,12,512]{2,0,1:T(8,128)S(1)}) fusion(f32[32,12,512]{2,1,0:T(8,128)S(1)} %select_n.146, pred[]{:T(512)S(6)} %eq.47, f32[32,12,512]{2,1,0:T(8,128)} %select_n.164, pred[]{:T(512)S(6)} %eq.53, ...), kind=kOutput, calls=%fused_computation.80 | convolution fusion | flops 605093888 | bytes 7995444 | tf_op jit(solution)/shard_map/dot_general | solution.py:51
  50.5 41.5 %while.40 = (s32[]{:T(128)}, f32[4,64,512]{2,1,0:T(8,128)}, s32[4,64]{1,0:T(4,128)S(1)}, f32[32,12,512]{2,1,0:T(8,128)S(1)}, s32[4,64]{1,0:T(4,128)S(1)}, /*index=5*/f32[32,12,512]{2,1,0:T(8,128)}, s32[]{:T(128)}) while((s32[]{:T(128)}, f32[4,64,512]{2,1,0:T(8,128)}, s32[4,64]{1,0:T(4,128)S(1)}, f32[32,12,512]{2,1,0:T(8,128)S(1)}, ...), condition=%wide.region_4.6_spmd, body=%wide.region_1.5_spmd.sunk | while | flops 2362114 | bytes 16132945 | solution.py:81
  50.5 2.0 gather_fusion.1
  54.3 3.3 %gather_fusion = f32[64,12,512]{2,1,0:T(8,128)} fusion(f32[32,12,512]{2,1,0:T(8,128)} %get-tuple-element.636, s32[1024]{0:T(1024)S(1)} %pad_clamp_fusion.16), kind=kCustom, calls=%fused_computation.1.clone.clone.1 | custom fusion | bytes 3145984 | tf_op jit(solution)/shard_map/while/body/eval_jaxpr/jit(_take)/gather | solution.py:58
  60.9 2.0 gather_fusion.1
  64.7 3.3 %gather_fusion = f32[64,12,512]{2,1,0:T(8,128)} fusion(f32[32,12,512]{2,1,0:T(8,128)} %get-tuple-element.636, s32[1024]{0:T(1024)S(1)} %pad_clamp_fusion.16), kind=kCustom, calls=%fused_computation.1.clone.clone.1 | custom fusion | bytes 3145984 | tf_op jit(solution)/shard_map/while/body/eval_jaxpr/jit(_take)/gather | solution.py:58
  71.2 2.0 gather_fusion.1
  75.1 3.3 %gather_fusion = f32[64,12,512]{2,1,0:T(8,128)} fusion(f32[32,12,512]{2,1,0:T(8,128)} %get-tuple-element.636, s32[1024]{0:T(1024)S(1)} %pad_clamp_fusion.16), kind=kCustom, calls=%fused_computation.1.clone.clone.1 | custom fusion | bytes 3145984 | tf_op jit(solution)/shard_map/while/body/eval_jaxpr/jit(_take)/gather | solution.py:58
  81.6 2.0 gather_fusion.1
  85.4 3.3 %gather_fusion = f32[64,12,512]{2,1,0:T(8,128)} fusion(f32[32,12,512]{2,1,0:T(8,128)} %get-tuple-element.636, s32[1024]{0:T(1024)S(1)} %pad_clamp_fusion.16), kind=kCustom, calls=%fused_computation.1.clone.clone.1 | custom fusion | bytes 3145984 | tf_op jit(solution)/shard_map/while/body/eval_jaxpr/jit(_take)/gather | solution.py:58
  91.9 2.0 bitcast_multiply_fusion.3
  96.6 41.5 %while.41 = (s32[]{:T(128)}, f32[4,64,512]{2,1,0:T(8,128)}, s32[4,64]{1,0:T(4,128)S(1)}, f32[32,12,512]{2,1,0:T(8,128)S(1)}, s32[4,64]{1,0:T(4,128)S(1)}, /*index=5*/f32[32,12,512]{2,1,0:T(8,128)}, s32[]{:T(128)}) while((s32[]{:T(128)}, f32[4,64,512]{2,1,0:T(8,128)}, s32[4,64]{1,0:T(4,128)S(1)}, f32[32,12,512]{2,1,0:T(8,128)S(1)}, ...), condition=%wide.region_9.11_spmd, body=%wide.region_6.10_spmd.sunk | while | flops 2362114 | bytes 16132945 | solution.py:81
  96.6 2.0 gather_fusion.3
  100.4 3.3 %gather_fusion.2 = f32[64,12,512]{2,1,0:T(8,128)} fusion(f32[32,12,512]{2,1,0:T(8,128)} %get-tuple-element.615, s32[1024]{0:T(1024)S(1)} %pad_clamp_fusion.18), kind=kCustom, calls=%fused_computation.3.clone.clone.1 | custom fusion | bytes 3145984 | tf_op jit(solution)/shard_map/while/body/eval_jaxpr/jit(_take)/gather | solution.py:58
  106.9 2.0 gather_fusion.3
  110.8 3.3 %gather_fusion.2 = f32[64,12,512]{2,1,0:T(8,128)} fusion(f32[32,12,512]{2,1,0:T(8,128)} %get-tuple-element.615, s32[1024]{0:T(1024)S(1)} %pad_clamp_fusion.18), kind=kCustom, calls=%fused_computation.3.clone.clone.1 | custom fusion | bytes 3145984 | tf_op jit(solution)/shard_map/while/body/eval_jaxpr/jit(_take)/gather | solution.py:58
  117.3 2.0 gather_fusion.3
  121.2 3.3 %gather_fusion.2 = f32[64,12,512]{2,1,0:T(8,128)} fusion(f32[32,12,512]{2,1,0:T(8,128)} %get-tuple-element.615, s32[1024]{0:T(1024)S(1)} %pad_clamp_fusion.18), kind=kCustom, calls=%fused_computation.3.clone.clone.1 | custom fusion | bytes 3145984 | tf_op jit(solution)/shard_map/while/body/eval_jaxpr/jit(_take)/gather | solution.py:58
  127.7 2.0 gather_fusion.3
  131.6 3.3 %gather_fusion.2 = f32[64,12,512]{2,1,0:T(8,128)} fusion(f32[32,12,512]{2,1,0:T(8,128)} %get-tuple-element.615, s32[1024]{0:T(1024)S(1)} %pad_clamp_fusion.18), kind=kCustom, calls=%fused_computation.3.clone.clone.1 | custom fusion | bytes 3145984 | tf_op jit(solution)/shard_map/while/body/eval_jaxpr/jit(_take)/gather | solution.py:58
  138.0 2.6 copy.60
  140.6 1.9 bitcast_multiply_fusion.2
  143.5 41.5 %while.42 = (s32[]{:T(128)}, f32[4,64,512]{2,1,0:T(8,128)}, s32[4,64]{1,0:T(4,128)S(1)}, f32[32,12,512]{2,1,0:T(8,128)S(1)}, s32[4,64]{1,0:T(4,128)S(1)}, /*index=5*/f32[32,12,512]{2,1,0:T(8,128)}, s32[]{:T(128)}) while((s32[]{:T(128)}, f32[4,64,512]{2,1,0:T(8,128)}, s32[4,64]{1,0:T(4,128)S(1)}, f32[32,12,512]{2,1,0:T(8,128)S(1)}, ...), condition=%wide.region_14.16_spmd, body=%wide.region_11.15_spmd.sunk | while | flops 2362114 | bytes 16132945 | solution.py:81
  143.5 2.0 gather_fusion.5
  147.4 3.3 %gather_fusion.4 = f32[64,12,512]{2,1,0:T(8,128)} fusion(f32[32,12,512]{2,1,0:T(8,128)} %get-tuple-element.594, s32[1024]{0:T(1024)S(1)} %pad_clamp_fusion.20), kind=kCustom, calls=%fused_computation.5.clone.clone.1 | custom fusion | bytes 3145984 | tf_op jit(solution)/shard_map/while/body/eval_jaxpr/jit(_take)/gather | solution.py:58
  153.9 2.0 gather_fusion.5
  157.8 3.3 %gather_fusion.4 = f32[64,12,512]{2,1,0:T(8,128)} fusion(f32[32,12,512]{2,1,0:T(8,128)} %get-tuple-element.594, s32[1024]{0:T(1024)S(1)} %pad_clamp_fusion.20), kind=kCustom, calls=%fused_computation.5.clone.clone.1 | custom fusion | bytes 3145984 | tf_op jit(solution)/shard_map/while/body/eval_jaxpr/jit(_take)/gather | solution.py:58
  164.3 2.0 gather_fusion.5
  168.1 3.3 %gather_fusion.4 = f32[64,12,512]{2,1,0:T(8,128)} fusion(f32[32,12,512]{2,1,0:T(8,128)} %get-tuple-element.594, s32[1024]{0:T(1024)S(1)} %pad_clamp_fusion.20), kind=kCustom, calls=%fused_computation.5.clone.clone.1 | custom fusion | bytes 3145984 | tf_op jit(solution)/shard_map/while/body/eval_jaxpr/jit(_take)/gather | solution.py:58
  174.7 2.0 gather_fusion.5
  178.5 3.3 %gather_fusion.4 = f32[64,12,512]{2,1,0:T(8,128)} fusion(f32[32,12,512]{2,1,0:T(8,128)} %get-tuple-element.594, s32[1024]{0:T(1024)S(1)} %pad_clamp_fusion.20), kind=kCustom, calls=%fused_computation.5.clone.clone.1 | custom fusion | bytes 3145984 | tf_op jit(solution)/shard_map/while/body/eval_jaxpr/jit(_take)/gather | solution.py:58
  185.0 2.6 copy.63
  187.6 1.9 bitcast_multiply_fusion.1
  190.4 41.5 %while.43 = (s32[]{:T(128)}, f32[4,64,512]{2,1,0:T(8,128)}, s32[4,64]{1,0:T(4,128)S(1)}, f32[32,12,512]{2,1,0:T(8,128)S(1)}, s32[4,64]{1,0:T(4,128)S(1)}, /*index=5*/f32[32,12,512]{2,1,0:T(8,128)}, s32[]{:T(128)}) while((s32[]{:T(128)}, f32[4,64,512]{2,1,0:T(8,128)}, s32[4,64]{1,0:T(4,128)S(1)}, f32[32,12,512]{2,1,0:T(8,128)S(1)}, ...), condition=%wide.region_19.21_spmd, body=%wide.region_16.20_spmd.sunk | while | flops 2362114 | bytes 16132945 | solution.py:81
  190.5 2.0 gather_fusion.7
  194.3 3.3 %gather_fusion.6 = f32[64,12,512]{2,1,0:T(8,128)} fusion(f32[32,12,512]{2,1,0:T(8,128)} %get-tuple-element.573, s32[1024]{0:T(1024)S(1)} %pad_clamp_fusion.22), kind=kCustom, calls=%fused_computation.7.clone.clone.1 | custom fusion | bytes 3145984 | tf_op jit(solution)/shard_map/while/body/eval_jaxpr/jit(_take)/gather | solution.py:58
  200.9 2.0 gather_fusion.7
  204.7 3.3 %gather_fusion.6 = f32[64,12,512]{2,1,0:T(8,128)} fusion(f32[32,12,512]{2,1,0:T(8,128)} %get-tuple-element.573, s32[1024]{0:T(1024)S(1)} %pad_clamp_fusion.22), kind=kCustom, calls=%fused_computation.7.clone.clone.1 | custom fusion | bytes 3145984 | tf_op jit(solution)/shard_map/while/body/eval_jaxpr/jit(_take)/gather | solution.py:58
  211.2 2.0 gather_fusion.7
  215.1 3.3 %gather_fusion.6 = f32[64,12,512]{2,1,0:T(8,128)} fusion(f32[32,12,512]{2,1,0:T(8,128)} %get-tuple-element.573, s32[1024]{0:T(1024)S(1)} %pad_clamp_fusion.22), kind=kCustom, calls=%fused_computation.7.clone.clone.1 | custom fusion | bytes 3145984 | tf_op jit(solution)/shard_map/while/body/eval_jaxpr/jit(_take)/gather | solution.py:58
  221.6 2.0 gather_fusion.7
  225.5 3.3 %gather_fusion.6 = f32[64,12,512]{2,1,0:T(8,128)} fusion(f32[32,12,512]{2,1,0:T(8,128)} %get-tuple-element.573, s32[1024]{0:T(1024)S(1)} %pad_clamp_fusion.22), kind=kCustom, calls=%fused_computation.7.clone.clone.1 | custom fusion | bytes 3145984 | tf_op jit(solution)/shard_map/while/body/eval_jaxpr/jit(_take)/gather | solution.py:58
  231.9 1.9 bitcast_multiply_fusion
  235.2 2.1 cosine_multiply_fusion
  237.4 20.3 %reduce-scatter.11.cloned.1.call-done = f32[64,512]{1,0:T(8,128)} async-done(((f32[256,512]{1,0:T(8,128)}), f32[64,512]{1,0:T(8,128)}) %reduce-scatter.11.cloned.1.call-update) | async-done | bytes 131088 | tf_op jit(solution)/shard_map/reduce_scatter | solution.py:120
  (181 shorter events, 107.9 us)
Async XLA Ops:
  6.5 5.7 %copy-start = (s32[4,4]{1,0:T(4,128)S(1)}, s32[4,4]{1,0:T(4,128)}, u32[]{:S(2)}) copy-start(s32[4,4]{1,0:T(4,128)} %param.19) | copy-start | bytes 196
  6.5 230.8 %reduce-scatter.5.cloned.1.call-start = ((), (), s32[]{:S(2)}) async-start(), calls=%async_computation.4 | async-start | bytes 655360 | tf_op jit(solution)/shard_map/reduce_scatter | solution.py:120
  9.7 25.5 %copy-start.3 = (f32[32,4,3,256]{3,0,2,1:T(8,128)}, f32[32,4,3,256]{3,0,2,1:T(8,128)S(1)}, u32[]{:S(2)}) copy-start(f32[32,4,3,256]{3,0,2,1:T(8,128)S(1)} %fusion.24) | copy-start | bytes 1179652
  9.7 24.4 %collective-permute-start = (f32[32,4,3,256]{3,0,2,1:T(8,128)S(1)}, f32[32,4,3,256]{3,0,2,1:T(8,128)S(1)}, u32[]{:S(2)}, u32[]{:S(2)}) collective-permute-start(f32[32,4,3,256]{3,0,2,1:T(8,128)S(1)} %fusion.24), channel_id=1, source_target_pairs={{0,4},{4,8},{8,12},{12,0},{1,5},{5,9},{9,13},{13,1},{2,6},{6,10},{... | collective-permute-start | bytes 1179656 | tf_op jit(solution)/shard_map/ppermute | solution.py:14
  10.2 23.9 %collective-permute-start.1 = (f32[32,4,3,256]{3,0,2,1:T(8,128)S(1)}, f32[32,4,3,256]{3,0,2,1:T(8,128)S(1)}, u32[]{:S(2)}, u32[]{:S(2)}) collective-permute-start(f32[32,4,3,256]{3,0,2,1:T(8,128)S(1)} %fusion.24), channel_id=1, source_target_pairs={{0,12},{4,0},{8,4},{12,8},{1,13},{5,1},{9,5},{13,9},{2,14},{6,2},{... | collective-permute-start | bytes 1179656 | tf_op jit(solution)/shard_map/ppermute | solution.py:14
  32.2 3.0 %copy-start.2 = (f32[256,256]{1,0:T(8,128)}, f32[256,256]{1,0:T(8,128)S(1)}, u32[]{:S(2)}) copy-start(f32[256,256]{1,0:T(8,128)S(1)} %get-tuple-element.355) | copy-start | bytes 786436
  91.9 2.3 copy-start.1
  94.0 143.4 %reduce-scatter.7.cloned.1.call-start = ((), (), s32[]{:S(2)}) async-start(), calls=%async_computation.5 | async-start | bytes 655360 | tf_op jit(solution)/shard_map/reduce_scatter | solution.py:120
  142.6 94.8 %reduce-scatter.9.cloned.1.call-start = ((), (), s32[]{:S(2)}) async-start(), calls=%async_computation.6 | async-start | bytes 655360 | tf_op jit(solution)/shard_map/reduce_scatter | solution.py:120
  189.5 68.2 %reduce-scatter.11.cloned.1.call-start = ((), (), s32[]{:S(2)}) async-start(), calls=%async_computation.7 | async-start | bytes 655360 | tf_op jit(solution)/shard_map/reduce_scatter | solution.py:120
  190.4 43.5 %copy-start.4 = (f32[16]{0:T(128)S(1)}, f32[16]{0:T(128)}, u32[]{:S(2)}) copy-start(f32[16]{0:T(128)} %param.18) | copy-start | bytes 196
Sparse Core Ops, SparseCore 0:
  94.1 23.6 reduce-scatter.4
  142.7 23.7 reduce-scatter.6
  189.7 23.7 reduce-scatter.8
  234.0 23.6 reduce-scatter.10
where the time goes:
time: 270 us; the launch traced here: 267 us
  local copies, waits for them, and re-layouts  106 us (39%)
  other arithmetic  102 us (38%)
  between operations  26.5 us (10%)
  waiting for transfers between devices  20.5 us (8%)
  matrix products  9.13 us (3%)
  starting transfers between devices  2.8 us (1%)
    gather x16, local copies, waits for them, and re-layouts, cross_block(): right_rows = jnp.take(other_side, second, axis=0)  52.1 us
    gather x16, local copies, waits for them, and re-layouts, cross_block(): left_rows = jnp.take(own_side, first_index, axis=0)  32.6 us
    select_n x16, other arithmetic, cross_block(): left_rows = jnp.take(own_side, first_index, axis=0)  28.8 us
    select_n x16, other arithmetic, cross_block(): right_rows = jnp.take(other_side, second, axis=0)  28.7 us
    reduce_scatter x4, waiting for transfers between devices, on_device(): lax.psum_scatter(partial_value, 'station', scatter_dimension=0, tiled=True)  20.4 us
    reduce_sum x16, other arithmetic, cross_block(): jnp.sum(left_rows[..., :half_width] * right_rows[..., :half_width] + left...  12 us
    mul x6, other arithmetic, pair_spectra(): return stacked_rows * valid_pairs[:, None]  11.7 us
    dynamic_update_slice x16, other arithmetic, pair_spectra(): lax.map(one_block, (firsts, seconds))  10.7 us
  transfers between devices with their start and end apart: 6, of which 1 were waited for; matrix products, arithmetic and copies ran while one was open for 57% of the time, Pallas kernels for 0%

commit v1 on v0

v1 whole, which is shorter than its diff:
```python
import math

import jax
import jax.numpy as jnp
import ml_dtypes
import numpy as np
from jax import lax
from jax.experimental import pallas as pl
from jax.experimental.pallas import tpu as pltpu
from jax.sharding import PartitionSpec as P

epsilon = 1e-06
SUB, LANES = 8, 128
HALF = SUB // 2
VMEM_BYTES = 40 * 1024 * 1024
F32 = jnp.float32
BF16 = jnp.bfloat16


def split_table(table):
    high = table.astype(ml_dtypes.bfloat16)
    low = (table - high.astype(np.float64)).astype(ml_dtypes.bfloat16)
    return high, low


def forward_table(samples):
    steps = np.arange(samples)
    angles = (steps[:, None] * steps[None, :] % (2 * samples)) * (math.pi / samples)
    return split_table(np.concatenate([np.cos(angles), -np.sin(angles)], axis=1))


def inverse_table(samples):
    record = 2 * samples
    bins = np.arange(samples)
    lags = (np.arange(record) + samples) % record
    angles = (bins[:, None] * lags[None, :] % record) * (math.pi / samples)
    gain = np.where(bins == 0, 1.0, 2.0)[:, None] / record
    return split_table(np.concatenate([gain * np.cos(angles), -gain * np.sin(angles)], axis=0))


def split_dot(value, high_ref, low_ref):
    high = value.astype(BF16)
    low = (value - high.astype(F32)).astype(BF16)
    total = jnp.dot(high, low_ref[...], preferred_element_type=F32)
    total += jnp.dot(low, high_ref[...], preferred_element_type=F32)
    return total + jnp.dot(high, high_ref[...], preferred_element_type=F32)


def prepare_kernel(waves_ref, mask_ref, weight_ref, out_ref):
    twos, _, _, stations, _ = waves_ref.shape
    events = 2 * twos
    rows = 3 * SUB * twos
    station_here = lax.axis_index("station")
    for parity in range(2):
        for channel in range(2):
            spot = channel * HALF
            out_ref[parity, :, spot : spot + HALF, :] = waves_ref[:, parity, channel]
        spot = parity * HALF
        out_ref[2, :, spot : spot + HALF, :] = waves_ref[:, parity, 2]
    station_id = lax.broadcasted_iota(jnp.int32, (stations, events), 0)
    weight = jnp.zeros((stations, events), F32)
    for station in range(stations):
        weight = jnp.where(station_id == station, weight_ref[station_here, station], weight)
    amplitude = mask_ref[...].astype(F32) * jnp.sqrt(weight)
    row = lax.broadcasted_iota(jnp.int32, (rows, events), 0)
    group, row_here = row // (SUB * twos), row % (SUB * twos)
    event_of_row = jnp.where(group < 2, 2 * (row_here // SUB) + group, row_here // HALF)
    event_id = lax.broadcasted_iota(jnp.int32, (rows, events), 1)
    picked = lax.dot_general(
        (event_of_row == event_id).astype(F32),
        amplitude,
        (((1,), (1,)), ((), ())),
        precision=lax.Precision.HIGHEST,
        preferred_element_type=F32,
    )
    row = lax.broadcasted_iota(jnp.int32, (rows, stations), 0)
    station_id = lax.broadcasted_iota(jnp.int32, (rows, stations), 1)
    factor = jnp.sum(jnp.where(row % HALF == station_id, picked, 0.0), axis=1, keepdims=True)
    traces = out_ref[...]
    energy = jnp.sum(traces * traces, axis=-1, keepdims=True)
    scale = lax.rsqrt(energy + epsilon) * factor.reshape(energy.shape)
    out_ref[...] = traces * scale


def prepare(waveforms, event_mask, station_weight):
    events, stations, channels, samples = waveforms.shape
    waves = jnp.transpose(waveforms, (0, 2, 1, 3)).reshape(events // 2, 2, channels, stations, samples)
    weights = station_weight.reshape(-1, stations)
    return pl.pallas_call(
        prepare_kernel,
        out_shape=jax.ShapeDtypeStruct((3, events // 2, SUB, samples), F32),
        in_specs=[
            pl.BlockSpec(memory_space=pltpu.VMEM),
            pl.BlockSpec(memory_space=pltpu.VMEM),
            pl.BlockSpec(memory_space=pltpu.SMEM),
        ],
        out_specs=pl.BlockSpec(memory_space=pltpu.VMEM),
        compiler_params=pltpu.CompilerParams(vmem_limit_bytes=VMEM_BYTES),
        name="prepare",
    )(waves, event_mask.T, weights)


def fill_spectra(traces_ref, high_ref, low_ref, spectra_ref, part):
    _, twos, _, samples = traces_ref.shape
    low_half = lax.broadcasted_iota(jnp.int32, (twos, SUB, LANES), 1) < HALF
    for parity in range(2):
        spectrum = split_dot(traces_ref[parity].reshape(twos * SUB, samples), high_ref, low_ref)
        for block in range(4):
            tile = spectrum[:, block * LANES : (block + 1) * LANES].reshape(twos, SUB, LANES)
            spectra_ref[part, :twos, parity, block + block // 2] = tile
    spectrum = split_dot(traces_ref[2].reshape(twos * SUB, samples), high_ref, low_ref)
    for side in range(2):
        spot = 2 * side * LANES
        lower = spectrum[:, spot : spot + LANES].reshape(twos, SUB, LANES)
        upper = spectrum[:, spot + LANES : spot + 2 * LANES].reshape(twos, SUB, LANES)
        turned_lower, turned_upper = pltpu.roll(lower, HALF, 1), pltpu.roll(upper, HALF, 1)
        spectra_ref[part, :twos, 0, 3 * side + 2] = jnp.where(low_half, lower, turned_upper)
        spectra_ref[part, :twos, 1, 3 * side + 2] = jnp.where(low_half, turned_lower, upper)


def cross_kernel(has_base, swap, *refs):
    partners_ref, counts_ref, pairs_ref, own_ref, sibling_ref, across_ref, high_ref, low_ref, *refs = refs
    if has_base:
        base_ref, *refs = refs
    *out_refs, spectra_ref, sums_ref = refs
    rounds, _, _, all_pairs = pairs_ref.shape
    twos = own_ref.shape[1]
    slots = 2 * (twos + 1)
    here = lax.axis_index("cluster")
    length = lax.axis_size("station")
    station_here = lax.axis_index("station")
    blocks = length // 2
    block_pairs = all_pairs // length
    sibling = jnp.where(here % 2 == 0, here + 1, here - 1)
    for part, traces_ref in enumerate((own_ref, sibling_ref, across_ref)):
        fill_spectra(traces_ref, high_ref, low_ref, spectra_ref, part)
    spectra_ref[0, twos] = jnp.zeros(spectra_ref.shape[2:], F32)
    flat_ref = spectra_ref.reshape(3 * slots, 6, SUB, LANES)
    own_count = counts_ref[here]
    low_half = lax.broadcasted_iota(jnp.int32, (SUB, LANES), 0) < HALF

    def folded(lower, upper, both):
        turned = pltpu.roll(jnp.where(low_half, upper, lower), HALF, 0)
        return jnp.where(low_half, lower, upper) + turned + both

    for turn in range(rounds):
        partner = partners_ref[turn, here]
        part = jnp.where(partner == here, 0, jnp.where(partner == sibling, slots, 2 * slots))
        partner_count = counts_ref[partner]
        for block in range(blocks):
            if blocks == 2:
                source = station_here if block == 0 else station_here + 1 - 2 * (station_here % 2)
            else:
                source = station_here // blocks * blocks + block
            start = source * block_pairs

            def one_pair(pair, carry):
                first = pairs_ref[turn, 0, 0, start + pair]
                second = pairs_ref[turn, 0, 1, start + pair]
                valid = (first < own_count) & (second < partner_count)
                left = flat_ref.at[jnp.where(valid, first, 2 * twos)]
                right = flat_ref.at[part + second]
                real, imag = [], []
                for tile in range(3):
                    left_real, left_imag = left[tile], left[tile + 3]
                    right_real, right_imag = right[tile], right[tile + 3]
                    real.append(left_real * right_real + left_imag * right_imag)
                    imag.append(left_imag * right_real - left_real * right_imag)
                spot = pl.multiple_of(pair * SUB, SUB)
                sums_ref[0, pl.ds(spot, SUB), :] = folded(*real)
                sums_ref[1, pl.ds(spot, SUB), :] = folded(*imag)
                return carry

            lax.fori_loop(0, block_pairs, one_pair, 0, unroll=8)
            out_ref = out_refs[block] if swap else out_refs[0]
            base_row = (turn * blocks + block) * block_pairs
            row = turn * block_pairs if swap else base_row
            for side in range(2):
                for half in range(2):
                    total = None
                    for lane_row in range(HALF):
                        piece = sums_ref[side, pl.ds(half * HALF + lane_row, block_pairs, stride=SUB), :]
                        total = piece if total is None else total + piece
                    column = (2 * side + half) * LANES
                    if has_base:
                        total += base_ref[base_row : base_row + block_pairs, column : column + LANES]
                    out_ref[row : row + block_pairs, column : column + LANES] = total


def cross_sums(scalars, traces, tables, base, swap):
    rounds, _, _, all_pairs = scalars[2].shape
    _, twos, _, samples = traces[0].shape
    length = lax.axis_size("station")
    half_rows = rounds * all_pairs // 2
    out_count = length // 2 if swap else 1
    block_pairs = all_pairs // length
    operands = [*scalars, *traces, *tables] + ([] if base is None else [base])
    vmem = pl.BlockSpec(memory_space=pltpu.VMEM)
    smem = pl.BlockSpec(memory_space=pltpu.SMEM)
    shape = jax.ShapeDtypeStruct((half_rows // out_count, 2 * samples), F32)
    return pl.pallas_call(
        lambda *refs: cross_kernel(base is not None, swap, *refs),
        out_shape=[shape] * out_count,
        in_specs=[smem] * 3 + [vmem] * (len(operands) - 3),
        out_specs=[vmem] * out_count,
        scratch_shapes=[
            pltpu.VMEM((3, twos + 1, 2, 6, SUB, LANES), F32),
            pltpu.VMEM((2, block_pairs * SUB, LANES), F32),
        ],
        compiler_params=pltpu.CompilerParams(vmem_limit_bytes=VMEM_BYTES),
        cost_estimate=pl.CostEstimate(flops=2 * 10**9, bytes_accessed=4 * 10**6, transcendentals=0),
        name="cross_sums",
    )(*operands)


def finish_kernel(channels, kept_ref, swapped_ref, weight_ref, high_ref, low_ref, out_ref):
    cross = kept_ref[...] + swapped_ref[...]
    scale = 1.0 / (channels * jnp.sum(weight_ref[...], axis=1, keepdims=True))
    out_ref[...] = split_dot(cross, high_ref, low_ref) * scale


def finish(channels, kept, swapped, station_weight, tables):
    return pl.pallas_call(
        lambda *refs: finish_kernel(channels, *refs),
        out_shape=jax.ShapeDtypeStruct(kept.shape, F32),
        compiler_params=pltpu.CompilerParams(vmem_limit_bytes=VMEM_BYTES),
        cost_estimate=pl.CostEstimate(flops=10**9, bytes_accessed=3 * 10**6, transcendentals=0),
        name="finish",
    )(kept, swapped, station_weight.reshape(1, -1), *tables)


def on_device(waveforms, event_mask, station_weight, partners, pair_list, counts):
    events, stations, channels, samples = waveforms.shape
    rounds, _, all_pairs, _ = pair_list.shape
    clusters = lax.axis_size("cluster")
    length = lax.axis_size("station")
    assert (stations, channels, samples) == (HALF, 3, 2 * LANES) and events % 2 == 0
    assert clusters % 2 == 0 and length % 4 == 0
    forward = [jnp.asarray(table) for table in forward_table(samples)]
    inverse = [jnp.asarray(table) for table in inverse_table(samples)]
    to_sibling = [(i, i ^ 1) for i in range(clusters)]
    to_across = [(i, (i + 1 if i % 2 else i - 1) % clusters) for i in range(clusters)]
    to_mirror = [(i, length - 1 - i) for i in range(length)]
    scalars = (partners, counts, jnp.transpose(pair_list, (0, 1, 3, 2)))

    own = prepare(waveforms, event_mask, station_weight)
    mirrored = lax.ppermute(own, "station", to_mirror)
    across = lax.ppermute(own, "cluster", to_across)
    sibling = lax.ppermute(own, "cluster", to_sibling)
    swap = length == 4
    (base,) = cross_sums(scalars, (own, sibling, across), forward, None, False)
    mirrored_across = lax.ppermute(mirrored, "cluster", to_across)
    mirrored_sibling = lax.ppermute(mirrored, "cluster", to_sibling)
    traces = (mirrored, mirrored_sibling, mirrored_across)
    if swap:
        kept, sent = cross_sums(scalars, traces, forward, base, True)
        received = lax.ppermute(sent, "station", [(i, i ^ 1) for i in range(length)])
    else:
        (partial,) = cross_sums(scalars, traces, forward, base, False)
        partial = partial.reshape(rounds, all_pairs // 2, 2 * samples)
        halves = np.arange(length).reshape(2, length // 2).tolist()
        kept = lax.psum_scatter(partial, "station", scatter_dimension=1, axis_index_groups=halves, tiled=True)
        kept = kept.reshape(-1, 2 * samples)
        received = jnp.zeros_like(kept)
    result = finish(channels, kept, received, station_weight, inverse)
    return result.reshape(rounds, 1, all_pairs // length, 2 * samples)


def solution(mesh):
    return jax.shard_map(
        on_device,
        mesh=mesh,
        in_specs=(
            P(("groups", "cluster"), "station", None, None),
            P(("groups", "cluster"), "station"),
            P("groups"),
            P(None, "groups"),
            P(None, ("groups", "cluster"), None, None),
            P("groups"),
        ),
        out_specs=P(None, ("groups", "cluster"), "station", None),
        check_vma=False,
    )
```

time: 270 us -> 57.7 us (0.21)
  local copies, waits for them, and re-layouts: 106 us -> 3.1 us
  other arithmetic: 102 us -> 0 us
  between operations: 26.5 us -> 0.09 us
  Pallas kernels: 0 us -> 14.2 us
  starting transfers between devices: 2.8 us -> 16.4 us
  matrix products: 9.13 us -> 0 us
  waiting for transfers between devices: 20.5 us -> 23.6 us
    gather x32 -> x0, local copies, waits for them, and re-layouts: 84.7 us -> none  [the longest x16 52.1 us: cross_block(): right_rows = jnp.take(other_side, second, axis=0)]
    select_n x34 -> x0, other arithmetic: 59.1 us -> none  [the longest x16 28.8 us: cross_block(): left_rows = jnp.take(own_side, first_index, axis=0)]
    ppermute x2 -> x6, waiting for transfers between devices: 0.01 us -> 23.6 us  [the longest x1 12.2 us: on_device(): lax.ppermute(sent, 'station', [(i, i ^ 1) for i in range(length)])]
    reduce_scatter x4 -> x0, waiting for transfers between devices: 20.4 us -> none  [on_device(): lax.psum_scatter(partial_value, 'station', scatter_dimension=0, tiled=True)]
    mul x8 -> x0, other arithmetic: 15 us -> none  [the longest x6 11.7 us: pair_spectra(): return stacked_rows * valid_pairs[:, None]]
    pallas_call x0 -> x4, Pallas kernels: none -> 14.2 us  [the longest x2 11.9 us: cross_sums(): pl.pallas_call(lambda *refs: cross_kernel(base is not None, swap, *refs),...]
    ppermute x2 -> x6, starting transfers between devices: 2.49 us -> 16.4 us  [the longest x1 8.09 us: on_device(): lax.ppermute(sent, 'station', [(i, i ^ 1) for i in range(length)])]
    reduce_sum x18 -> x0, other arithmetic: 13.8 us -> none  [the longest x16 12 us: cross_block(): jnp.sum(left_rows[..., :half_width] * right_rows[..., :half_width] + left...]
  transfers between devices with their start and end apart: 6 -> 6, of which waited for: 1 -> 4; matrix products, arithmetic and copies ran while one was open for 57% -> 0% of each run, Pallas kernels for 0% -> 10%
where the time goes in v1:
time: 57.7 us; the launch traced here: 57.5 us
  waiting for transfers between devices  23.6 us (41%)
  starting transfers between devices  16.4 us (28%)
  Pallas kernels  14.2 us (25%)
  local copies, waits for them, and re-layouts  3.1 us (5%)
    ppermute x1, waiting for transfers between devices, on_device(): lax.ppermute(sent, 'station', [(i, i ^ 1) for i in range(length)])  12.2 us
    pallas_call x2, Pallas kernels, cross_sums(): pl.pallas_call(lambda *refs: cross_kernel(base is not None, swap, *refs),...  11.9 us
    ppermute x1, starting transfers between devices, on_device(): lax.ppermute(sent, 'station', [(i, i ^ 1) for i in range(length)])  8.09 us
    ppermute x1, waiting for transfers between devices, on_device(): mirrored = lax.ppermute(own, 'station', to_mirror)  7.61 us
    ppermute x1, starting transfers between devices, on_device(): mirrored = lax.ppermute(own, 'station', to_mirror)  5.11 us
    ppermute x1, waiting for transfers between devices, on_device(): mirrored_across = lax.ppermute(mirrored, 'cluster', to_across)  3.24 us
    unnamed x20, local copies, waits for them, and re-layouts  2.36 us
    ppermute x1, starting transfers between devices, on_device(): mirrored_sibling = lax.ppermute(mirrored, 'cluster', to_sibling)  1.49 us
  transfers between devices with their start and end apart: 6, of which 4 were waited for; matrix products, arithmetic and copies ran while one was open for 0% of the time, Pallas kernels for 10%

profile of v1, /device:TPU:0, one launch (start us, length us, event | category | flops | bytes accessed | tf_op | source)
XLA Modules:
  0.0 57.5 jit_solution(4769514337240143554)
XLA Ops:
  0.0 0.7 %reshape.13.weight_ref = f32[4,4]{1,0:T(4,128)S(1)} reshape(f32[16]{0:T(128)} %param.12) | data formatting | bytes 128 | tf_op jit(solution)/shard_map/reshape | solution.py:88
  0.7 0.0 copy-start.1
  0.7 0.7 %copy-done.1 = s32[32,4]{0,1:T(4,128)S(1)} copy-done((s32[32,4]{0,1:T(4,128)S(1)}, s32[32,4]{0,1:T(4,128)}, u32[]{:S(2)}) %copy-start.1) | copy-done | bytes 536
  1.4 0.0 copy-start
  1.4 1.0 %copy-done = f32[32,4,3,256]{3,1,2,0:T(4,128)S(1)} copy-done((f32[32,4,3,256]{3,1,2,0:T(4,128)S(1)}, f32[32,4,3,256]{3,1,2,0:T(4,128)}, u32[]{:S(2)}) %copy-start) | copy-done | bytes 393240
  2.4 0.0 copy-start.3
  2.4 0.0 copy-start.4
  2.4 0.0 copy-start.8
  2.4 0.0 copy-start.9
  2.4 1.0 %prepare.1.refs_3_ = f32[3,16,8,256]{3,2,1,0:T(8,128)S(1)} custom-call(f32[16,2,3,4,256]{4,3,2,1,0:T(4,128)S(1)} %bitcast.9, s32[4,32]{1,0:T(4,128)S(1)} %bitcast.10, f32[4,4]{1,0:T(4,128)S(1)} %reshape.13.weight_ref), custom_call_target="tpu_custom_call" | custom-call | tf_op jit(solution)/shard_map/prepare/pallas_call | solution.py:89
  3.4 0.0 copy-start.5
  3.4 5.1 %collective-permute-start = (f32[3,16,8,256]{3,2,1,0:T(8,128)S(1)}, f32[3,16,8,256]{3,2,1,0:T(8,128)S(1)}, u32[]{:S(2)}, u32[]{:S(2)}) collective-permute-start(f32[3,16,8,256]{3,2,1,0:T(8,128)S(1)} %prepare.1.refs_3_), channel_id=1, source_target_pairs={{0,3},{1,2},{2,1},{3,0},{4,7},{5,6},{6,5},{7,4},{8,11},{9,10},{10,... | collective-permute-start | bytes 1179656 | tf_op jit(solution)/shard_map/ppermute | solution.py:247
  8.5 0.7 %collective-permute-start.4 = (f32[3,16,8,256]{3,2,1,0:T(8,128)S(1)}, f32[3,16,8,256]{3,2,1,0:T(8,128)S(1)}, u32[]{:S(2)}, u32[]{:S(2)}) collective-permute-start(f32[3,16,8,256]{3,2,1,0:T(8,128)S(1)} %prepare.1.refs_3_), channel_id=1, source_target_pairs={{0,12},{4,8},{8,4},{12,0},{1,13},{5,9},{9,5},{13,1},{2,14},{6,10},... | collective-permute-start | bytes 1179656 | tf_op jit(solution)/shard_map/ppermute | solution.py:248
  9.2 1.0 %collective-permute-start.3 = (f32[3,16,8,256]{3,2,1,0:T(8,128)S(1)}, f32[3,16,8,256]{3,2,1,0:T(8,128)S(1)}, u32[]{:S(2)}, u32[]{:S(2)}) collective-permute-start(f32[3,16,8,256]{3,2,1,0:T(8,128)S(1)} %prepare.1.refs_3_), channel_id=1, source_target_pairs={{0,4},{4,0},{8,12},{12,8},{1,5},{5,1},{9,13},{13,9},{2,6},{6,2},{1... | collective-permute-start | bytes 1179656 | tf_op jit(solution)/shard_map/ppermute | solution.py:249
  10.1 7.6 %collective-permute-done.refs_3_ = f32[3,16,8,256]{3,2,1,0:T(8,128)S(1)} collective-permute-done((f32[3,16,8,256]{3,2,1,0:T(8,128)S(1)}, f32[3,16,8,256]{3,2,1,0:T(8,128)S(1)}, u32[]{:S(2)}, u32[]{:S(2)}) %collective-permute-start) | collective-permute-done | bytes 393248 | tf_op jit(solution)/shard_map/ppermute | solution.py:247
  17.8 0.1 collective-permute-start.2
  17.9 1.5 %collective-permute-start.1 = (f32[3,16,8,256]{3,2,1,0:T(8,128)S(1)}, f32[3,16,8,256]{3,2,1,0:T(8,128)S(1)}, u32[]{:S(2)}, u32[]{:S(2)}) collective-permute-start(f32[3,16,8,256]{3,2,1,0:T(8,128)S(1)} %collective-permute-done.refs_3_), channel_id=1, source_target_pairs={{0,4},{4,0},{8,12},{12,8},{1,5},{5,1},{9,13},{13,9},{2,6},{6,2},{1... | collective-permute-start | bytes 1179656 | tf_op jit(solution)/shard_map/ppermute | solution.py:253
  19.4 0.5 collective-permute-done.4.refs_5_
  19.9 0.0 collective-permute-done.3.refs_4_
  19.9 0.0 copy-done.3
  19.9 0.0 copy-done.4
  19.9 0.0 copy-done.8
  19.9 0.0 copy-done.9
  19.9 0.0 copy-done.5
  19.9 5.9 %cross_sums.2.refs_8_ = f32[512,512]{1,0:T(8,128)S(1)} custom-call(s32[4,4]{1,0:T(4,128)S(1)} %copy-done.4, s32[4]{0:T(128)S(1)} %copy-done.5, s32[4,1,2,256]{3,2,1,0:T(2,128)S(1)} %bitcast.12, f32[3,16,8,256]{3,2,1,0:T(8,128)S(1)} %prepare.1.refs_3_, f32[3,16,8,256]{3,2,1,0:T(8,128)S(1)} %collective-permute-done.3.refs_4_, ...), custom_call_target="tpu_custom_call" | custom-call | flops 2000000000 | bytes 4000000 | tf_op jit(solution)/shard_map/cross_sums/pallas_call | solution.py:201
  25.9 0.0 copy-start.6
  25.9 0.0 copy-start.7
  25.9 3.2 %collective-permute-done.2.refs_5_ = f32[3,16,8,256]{3,2,1,0:T(8,128)S(1)} collective-permute-done((f32[3,16,8,256]{3,2,1,0:T(8,128)S(1)}, f32[3,16,8,256]{3,2,1,0:T(8,128)S(1)}, u32[]{:S(2)}, u32[]{:S(2)}) %collective-permute-start.2) | collective-permute-done | bytes 393248 | tf_op jit(solution)/shard_map/ppermute | solution.py:252
  29.1 0.0 collective-permute-done.1.refs_4_
  29.1 6.0 %cross_sums.3 = (f32[256,512]{1,0:T(8,128)S(1)}, f32[256,512]{1,0:T(8,128)S(1)}) custom-call(s32[4,4]{1,0:T(4,128)S(1)} %copy-done.4, s32[4]{0:T(128)S(1)} %copy-done.5, s32[4,1,2,256]{3,2,1,0:T(2,128)S(1)} %bitcast.13, f32[3,16,8,256]{3,2,1,0:T(8,128)S(1)} %collective-permute-done.refs_3_, f32[3,16,8,256]{3,2,1,0:T(8,128)S(1)} %collective-permute-done.1.refs_4_, ...), custom_call_target="tpu_custom_call" | custom-call | flops 2000000000 | bytes 4000000 | tf_op jit(solution)/shard_map/cross_sums/pallas_call | solution.py:201
  35.1 8.1 %collective-permute-start.5 = (f32[256,512]{1,0:T(8,128)S(1)}, f32[256,512]{1,0:T(8,128)S(1)}, u32[]{:S(2)}, u32[]{:S(2)}) collective-permute-start(f32[256,512]{1,0:T(8,128)S(1)} %get-tuple-element.8), channel_id=1, source_target_pairs={{0,1},{1,0},{2,3},{3,2},{4,5},{5,4},{6,7},{7,6},{8,9},{9,8},{10,11... | collective-permute-start | bytes 1572872 | tf_op jit(solution)/shard_map/ppermute | solution.py:257
  43.2 12.2 %collective-permute-done.5.refs_1_ = f32[256,512]{1,0:T(8,128)S(1)} collective-permute-done((f32[256,512]{1,0:T(8,128)S(1)}, f32[256,512]{1,0:T(8,128)S(1)}, u32[]{:S(2)}, u32[]{:S(2)}) %collective-permute-start.5) | collective-permute-done | bytes 524320 | tf_op jit(solution)/shard_map/ppermute | solution.py:257
  55.4 0.0 copy-start.2
  55.4 0.0 copy-done.6
  55.4 0.0 copy-done.7
  55.4 0.6 %copy-done.2 = f32[16]{0:T(128)S(1)} copy-done((f32[16]{0:T(128)S(1)}, f32[16]{0:T(128)}, u32[]{:S(2)}) %copy-start.2) | copy-done | bytes 88
  56.1 1.4 %finish.1 = f32[256,512]{1,0:T(8,128)} custom-call(f32[256,512]{1,0:T(8,128)S(1)} %get-tuple-element.7.refs_0_, f32[256,512]{1,0:T(8,128)S(1)} %collective-permute-done.5.refs_1_, f32[1,16]{1,0:T(1,128)S(1)} %bitcast.11, bf16[512,512]{1,0:T(8,128)(2,1)S(1)} %copy-done.7, bf16[512,512]{1,0:T(8,128)(2,1)S(1)} %copy-done.6), custom_call_target="tpu_custom_call" | custom-call | flops 1000000000 | bytes 3000000 | tf_op jit(solution)/shard_map/finish/pallas_call | solution.py:223
Async XLA Ops:
  0.7 0.7 %copy-start.1 = (s32[32,4]{0,1:T(4,128)S(1)}, s32[32,4]{0,1:T(4,128)}, u32[]{:S(2)}) copy-start(s32[32,4]{0,1:T(4,128)} %param.11) | copy-start | bytes 1540
  1.4 1.0 %copy-start = (f32[32,4,3,256]{3,1,2,0:T(4,128)S(1)}, f32[32,4,3,256]{3,1,2,0:T(4,128)}, u32[]{:S(2)}) copy-start(f32[32,4,3,256]{3,1,2,0:T(4,128)} %param.10) | copy-start | bytes 1179652
  2.4 17.5 %copy-start.3 = (s32[4,1,256,2]{2,3,1,0:T(2,128)S(1)}, s32[4,1,256,2]{2,3,1,0:T(2,128)}, u32[]{:S(2)}) copy-start(s32[4,1,256,2]{2,3,1,0:T(2,128)} %param.14) | copy-start | bytes 24580
  2.4 17.5 %copy-start.4 = (s32[4,4]{1,0:T(4,128)S(1)}, s32[4,4]{1,0:T(4,128)}, u32[]{:S(2)}) copy-start(s32[4,4]{1,0:T(4,128)} %refs_0_.3) | copy-start | bytes 196
  2.4 17.5 %copy-start.8 = (bf16[256,512]{1,0:T(8,128)(2,1)S(1)}, bf16[256,512]{1,0:T(8,128)(2,1)}, u32[]{:S(2)}) copy-start(bf16[256,512]{1,0:T(8,128)(2,1)} %constant.9.clone.refs_7_) | copy-start | bytes 786436
  2.4 17.5 %copy-start.9 = (bf16[256,512]{1,0:T(8,128)(2,1)S(1)}, bf16[256,512]{1,0:T(8,128)(2,1)}, u32[]{:S(2)}) copy-start(bf16[256,512]{1,0:T(8,128)(2,1)} %constant.8.clone.refs_6_) | copy-start | bytes 786436
  3.4 16.5 %copy-start.5 = (s32[4]{0:T(128)S(1)}, s32[4]{0:T(128)}, u32[]{:S(2)}) copy-start(s32[4]{0:T(128)} %refs_1_.3) | copy-start | bytes 52
  3.4 14.3 %collective-permute-start = (f32[3,16,8,256]{3,2,1,0:T(8,128)S(1)}, f32[3,16,8,256]{3,2,1,0:T(8,128)S(1)}, u32[]{:S(2)}, u32[]{:S(2)}) collective-permute-start(f32[3,16,8,256]{3,2,1,0:T(8,128)S(1)} %prepare.1.refs_3_), channel_id=1, source_target_pairs={{0,3},{1,2},{2,1},{3,0},{4,7},{5,6},{6,5},{7,4},{8,11},{9,10},{10,... | collective-permute-start | bytes 1179656 | tf_op jit(solution)/shard_map/ppermute | solution.py:247
  8.5 11.4 %collective-permute-start.4 = (f32[3,16,8,256]{3,2,1,0:T(8,128)S(1)}, f32[3,16,8,256]{3,2,1,0:T(8,128)S(1)}, u32[]{:S(2)}, u32[]{:S(2)}) collective-permute-start(f32[3,16,8,256]{3,2,1,0:T(8,128)S(1)} %prepare.1.refs_3_), channel_id=1, source_target_pairs={{0,12},{4,8},{8,4},{12,0},{1,13},{5,9},{9,5},{13,1},{2,14},{6,10},... | collective-permute-start | bytes 1179656 | tf_op jit(solution)/shard_map/ppermute | solution.py:248
  9.2 10.7 %collective-permute-start.3 = (f32[3,16,8,256]{3,2,1,0:T(8,128)S(1)}, f32[3,16,8,256]{3,2,1,0:T(8,128)S(1)}, u32[]{:S(2)}, u32[]{:S(2)}) collective-permute-start(f32[3,16,8,256]{3,2,1,0:T(8,128)S(1)} %prepare.1.refs_3_), channel_id=1, source_target_pairs={{0,4},{4,0},{8,12},{12,8},{1,5},{5,1},{9,13},{13,9},{2,6},{6,2},{1... | collective-permute-start | bytes 1179656 | tf_op jit(solution)/shard_map/ppermute | solution.py:249
  17.8 11.4 %collective-permute-start.2 = (f32[3,16,8,256]{3,2,1,0:T(8,128)S(1)}, f32[3,16,8,256]{3,2,1,0:T(8,128)S(1)}, u32[]{:S(2)}, u32[]{:S(2)}) collective-permute-start(f32[3,16,8,256]{3,2,1,0:T(8,128)S(1)} %collective-permute-done.refs_3_), channel_id=1, source_target_pairs={{0,12},{4,8},{8,4},{12,0},{1,13},{5,9},{9,5},{13,1},{2,14},{6,10},... | collective-permute-start | bytes 1179656 | tf_op jit(solution)/shard_map/ppermute | solution.py:252
  17.9 11.3 %collective-permute-start.1 = (f32[3,16,8,256]{3,2,1,0:T(8,128)S(1)}, f32[3,16,8,256]{3,2,1,0:T(8,128)S(1)}, u32[]{:S(2)}, u32[]{:S(2)}) collective-permute-start(f32[3,16,8,256]{3,2,1,0:T(8,128)S(1)} %collective-permute-done.refs_3_), channel_id=1, source_target_pairs={{0,4},{4,0},{8,12},{12,8},{1,5},{5,1},{9,13},{13,9},{2,6},{6,2},{1... | collective-permute-start | bytes 1179656 | tf_op jit(solution)/shard_map/ppermute | solution.py:253
  25.9 29.6 %copy-start.6 = (bf16[512,512]{1,0:T(8,128)(2,1)S(1)}, bf16[512,512]{1,0:T(8,128)(2,1)}, u32[]{:S(2)}) copy-start(bf16[512,512]{1,0:T(8,128)(2,1)} %constant.11.clone.refs_4_) | copy-start | bytes 1572868
  25.9 29.6 %copy-start.7 = (bf16[512,512]{1,0:T(8,128)(2,1)S(1)}, bf16[512,512]{1,0:T(8,128)(2,1)}, u32[]{:S(2)}) copy-start(bf16[512,512]{1,0:T(8,128)(2,1)} %constant.10.clone.refs_3_) | copy-start | bytes 1572868
  35.1 20.3 %collective-permute-start.5 = (f32[256,512]{1,0:T(8,128)S(1)}, f32[256,512]{1,0:T(8,128)S(1)}, u32[]{:S(2)}, u32[]{:S(2)}) collective-permute-start(f32[256,512]{1,0:T(8,128)S(1)} %get-tuple-element.8), channel_id=1, source_target_pairs={{0,1},{1,0},{2,3},{3,2},{4,5},{5,4},{6,7},{7,6},{8,9},{9,8},{10,11... | collective-permute-start | bytes 1572872 | tf_op jit(solution)/shard_map/ppermute | solution.py:257
  55.4 0.7 %copy-start.2 = (f32[16]{0:T(128)S(1)}, f32[16]{0:T(128)}, u32[]{:S(2)}) copy-start(f32[16]{0:T(128)} %param.12) | copy-start | bytes 196

commit v2 on v1

v2 whole, which is shorter than its diff:
```python
import math

import jax
import jax.numpy as jnp
import ml_dtypes
import numpy as np
from jax import lax
from jax.experimental import pallas as pl
from jax.experimental.pallas import tpu as pltpu
from jax.sharding import PartitionSpec as P

epsilon = 1e-06
SUB, LANES = 8, 128
HALF = SUB // 2
VMEM_BYTES = 40 * 1024 * 1024
F32 = jnp.float32
BF16 = jnp.bfloat16


def split_table(table):
    high = table.astype(ml_dtypes.bfloat16)
    low = (table - high.astype(np.float64)).astype(ml_dtypes.bfloat16)
    return high, low


def forward_table(samples):
    steps = np.arange(samples)
    angles = (steps[:, None] * steps[None, :] % (2 * samples)) * (math.pi / samples)
    return split_table(np.concatenate([np.cos(angles), -np.sin(angles)], axis=1))


def inverse_table(samples):
    record = 2 * samples
    bins = np.arange(samples)
    lags = (np.arange(record) + samples) % record
    angles = (bins[:, None] * lags[None, :] % record) * (math.pi / samples)
    gain = np.where(bins == 0, 1.0, 2.0)[:, None] / record
    return split_table(np.concatenate([gain * np.cos(angles), -gain * np.sin(angles)], axis=0))


def split_dot(value, high_ref, low_ref):
    high = value.astype(BF16)
    low = (value - high.astype(F32)).astype(BF16)
    total = jnp.dot(high, low_ref[...], preferred_element_type=F32)
    total += jnp.dot(low, high_ref[...], preferred_element_type=F32)
    return total + jnp.dot(high, high_ref[...], preferred_element_type=F32)


def prepare_kernel(waves_hbm, mask_hbm, weight_ref, all_ref, first_ref, rest_ref, waves_ref, mask_ref, sems):
    waves_copy = pltpu.make_async_copy(waves_hbm, waves_ref, sems.at[0])
    mask_copy = pltpu.make_async_copy(mask_hbm, mask_ref, sems.at[1])
    waves_copy.start()
    mask_copy.start()
    twos, _, _, stations, _ = waves_ref.shape
    events = 2 * twos
    rows = 3 * SUB * twos
    first_weight = lax.axis_index("station") * stations
    station_id = lax.broadcasted_iota(jnp.int32, (stations, events), 0)
    weight = jnp.zeros((stations, events), F32)
    for station in range(stations):
        weight = jnp.where(station_id == station, weight_ref[first_weight + station], weight)
    row = lax.broadcasted_iota(jnp.int32, (rows, events), 0)
    group, row_here = row // (SUB * twos), row % (SUB * twos)
    event_of_row = jnp.where(group < 2, 2 * (row_here // SUB) + group, row_here // HALF)
    event_id = lax.broadcasted_iota(jnp.int32, (rows, events), 1)
    at_event = (event_of_row == event_id).astype(F32)
    row = lax.broadcasted_iota(jnp.int32, (rows, stations), 0)
    at_station = row % HALF == lax.broadcasted_iota(jnp.int32, (rows, stations), 1)
    mask_copy.wait()
    amplitude = mask_ref[...].astype(F32) * jnp.sqrt(weight)
    picked = lax.dot_general(
        at_event,
        amplitude,
        (((1,), (1,)), ((), ())),
        precision=lax.Precision.HIGHEST,
        preferred_element_type=F32,
    )
    factor = jnp.sum(jnp.where(at_station, picked, 0.0), axis=1, keepdims=True)
    waves_copy.wait()
    for parity in range(2):
        for channel in range(2):
            spot = channel * HALF
            all_ref[parity, :, spot : spot + HALF, :] = waves_ref[:, parity, channel]
        spot = parity * HALF
        all_ref[2, :, spot : spot + HALF, :] = waves_ref[:, parity, 2]
    traces = all_ref[...]
    energy = jnp.sum(traces * traces, axis=-1, keepdims=True)
    traces = traces * (lax.rsqrt(energy + epsilon) * factor.reshape(energy.shape))
    all_ref[...] = traces
    first_ref[...] = traces[:2]
    rest_ref[...] = traces[2:]


def prepare(waveforms, event_mask, station_weight):
    events, stations, channels, samples = waveforms.shape
    waves = jnp.transpose(waveforms, (0, 2, 1, 3)).reshape(events // 2, 2, channels, stations, samples)
    hbm = pl.BlockSpec(memory_space=pltpu.HBM)
    vmem = pl.BlockSpec(memory_space=pltpu.VMEM)
    return pl.pallas_call(
        prepare_kernel,
        out_shape=[jax.ShapeDtypeStruct((parts, events // 2, SUB, samples), F32) for parts in (3, 2, 1)],
        in_specs=[hbm, hbm, pl.BlockSpec(memory_space=pltpu.SMEM)],
        out_specs=[vmem] * 3,
        scratch_shapes=[
            pltpu.VMEM(waves.shape, F32),
            pltpu.VMEM((stations, events), event_mask.dtype),
            pltpu.SemaphoreType.DMA((2,)),
        ],
        compiler_params=pltpu.CompilerParams(vmem_limit_bytes=VMEM_BYTES),
        name="prepare",
    )(waves, event_mask.T, station_weight)


def fill_spectra(trace_refs, high_ref, low_ref, spectra_ref, part):
    pieces = [(ref, index) for ref in trace_refs for index in range(ref.shape[0])]
    _, twos, _, samples = trace_refs[0].shape
    low_half = lax.broadcasted_iota(jnp.int32, (twos, SUB, LANES), 1) < HALF
    for parity in range(2):
        ref, index = pieces[parity]
        spectrum = split_dot(ref[index].reshape(twos * SUB, samples), high_ref, low_ref)
        for block in range(4):
            tile = spectrum[:, block * LANES : (block + 1) * LANES].reshape(twos, SUB, LANES)
            spectra_ref[part, :twos, parity, block + block // 2] = tile
    ref, index = pieces[2]
    spectrum = split_dot(ref[index].reshape(twos * SUB, samples), high_ref, low_ref)
    for side in range(2):
        spot = 2 * side * LANES
        lower = spectrum[:, spot : spot + LANES].reshape(twos, SUB, LANES)
        upper = spectrum[:, spot + LANES : spot + 2 * LANES].reshape(twos, SUB, LANES)
        turned_lower, turned_upper = pltpu.roll(lower, HALF, 1), pltpu.roll(upper, HALF, 1)
        spectra_ref[part, :twos, 0, 3 * side + 2] = jnp.where(low_half, lower, turned_upper)
        spectra_ref[part, :twos, 1, 3 * side + 2] = jnp.where(low_half, turned_lower, upper)
    if part == 0:
        spectra_ref[0, twos] = jnp.zeros(spectra_ref.shape[2:], F32)


def add_pairs(scalar_refs, turns, wanted, spectra_ref, base_refs, out_refs, sums_ref):
    partners_ref, counts_ref, pairs_ref = scalar_refs
    _, _, _, all_pairs = pairs_ref.shape
    slots = 2 * spectra_ref.shape[1]
    here = lax.axis_index("cluster")
    length = lax.axis_size("station")
    station_here = lax.axis_index("station")
    blocks = length // 2
    block_pairs = all_pairs // length
    sibling = jnp.where(here % 2 == 0, here + 1, here - 1)
    flat_ref = spectra_ref.reshape(spectra_ref.shape[0] * slots, 6, SUB, LANES)
    own_count = counts_ref[here]
    low_half = lax.broadcasted_iota(jnp.int32, (SUB, LANES), 0) < HALF

    def folded(lower, upper, both):
        turned = pltpu.roll(jnp.where(low_half, upper, lower), HALF, 0)
        return jnp.where(low_half, lower, upper) + turned + both

    def one_turn(place, turn, partner, part):
        partner_count = counts_ref[partner]
        for block in range(blocks):
            if len(out_refs) == 2:
                source = station_here if block == 0 else station_here + 1 - 2 * (station_here % 2)
            else:
                source = station_here // blocks * blocks + block
            start = source * block_pairs

            def one_pair(pair, carry):
                first = pairs_ref[turn, 0, 0, start + pair]
                second = pairs_ref[turn, 0, 1, start + pair]
                valid = (first < own_count) & (second < partner_count)
                left = flat_ref.at[jnp.where(valid, first, slots - 2)]
                right = flat_ref.at[part * slots + second]
                real, imag = [], []
                for tile in range(3):
                    left_real, left_imag = left[tile], left[tile + 3]
                    right_real, right_imag = right[tile], right[tile + 3]
                    real.append(left_real * right_real + left_imag * right_imag)
                    imag.append(left_imag * right_real - left_real * right_imag)
                spot = pl.multiple_of(pair * SUB, SUB)
                sums_ref[0, pl.ds(spot, SUB), :] = folded(*real)
                sums_ref[1, pl.ds(spot, SUB), :] = folded(*imag)
                return carry

            lax.fori_loop(0, block_pairs, one_pair, 0, unroll=min(16, block_pairs))
            if len(out_refs) == 2:
                which, row = block, place * block_pairs
            else:
                which, row = 0, (place * blocks + block) * block_pairs
            for side in range(2):
                for half in range(2):
                    spot = pl.ds((2 * side + half) * LANES, LANES)
                    total = None if base_refs is None else base_refs[which][row : row + block_pairs, spot]
                    for lane_row in range(HALF):
                        piece = sums_ref[side, pl.ds(half * HALF + lane_row, block_pairs, stride=SUB), :]
                        total = piece if total is None else total + piece
                    out_refs[which][row : row + block_pairs, spot] = total

    for place, turn in enumerate(turns):
        partner = partners_ref[turn, here]
        part = jnp.where(partner == here, 0, jnp.where(partner == sibling, 1, 2))
        if wanted is None:
            one_turn(place, turn, partner, part)
        else:
            pl.when(wanted(part))(lambda: one_turn(place, turn, partner, part))


def half_turns(rounds, half):
    return range(half * rounds // 2, (half + 1) * rounds // 2)


def first_sums_kernel(outs, *refs):
    scalar_refs, (own, sibling, across, high, low), refs = refs[:3], refs[3:8], refs[8:]
    out_refs, (spectra_ref, sums_ref) = refs[: 2 * outs], refs[2 * outs :]
    for part, traces in enumerate((own, sibling, across)):
        fill_spectra([traces], high, low, spectra_ref, part)
    for half in range(2):
        turns = half_turns(scalar_refs[2].shape[0], half)
        add_pairs(scalar_refs, turns, None, spectra_ref, None, out_refs[half * outs : (half + 1) * outs], sums_ref)


def near_sums_kernel(outs, *refs):
    scalar_refs, (own_a, own_b, sibling_a, sibling_b, high, low), refs = refs[:3], refs[3:9], refs[9:]
    base_refs, refs = refs[: 2 * outs], refs[2 * outs :]
    spectra_ref, out_refs, sums_ref = refs[0], refs[1:-1], refs[-1]
    fill_spectra([own_a, own_b], high, low, spectra_ref, 0)
    fill_spectra([sibling_a, sibling_b], high, low, spectra_ref, 1)
    for half in range(2):
        turns = half_turns(scalar_refs[2].shape[0], half)
        some = slice(half * outs, (half + 1) * outs)
        add_pairs(
            scalar_refs, turns, lambda part: part < 2, spectra_ref, base_refs[some], out_refs[some], sums_ref
        )


def far_sums_kernel(outs, half, *refs):
    scalar_refs, refs = refs[:3], refs[3:]
    if half == 0:
        (across_a, across_b, high, low), refs = refs[:4], refs[4:]
    spectra_in, base_refs, refs = refs[0], refs[1 : 1 + outs], refs[1 + outs :]
    if half == 0:
        spectra_ref, refs = refs[0], refs[1:]
        fill_spectra([across_a, across_b], high, low, spectra_ref, 2)
    else:
        spectra_ref = spectra_in
    out_refs, (sums_ref,) = refs[:outs], refs[outs:]
    turns = half_turns(scalar_refs[2].shape[0], half)
    add_pairs(scalar_refs, turns, lambda part: part == 2, spectra_ref, base_refs, out_refs, sums_ref)


def call_sums(kernel, name, scalars, arrays, updated, out_shapes, scratch, flops):
    vmem = pl.BlockSpec(memory_space=pltpu.VMEM)
    smem = pl.BlockSpec(memory_space=pltpu.SMEM)
    operands = [*scalars, *arrays, *updated]
    shapes = [*out_shapes, *(jax.ShapeDtypeStruct(value.shape, value.dtype) for value in updated)]
    first_in, first_out = len(operands) - len(updated), len(shapes) - len(updated)
    return pl.pallas_call(
        kernel,
        out_shape=shapes,
        in_specs=[smem] * len(scalars) + [vmem] * (len(operands) - len(scalars)),
        out_specs=[vmem] * len(shapes),
        scratch_shapes=scratch,
        input_output_aliases={first_in + i: first_out + i for i in range(len(updated))},
        compiler_params=pltpu.CompilerParams(vmem_limit_bytes=VMEM_BYTES),
        cost_estimate=pl.CostEstimate(flops=flops, bytes_accessed=10**6, transcendentals=0),
        name=name,
    )(*operands)


def finish_kernel(channels, kept_ref, swapped_ref, weight_ref, high_ref, low_ref, *refs):
    out_ref = refs[-1]
    total = sum(weight_ref[station] for station in range(weight_ref.shape[0]))
    scale = 1.0 / (channels * jnp.full((1, out_ref.shape[1]), total, F32))
    out_ref[...] = split_dot(kept_ref[...] + swapped_ref[...], high_ref, low_ref) * scale


def finish(channels, kept, swapped, station_weight, tables, half, result):
    rows, lags = kept.shape
    vmem = pl.BlockSpec(memory_space=pltpu.VMEM)
    smem = pl.BlockSpec(memory_space=pltpu.SMEM)
    operands = [kept, swapped, station_weight, *tables]
    specs = [vmem, vmem, smem, vmem, vmem]
    if result is not None:
        operands.append(result)
        specs.append(pl.BlockSpec(memory_space=pltpu.HBM))
    return pl.pallas_call(
        lambda *refs: finish_kernel(channels, *refs),
        grid=(1,),
        out_shape=jax.ShapeDtypeStruct((2 * rows, lags), F32),
        in_specs=specs,
        out_specs=pl.BlockSpec((rows, lags), lambda i: (half, 0)),
        input_output_aliases={} if result is None else {5: 0},
        compiler_params=pltpu.CompilerParams(vmem_limit_bytes=VMEM_BYTES),
        cost_estimate=pl.CostEstimate(flops=10**9, bytes_accessed=10**6, transcendentals=0),
        name="finish",
    )(*operands)


def on_device(waveforms, event_mask, station_weight, partners, pair_list, counts):
    events, stations, channels, samples = waveforms.shape
    rounds, _, all_pairs, _ = pair_list.shape
    clusters = lax.axis_size("cluster")
    length = lax.axis_size("station")
    assert (stations, channels, samples) == (HALF, 3, 2 * LANES)
    assert events % 2 == 0 and rounds % 2 == 0 and clusters % 2 == 0 and length % 4 == 0
    forward = [jnp.asarray(table) for table in forward_table(samples)]
    inverse = [jnp.asarray(table) for table in inverse_table(samples)]
    scalars = (partners, counts, jnp.transpose(pair_list, (0, 1, 3, 2)))

    def to_sibling(value):
        return lax.ppermute(value, "cluster", [(i, i ^ 1) for i in range(clusters)])

    def to_across(value):
        return lax.ppermute(value, "cluster", [(i, (i + 1 if i % 2 else i - 1) % clusters) for i in range(clusters)])

    def to_mirror(value):
        return lax.ppermute(value, "station", [(i, length - 1 - i) for i in range(length)])

    swap = length == 4
    outs = 2 if swap else 1
    half_shape = jax.ShapeDtypeStruct((rounds * all_pairs // 4 // outs, 2 * samples), F32)
    spectra_shape = (3, events // 2 + 1, 2, 6, SUB, LANES)
    sums = pltpu.VMEM((2, all_pairs // length * SUB, LANES), F32)

    own, own_first, own_rest = prepare(waveforms, event_mask, station_weight)
    mirror_first = to_mirror(own_first)
    across = to_across(own)
    sibling = to_sibling(own)
    own_rest, mirror_first, across = lax.optimization_barrier((own_rest, mirror_first, across))
    mirror_rest = to_mirror(own_rest)
    far_first = to_across(mirror_first)
    near_first = to_sibling(mirror_first)
    partial = call_sums(
        lambda *refs: first_sums_kernel(outs, *refs),
        "first_sums",
        scalars,
        [own, sibling, across, *forward],
        [],
        [half_shape] * (2 * outs),
        [pltpu.VMEM(spectra_shape, F32), sums],
        4 * 10**9,
    )
    far_rest = to_across(mirror_rest)
    near_rest = to_sibling(mirror_rest)
    spectra, *partial = call_sums(
        lambda *refs: near_sums_kernel(outs, *refs),
        "near_sums",
        scalars,
        [mirror_first, mirror_rest, near_first, near_rest, *forward],
        partial,
        [jax.ShapeDtypeStruct(spectra_shape, F32)],
        [sums],
        3 * 10**9,
    )
    spectra, *early = call_sums(
        lambda *refs: far_sums_kernel(outs, 0, *refs),
        "far_sums",
        scalars,
        [far_first, far_rest, *forward],
        [spectra, *partial[:outs]],
        [],
        [sums],
        2 * 10**9,
    )
    late = call_sums(
        lambda *refs: far_sums_kernel(outs, 1, *refs),
        "far_sums",
        scalars,
        [spectra],
        partial[outs:],
        [],
        [sums],
        2 * 10**9,
    )
    result = None
    for half, values in enumerate((early, late)):
        if swap:
            kept, sent = values
            received = lax.ppermute(sent, "station", [(i, i ^ 1) for i in range(length)])
        else:
            groups = np.arange(length).reshape(2, length // 2).tolist()
            value = values[0].reshape(rounds // 2, all_pairs // 2, 2 * samples)
            kept = lax.psum_scatter(value, "station", scatter_dimension=1, axis_index_groups=groups, tiled=True)
            kept = kept.reshape(-1, 2 * samples)
            received = jnp.zeros_like(kept)
        result = finish(channels, kept, received, station_weight, inverse, half, result)
    return result.reshape(rounds, 1, all_pairs // length, 2 * samples)


def solution(mesh):
    return jax.shard_map(
        on_device,
        mesh=mesh,
        in_specs=(
            P(("groups", "cluster"), "station", None, None),
            P(("groups", "cluster"), "station"),
            P("groups"),
            P(None, "groups"),
            P(None, ("groups", "cluster"), None, None),
            P("groups"),
        ),
        out_specs=P(None, ("groups", "cluster"), "station", None),
        check_vma=False,
    )
```

time: 57.7 us -> 61.2 us (1.061)
  waiting for transfers between devices: 23.6 us -> 17.3 us
  Pallas kernels: 14.2 us -> 17.5 us
  local copies, waits for them, and re-layouts: 3.1 us -> 6.29 us
  starting transfers between devices: 16.4 us -> 19.2 us
    ppermute x5 -> x8, starting transfers between devices: 8.33 us -> 12.9 us  [the longest x2 7.15 us: to_mirror(): lax.ppermute(value, 'station', [(i, length - 1 - i) for i in range(length)])]
    ppermute x1 -> x2, waiting for transfers between devices: 12.2 us -> 8.11 us  [on_device(): lax.ppermute(sent, 'station', [(i, i ^ 1) for i in range(length)])]
    unnamed x20 -> x32, local copies, waits for them, and re-layouts: 2.36 us -> 6.29 us
    pallas_call x4 -> x7, Pallas kernels: 14.2 us -> 17.5 us  [the longest x4 12.9 us: call_sums(): pl.pallas_call(kernel, out_shape=shapes, in_specs=[smem] * len(scalars) +...]
    ppermute x5 -> x8, waiting for transfers between devices: 11.4 us -> 9.22 us  [the longest x2 9.17 us: to_mirror(): lax.ppermute(value, 'station', [(i, length - 1 - i) for i in range(length)])]
    ppermute x1 -> x2, starting transfers between devices: 8.09 us -> 6.31 us  [on_device(): lax.ppermute(sent, 'station', [(i, i ^ 1) for i in range(length)])]
    reshape x1 -> x0, local copies, waits for them, and re-layouts: 0.74 us -> none  [prepare(): weights = station_weight.reshape(-1, stations)]
  transfers between devices with their start and end apart: 6 -> 10, of which waited for: 4 -> 4; matrix products, arithmetic and copies ran while one was open for 0% -> 0% of each run, Pallas kernels for 10% -> 20%
where the time goes in v2:
time: 61.2 us; the launch traced here: 60.4 us
  starting transfers between devices  19.2 us (31%)
  Pallas kernels  17.5 us (29%)
  waiting for transfers between devices  17.3 us (28%)
  local copies, waits for them, and re-layouts  6.29 us (10%)
    pallas_call x4, Pallas kernels, call_sums(): pl.pallas_call(kernel, out_shape=shapes, in_specs=[smem] * len(scalars) +...  12.9 us
    ppermute x2, waiting for transfers between devices, to_mirror(): lax.ppermute(value, 'station', [(i, length - 1 - i) for i in range(length)])  9.17 us
    ppermute x2, waiting for transfers between devices, on_device(): lax.ppermute(sent, 'station', [(i, i ^ 1) for i in range(length)])  8.11 us
    ppermute x2, starting transfers between devices, to_mirror(): lax.ppermute(value, 'station', [(i, length - 1 - i) for i in range(length)])  7.15 us
    ppermute x2, starting transfers between devices, on_device(): lax.ppermute(sent, 'station', [(i, i ^ 1) for i in range(length)])  6.31 us
    unnamed x32, local copies, waits for them, and re-layouts  6.29 us
    ppermute x3, starting transfers between devices, to_across(): lax.ppermute(value, 'cluster', [(i, (i + 1 if i % 2 else i - 1) % cluster...  5.33 us
    pallas_call x2, Pallas kernels, finish(): pl.pallas_call(lambda *refs: finish_kernel(channels, *refs), grid=(1,), o...  3.25 us
  transfers between devices with their start and end apart: 10, of which 4 were waited for; matrix products, arithmetic and copies ran while one was open for 0% of the time, Pallas kernels for 20%

profile of v2, /device:TPU:0, one launch (start us, length us, event | category | flops | bytes accessed | tf_op | source)
XLA Modules:
  0.0 60.4 jit_solution(12997613347160083944)
XLA Ops:
  0.0 0.0 copy-start
  0.0 1.0 %copy-done = f32[32,4,3,256]{3,1,2,0:T(4,128)S(1)} copy-done((f32[32,4,3,256]{3,1,2,0:T(4,128)S(1)}, f32[32,4,3,256]{3,1,2,0:T(4,128)}, u32[]{:S(2)}) %copy-start) | copy-done | bytes 393240
  1.0 0.0 copy-start.1
  1.0 0.7 %copy-done.1 = s32[32,4]{0,1:T(4,128)S(1)} copy-done((s32[32,4]{0,1:T(4,128)S(1)}, s32[32,4]{0,1:T(4,128)}, u32[]{:S(2)}) %copy-start.1) | copy-done | bytes 536
  1.7 0.0 copy-start.2
  1.7 0.7 %copy-done.2 = f32[16]{0:T(128)S(1)} copy-done((f32[16]{0:T(128)S(1)}, f32[16]{0:T(128)}, u32[]{:S(2)}) %copy-start.2) | copy-done | bytes 88
  2.3 1.4 %prepare.1 = (f32[3,16,8,256]{3,2,1,0:T(8,128)S(1)}, f32[2,16,8,256]{3,2,1,0:T(8,128)S(1)}, f32[1,16,8,256]{3,2,1,0:T(8,128)S(1)}) custom-call(f32[16,2,3,4,256]{4,3,2,1,0:T(4,128)S(1)} %bitcast.8, s32[4,32]{1,0:T(4,128)S(1)} %bitcast.9, f32[16]{0:T(128)S(1)} %copy-done.2), custom_call_target="tpu_custom_call" | custom-call | tf_op jit(solution)/shard_map/prepare/pallas_call | solution.py:99
  3.7 2.4 %collective-permute-start.1 = (f32[3,16,8,256]{3,2,1,0:T(8,128)S(1)}, f32[3,16,8,256]{3,2,1,0:T(8,128)S(1)}, u32[]{:S(2)}, u32[]{:S(2)}) collective-permute-start(f32[3,16,8,256]{3,2,1,0:T(8,128)S(1)} %get-tuple-element.27.refs_3_), channel_id=1, source_target_pairs={{0,12},{4,8},{8,4},{12,0},{1,13},{5,9},{9,5},{13,1},{2,14},{6,10},... | collective-permute-start | bytes 1179656 | tf_op jit(solution)/shard_map/ppermute | solution.py:310
  6.2 3.6 %collective-permute-start = (f32[2,16,8,256]{3,2,1,0:T(8,128)S(1)}, f32[2,16,8,256]{3,2,1,0:T(8,128)S(1)}, u32[]{:S(2)}, u32[]{:S(2)}) collective-permute-start(f32[2,16,8,256]{3,2,1,0:T(8,128)S(1)} %get-tuple-element.26), channel_id=1, source_target_pairs={{0,3},{1,2},{2,1},{3,0},{4,7},{5,6},{6,5},{7,4},{8,11},{9,10},{10,... | collective-permute-start | bytes 786440 | tf_op jit(solution)/shard_map/ppermute | solution.py:313
  9.8 0.4 collective-permute-start.7
  10.1 6.9 %collective-permute-done.refs_3_ = f32[2,16,8,256]{3,2,1,0:T(8,128)S(1)} collective-permute-done((f32[2,16,8,256]{3,2,1,0:T(8,128)S(1)}, f32[2,16,8,256]{3,2,1,0:T(8,128)S(1)}, u32[]{:S(2)}, u32[]{:S(2)}) %collective-permute-start) | collective-permute-done | bytes 262176 | tf_op jit(solution)/shard_map/ppermute | solution.py:313
  17.0 0.0 collective-permute-done.1.refs_5_
  17.0 3.5 %collective-permute-start.3 = (f32[1,16,8,256]{3,2,1,0:T(8,128)S(1)}, f32[1,16,8,256]{3,2,1,0:T(8,128)S(1)}, u32[]{:S(2)}, u32[]{:S(2)}) collective-permute-start(f32[1,16,8,256]{3,2,1,0:T(8,128)S(1)} %get-tuple-element.29), channel_id=1, source_target_pairs={{0,3},{1,2},{2,1},{3,0},{4,7},{5,6},{6,5},{7,4},{8,11},{9,10},{10,... | collective-permute-start | bytes 393224 | tf_op jit(solution)/shard_map/ppermute | solution.py:313
  20.6 0.0 collective-permute-start.5
  20.6 1.3 %collective-permute-start.2 = (f32[2,16,8,256]{3,2,1,0:T(8,128)S(1)}, f32[2,16,8,256]{3,2,1,0:T(8,128)S(1)}, u32[]{:S(2)}, u32[]{:S(2)}) collective-permute-start(f32[2,16,8,256]{3,2,1,0:T(8,128)S(1)} %collective-permute-done.refs_3_), channel_id=1, source_target_pairs={{0,12},{4,8},{8,4},{12,0},{1,13},{5,9},{9,5},{13,1},{2,14},{6,10},... | collective-permute-start | bytes 786440 | tf_op jit(solution)/shard_map/ppermute | solution.py:310
  21.8 2.3 %collective-permute-done.3.refs_4_ = f32[1,16,8,256]{3,2,1,0:T(8,128)S(1)} collective-permute-done((f32[1,16,8,256]{3,2,1,0:T(8,128)S(1)}, f32[1,16,8,256]{3,2,1,0:T(8,128)S(1)}, u32[]{:S(2)}, u32[]{:S(2)}) %collective-permute-start.3) | collective-permute-done | bytes 131104 | tf_op jit(solution)/shard_map/ppermute | solution.py:313
  24.1 0.0 collective-permute-start.6
  24.1 0.0 collective-permute-done.7.refs_4_
  24.1 0.0 copy-start.4
  24.1 0.7 %copy-done.4 = s32[4,1,256,2]{2,3,1,0:T(2,128)S(1)} copy-done((s32[4,1,256,2]{2,3,1,0:T(2,128)S(1)}, s32[4,1,256,2]{2,3,1,0:T(2,128)}, u32[]{:S(2)}) %copy-start.4) | copy-done | bytes 8216
  24.8 0.7 %copy-done.6 = s32[4,4]{1,0:T(4,128)S(1)} copy-done((s32[4,4]{1,0:T(4,128)S(1)}, s32[4,4]{1,0:T(4,128)}, u32[]{:S(2)}) %copy-start.6) | copy-done | bytes 88
  25.5 0.7 %copy-done.8 = s32[4]{0:T(128)S(1)} copy-done((s32[4]{0:T(128)S(1)}, s32[4]{0:T(128)}, u32[]{:S(2)}) %copy-start.8) | copy-done | bytes 40
  26.2 0.9 %copy-done.12 = bf16[256,512]{1,0:T(8,128)(2,1)S(1)} copy-done((bf16[256,512]{1,0:T(8,128)(2,1)S(1)}, bf16[256,512]{1,0:T(8,128)(2,1)}, u32[]{:S(2)}) %copy-start.12) | copy-done | bytes 262168
  27.1 0.9 %copy-done.14 = bf16[256,512]{1,0:T(8,128)(2,1)S(1)} copy-done((bf16[256,512]{1,0:T(8,128)(2,1)S(1)}, bf16[256,512]{1,0:T(8,128)(2,1)}, u32[]{:S(2)}) %copy-start.14) | copy-done | bytes 262168
  28.1 5.5 %first_sums.1 = (f32[128,512]{1,0:T(8,128)S(1)}, f32[128,512]{1,0:T(8,128)S(1)}, f32[128,512]{1,0:T(8,128)S(1)}, f32[128,512]{1,0:T(8,128)S(1)}) custom-call(s32[4,4]{1,0:T(4,128)S(1)} %copy-done.6, s32[4]{0:T(128)S(1)} %copy-done.8, s32[4,1,2,256]{3,2,1,0:T(2,128)S(1)} %bitcast.10, f32[3,16,8,256]{3,2,1,0:T(8,128)S(1)} %get-tuple-element.27.refs_3_, ...), custom_call_target="tpu_custom_call" | custom-call | flops 4000000000 | bytes 1000000 | tf_op jit(solution)/shard_map/first_sums/pallas_call | solution.py:253
  33.6 1.6 %collective-permute-start.4 = (f32[1,16,8,256]{3,2,1,0:T(8,128)S(1)}, f32[1,16,8,256]{3,2,1,0:T(8,128)S(1)}, u32[]{:S(2)}, u32[]{:S(2)}) collective-permute-start(f32[1,16,8,256]{3,2,1,0:T(8,128)S(1)} %collective-permute-done.3.refs_4_), channel_id=1, source_target_pairs={{0,12},{4,8},{8,4},{12,0},{1,13},{5,9},{9,5},{13,1},{2,14},{6,10},... | collective-permute-start | bytes 393224 | tf_op jit(solution)/shard_map/ppermute | solution.py:310
  35.2 0.0 collective-permute-done.6.refs_6_
  35.2 0.0 collective-permute-done.5.refs_5_
  35.2 0.0 copy-done.5
  35.2 0.0 copy-done.7
  35.2 0.0 copy-done.9
  35.3 0.0 copy-done.15
  35.3 0.0 copy-start.13
  35.3 3.5 %near_sums.1 = (f32[3,17,2,6,8,128]{5,4,3,2,1,0:T(8,128)S(1)}, f32[128,512]{1,0:T(8,128)S(1)}, f32[128,512]{1,0:T(8,128)S(1)}, f32[128,512]{1,0:T(8,128)S(1)}, f32[128,512]{1,0:T(8,128)S(1)}) custom-call(s32[4,4]{1,0:T(4,128)S(1)} %copy-done.7, s32[4]{0:T(128)S(1)} %copy-done.9, ...), custom_call_target="tpu_custom_call", output_to_operand_aliasing={{1}: (9, {}), {2}: (10, {}), {3}: (11, {}), {4}: (12, {})} | custom-call | flops 3000000000 | bytes 1000000 | tf_op jit(solution)/shard_map/near_sums/pallas_call | solution.py:253
  38.8 0.0 collective-permute-done.4.refs_4_
  38.8 0.0 collective-permute-done.2.refs_3_
  38.8 0.0 copy-done.13
  38.8 2.1 %far_sums.2 = (f32[3,17,2,6,8,128]{5,4,3,2,1,0:T(8,128)S(1)}, f32[128,512]{1,0:T(8,128)S(1)}, f32[128,512]{1,0:T(8,128)S(1)}) custom-call(s32[4,4]{1,0:T(4,128)S(1)} %copy-done.7, s32[4]{0:T(128)S(1)} %copy-done.9, s32[4,1,2,256]{3,2,1,0:T(2,128)S(1)} %bitcast.12, ...), custom_call_target="tpu_custom_call", output_to_operand_aliasing={{0}: (7, {}), {1}: (8, {}), {2}: (9, {})} | custom-call | flops 2000000000 | bytes 1000000 | tf_op jit(solution)/shard_map/far_sums/pallas_call | solution.py:253
  41.0 6.2 %collective-permute-start.9 = (f32[128,512]{1,0:T(8,128)S(1)}, f32[128,512]{1,0:T(8,128)S(1)}, u32[]{:S(2)}, u32[]{:S(2)}) collective-permute-start(f32[128,512]{1,0:T(8,128)S(1)} %get-tuple-element.44), channel_id=1, source_target_pairs={{0,1},{1,0},{2,3},{3,2},{4,5},{5,4},{6,7},{7,6},{8,9},{9,8},{10,11... | collective-permute-start | bytes 786440 | tf_op jit(solution)/shard_map/ppermute | solution.py:375
  47.2 1.7 %far_sums.3 = (f32[128,512]{1,0:T(8,128)S(1)}, f32[128,512]{1,0:T(8,128)S(1)}) custom-call(s32[4,4]{1,0:T(4,128)S(1)} %copy-done.7, s32[4]{0:T(128)S(1)} %copy-done.9, s32[4,1,2,256]{3,2,1,0:T(2,128)S(1)} %bitcast.13, f32[3,17,2,6,8,128]{5,4,3,2,1,0:T(8,128)S(1)} %get-tuple-element.38.refs_3_, ...), custom_call_target="tpu_custom_call", output_to_operand_aliasing={{0}: (4, {}), {1}: (5, {})} | custom-call | flops 2000000000 | bytes 1000000 | tf_op jit(solution)/shard_map/far_sums/pallas_call | solution.py:253
  48.9 0.1 collective-permute-start.8
  49.0 5.3 %collective-permute-done.9.refs_1_ = f32[128,512]{1,0:T(8,128)S(1)} collective-permute-done((f32[128,512]{1,0:T(8,128)S(1)}, f32[128,512]{1,0:T(8,128)S(1)}, u32[]{:S(2)}, u32[]{:S(2)}) %collective-permute-start.9) | collective-permute-done | bytes 262176 | tf_op jit(solution)/shard_map/ppermute | solution.py:375
  54.4 0.0 copy-done.3
  54.4 0.0 copy-done.10
  54.4 0.0 copy-done.11
  54.4 1.6 %finish.2.refs_5_ = f32[256,512]{1,0:T(8,128)} custom-call(f32[128,512]{1,0:T(8,128)S(1)} %get-tuple-element.43.refs_0_, f32[128,512]{1,0:T(8,128)S(1)} %collective-permute-done.9.refs_1_, f32[16]{0:T(128)S(1)} %copy-done.3, bf16[512,512]{1,0:T(8,128)(2,1)S(1)} %copy-done.11, bf16[512,512]{1,0:T(8,128)(2,1)S(1)} %copy-done.10), custom_call_target="tpu_custom_call" | custom-call | flops 1000000000 | bytes 1000000 | tf_op jit(solution)/shard_map/finish/pallas_call | solution.py:282
  56.0 2.8 %collective-permute-done.8.refs_1_ = f32[128,512]{1,0:T(8,128)S(1)} collective-permute-done((f32[128,512]{1,0:T(8,128)S(1)}, f32[128,512]{1,0:T(8,128)S(1)}, u32[]{:S(2)}, u32[]{:S(2)}) %collective-permute-start.8) | collective-permute-done | bytes 262176 | tf_op jit(solution)/shard_map/ppermute | solution.py:375
  58.8 1.6 %finish.3 = f32[256,512]{1,0:T(8,128)} custom-call(f32[128,512]{1,0:T(8,128)S(1)} %get-tuple-element.41.refs_0_, f32[128,512]{1,0:T(8,128)S(1)} %collective-permute-done.8.refs_1_, f32[16]{0:T(128)S(1)} %copy-done.3, bf16[512,512]{1,0:T(8,128)(2,1)S(1)} %copy-done.11, bf16[512,512]{1,0:T(8,128)(2,1)S(1)} %copy-done.10, ...), custom_call_target="tpu_custom_call", output_to_operand_aliasing={{}: (5, {})} | custom-call | flops 1000000000 | bytes 1000000 | tf_op jit(solution)/shard_map/finish/pallas_call | solution.py:282
  (11 shorter events, 0.0 us)
Async XLA Ops:
  0.0 1.0 %copy-start = (f32[32,4,3,256]{3,1,2,0:T(4,128)S(1)}, f32[32,4,3,256]{3,1,2,0:T(4,128)}, u32[]{:S(2)}) copy-start(f32[32,4,3,256]{3,1,2,0:T(4,128)} %param.10) | copy-start | bytes 1179652
  1.0 0.7 %copy-start.1 = (s32[32,4]{0,1:T(4,128)S(1)}, s32[32,4]{0,1:T(4,128)}, u32[]{:S(2)}) copy-start(s32[32,4]{0,1:T(4,128)} %param.11) | copy-start | bytes 1540
  1.7 0.7 %copy-start.2 = (f32[16]{0:T(128)S(1)}, f32[16]{0:T(128)}, u32[]{:S(2)}) copy-start(f32[16]{0:T(128)} %refs_2_.3) | copy-start | bytes 196
  3.7 13.3 %collective-permute-start.1 = (f32[3,16,8,256]{3,2,1,0:T(8,128)S(1)}, f32[3,16,8,256]{3,2,1,0:T(8,128)S(1)}, u32[]{:S(2)}, u32[]{:S(2)}) collective-permute-start(f32[3,16,8,256]{3,2,1,0:T(8,128)S(1)} %get-tuple-element.27.refs_3_), channel_id=1, source_target_pairs={{0,12},{4,8},{8,4},{12,0},{1,13},{5,9},{9,5},{13,1},{2,14},{6,10},... | collective-permute-start | bytes 1179656 | tf_op jit(solution)/shard_map/ppermute | solution.py:310
  6.2 10.9 %collective-permute-start = (f32[2,16,8,256]{3,2,1,0:T(8,128)S(1)}, f32[2,16,8,256]{3,2,1,0:T(8,128)S(1)}, u32[]{:S(2)}, u32[]{:S(2)}) collective-permute-start(f32[2,16,8,256]{3,2,1,0:T(8,128)S(1)} %get-tuple-element.26), channel_id=1, source_target_pairs={{0,3},{1,2},{2,1},{3,0},{4,7},{5,6},{6,5},{7,4},{8,11},{9,10},{10,... | collective-permute-start | bytes 786440 | tf_op jit(solution)/shard_map/ppermute | solution.py:313
  9.8 14.4 %collective-permute-start.7 = (f32[3,16,8,256]{3,2,1,0:T(8,128)S(1)}, f32[3,16,8,256]{3,2,1,0:T(8,128)S(1)}, u32[]{:S(2)}, u32[]{:S(2)}) collective-permute-start(f32[3,16,8,256]{3,2,1,0:T(8,128)S(1)} %get-tuple-element.27.refs_3_), channel_id=1, source_target_pairs={{0,4},{4,0},{8,12},{12,8},{1,5},{5,1},{9,13},{13,9},{2,6},{6,2},{1... | collective-permute-start | bytes 1179656 | tf_op jit(solution)/shard_map/ppermute | solution.py:307
  17.0 7.1 %collective-permute-start.3 = (f32[1,16,8,256]{3,2,1,0:T(8,128)S(1)}, f32[1,16,8,256]{3,2,1,0:T(8,128)S(1)}, u32[]{:S(2)}, u32[]{:S(2)}) collective-permute-start(f32[1,16,8,256]{3,2,1,0:T(8,128)S(1)} %get-tuple-element.29), channel_id=1, source_target_pairs={{0,3},{1,2},{2,1},{3,0},{4,7},{5,6},{6,5},{7,4},{8,11},{9,10},{10,... | collective-permute-start | bytes 393224 | tf_op jit(solution)/shard_map/ppermute | solution.py:313
  20.6 14.7 %collective-permute-start.5 = (f32[2,16,8,256]{3,2,1,0:T(8,128)S(1)}, f32[2,16,8,256]{3,2,1,0:T(8,128)S(1)}, u32[]{:S(2)}, u32[]{:S(2)}) collective-permute-start(f32[2,16,8,256]{3,2,1,0:T(8,128)S(1)} %collective-permute-done.refs_3_), channel_id=1, source_target_pairs={{0,4},{4,0},{8,12},{12,8},{1,5},{5,1},{9,13},{13,9},{2,6},{6,2},{1... | collective-permute-start | bytes 786440 | tf_op jit(solution)/shard_map/ppermute | solution.py:307
  20.6 18.3 %collective-permute-start.2 = (f32[2,16,8,256]{3,2,1,0:T(8,128)S(1)}, f32[2,16,8,256]{3,2,1,0:T(8,128)S(1)}, u32[]{:S(2)}, u32[]{:S(2)}) collective-permute-start(f32[2,16,8,256]{3,2,1,0:T(8,128)S(1)} %collective-permute-done.refs_3_), channel_id=1, source_target_pairs={{0,12},{4,8},{8,4},{12,0},{1,13},{5,9},{9,5},{13,1},{2,14},{6,10},... | collective-permute-start | bytes 786440 | tf_op jit(solution)/shard_map/ppermute | solution.py:310
  24.1 11.1 %collective-permute-start.6 = (f32[1,16,8,256]{3,2,1,0:T(8,128)S(1)}, f32[1,16,8,256]{3,2,1,0:T(8,128)S(1)}, u32[]{:S(2)}, u32[]{:S(2)}) collective-permute-start(f32[1,16,8,256]{3,2,1,0:T(8,128)S(1)} %collective-permute-done.3.refs_4_), channel_id=1, source_target_pairs={{0,4},{4,0},{8,12},{12,8},{1,5},{5,1},{9,13},{13,9},{2,6},{6,2},{1... | collective-permute-start | bytes 393224 | tf_op jit(solution)/shard_map/ppermute | solution.py:307
  24.1 0.7 %copy-start.4 = (s32[4,1,256,2]{2,3,1,0:T(2,128)S(1)}, s32[4,1,256,2]{2,3,1,0:T(2,128)}, u32[]{:S(2)}) copy-start(s32[4,1,256,2]{2,3,1,0:T(2,128)} %param.14) | copy-start | bytes 24580
  24.8 0.7 %copy-start.6 = (s32[4,4]{1,0:T(4,128)S(1)}, s32[4,4]{1,0:T(4,128)}, u32[]{:S(2)}) copy-start(s32[4,4]{1,0:T(4,128)} %refs_0_.7) | copy-start | bytes 196
  25.5 0.7 %copy-start.8 = (s32[4]{0:T(128)S(1)}, s32[4]{0:T(128)}, u32[]{:S(2)}) copy-start(s32[4]{0:T(128)} %refs_1_.7) | copy-start | bytes 52
  26.2 0.9 %copy-start.12 = (bf16[256,512]{1,0:T(8,128)(2,1)S(1)}, bf16[256,512]{1,0:T(8,128)(2,1)}, u32[]{:S(2)}) copy-start(bf16[256,512]{1,0:T(8,128)(2,1)} %constant.9.clone.refs_7_.refs_8_.refs_6_) | copy-start | bytes 786436
  27.1 0.9 %copy-start.14 = (bf16[256,512]{1,0:T(8,128)(2,1)S(1)}, bf16[256,512]{1,0:T(8,128)(2,1)}, u32[]{:S(2)}) copy-start(bf16[256,512]{1,0:T(8,128)(2,1)} %constant.8.clone.refs_6_.refs_7_.refs_5_) | copy-start | bytes 786436
  28.1 7.1 %copy-start.5 = (s32[4,1,256,2]{2,3,1,0:T(2,128)S(1)}, s32[4,1,256,2]{2,3,1,0:T(2,128)}, u32[]{:S(2)}) copy-start(s32[4,1,256,2]{2,3,1,0:T(2,128)} %param.14) | copy-start | bytes 24580
  28.1 7.2 %copy-start.7 = (s32[4,4]{1,0:T(4,128)S(1)}, s32[4,4]{1,0:T(4,128)}, u32[]{:S(2)}) copy-start(s32[4,4]{1,0:T(4,128)} %refs_0_.7) | copy-start | bytes 196
  28.1 7.2 %copy-start.9 = (s32[4]{0:T(128)S(1)}, s32[4]{0:T(128)}, u32[]{:S(2)}) copy-start(s32[4]{0:T(128)} %refs_1_.7) | copy-start | bytes 52
  28.1 7.2 %copy-start.15 = (bf16[256,512]{1,0:T(8,128)(2,1)S(1)}, bf16[256,512]{1,0:T(8,128)(2,1)}, u32[]{:S(2)}) copy-start(bf16[256,512]{1,0:T(8,128)(2,1)} %constant.8.clone.refs_6_.refs_7_.refs_5_) | copy-start | bytes 786436
  33.6 5.2 %collective-permute-start.4 = (f32[1,16,8,256]{3,2,1,0:T(8,128)S(1)}, f32[1,16,8,256]{3,2,1,0:T(8,128)S(1)}, u32[]{:S(2)}, u32[]{:S(2)}) collective-permute-start(f32[1,16,8,256]{3,2,1,0:T(8,128)S(1)} %collective-permute-done.3.refs_4_), channel_id=1, source_target_pairs={{0,12},{4,8},{8,4},{12,0},{1,13},{5,9},{9,5},{13,1},{2,14},{6,10},... | collective-permute-start | bytes 393224 | tf_op jit(solution)/shard_map/ppermute | solution.py:310
  35.3 3.6 %copy-start.13 = (bf16[256,512]{1,0:T(8,128)(2,1)S(1)}, bf16[256,512]{1,0:T(8,128)(2,1)}, u32[]{:S(2)}) copy-start(bf16[256,512]{1,0:T(8,128)(2,1)} %constant.9.clone.refs_7_.refs_8_.refs_6_) | copy-start | bytes 786436
  41.0 13.4 %collective-permute-start.9 = (f32[128,512]{1,0:T(8,128)S(1)}, f32[128,512]{1,0:T(8,128)S(1)}, u32[]{:S(2)}, u32[]{:S(2)}) collective-permute-start(f32[128,512]{1,0:T(8,128)S(1)} %get-tuple-element.44), channel_id=1, source_target_pairs={{0,1},{1,0},{2,3},{3,2},{4,5},{5,4},{6,7},{7,6},{8,9},{9,8},{10,11... | collective-permute-start | bytes 786440 | tf_op jit(solution)/shard_map/ppermute | solution.py:375
  47.2 7.2 %copy-start.3 = (f32[16]{0:T(128)S(1)}, f32[16]{0:T(128)}, u32[]{:S(2)}) copy-start(f32[16]{0:T(128)} %refs_2_.3) | copy-start | bytes 196
  47.2 7.2 %copy-start.10 = (bf16[512,512]{1,0:T(8,128)(2,1)S(1)}, bf16[512,512]{1,0:T(8,128)(2,1)}, u32[]{:S(2)}) copy-start(bf16[512,512]{1,0:T(8,128)(2,1)} %constant.11.clone.refs_4_) | copy-start | bytes 1572868
  47.2 7.2 %copy-start.11 = (bf16[512,512]{1,0:T(8,128)(2,1)S(1)}, bf16[512,512]{1,0:T(8,128)(2,1)}, u32[]{:S(2)}) copy-start(bf16[512,512]{1,0:T(8,128)(2,1)} %constant.10.clone.refs_3_) | copy-start | bytes 1572868
  48.9 9.9 %collective-permute-start.8 = (f32[128,512]{1,0:T(8,128)S(1)}, f32[128,512]{1,0:T(8,128)S(1)}, u32[]{:S(2)}, u32[]{:S(2)}) collective-permute-start(f32[128,512]{1,0:T(8,128)S(1)} %get-tuple-element.42), channel_id=1, source_target_pairs={{0,1},{1,0},{2,3},{3,2},{4,5},{5,4},{6,7},{7,6},{8,9},{9,8},{10,11... | collective-permute-start | bytes 786440 | tf_op jit(solution)/shard_map/ppermute | solution.py:375

commit v3 on v2

--- a/solution.py
+++ b/solution.py
@@ -20,7 +20,7 @@
 def split_table(table):
     high = table.astype(ml_dtypes.bfloat16)
     low = (table - high.astype(np.float64)).astype(ml_dtypes.bfloat16)
-    return high, low
+    return np.stack([high, low])
 
 
 def forward_table(samples):
@@ -38,22 +38,23 @@
     return split_table(np.concatenate([gain * np.cos(angles), -gain * np.sin(angles)], axis=0))
 
 
-def split_dot(value, high_ref, low_ref):
+def split_dot(value, table_ref):
+    rows = value.shape[0]
     high = value.astype(BF16)
     low = (value - high.astype(F32)).astype(BF16)
-    total = jnp.dot(high, low_ref[...], preferred_element_type=F32)
-    total += jnp.dot(low, high_ref[...], preferred_element_type=F32)
-    return total + jnp.dot(high, high_ref[...], preferred_element_type=F32)
-
-
-def prepare_kernel(waves_hbm, mask_hbm, weight_ref, all_ref, first_ref, rest_ref, waves_ref, mask_ref, sems):
+    both = jnp.dot(jnp.concatenate([high, low], axis=0), table_ref[0], preferred_element_type=F32)
+    return both[:rows] + (both[rows:] + jnp.dot(high, table_ref[1], preferred_element_type=F32))
+
+
+def prepare_kernel(waves_hbm, mask_hbm, weight_ref, all_ref, even_ref, odd_ref, both_ref, waves_ref, mask_ref, sems):
     waves_copy = pltpu.make_async_copy(waves_hbm, waves_ref, sems.at[0])
     mask_copy = pltpu.make_async_copy(mask_hbm, mask_ref, sems.at[1])
     waves_copy.start()
     mask_copy.start()
-    twos, _, _, stations, _ = waves_ref.shape
+    twos, _, channels, stations, _ = waves_ref.shape
     events = 2 * twos
     rows = 3 * SUB * twos
+    network = channels * sum(weight_ref[station] for station in range(weight_ref.shape[0]))
     first_weight = lax.axis_index("station") * stations
     station_id = lax.broadcasted_iota(jnp.int32, (stations, events), 0)
     weight = jnp.zeros((stations, events), F32)
@@ -67,7 +68,7 @@
     row = lax.broadcasted_iota(jnp.int32, (rows, stations), 0)
     at_station = row % HALF == lax.broadcasted_iota(jnp.int32, (rows, stations), 1)
     mask_copy.wait()
-    amplitude = mask_ref[...].astype(F32) * jnp.sqrt(weight)
+    amplitude = mask_ref[...].astype(F32) * jnp.sqrt(weight / network)
     picked = lax.dot_general(
         at_event,
         amplitude,
@@ -87,8 +88,9 @@
     energy = jnp.sum(traces * traces, axis=-1, keepdims=True)
     traces = traces * (lax.rsqrt(energy + epsilon) * factor.reshape(energy.shape))
     all_ref[...] = traces
-    first_ref[...] = traces[:2]
-    rest_ref[...] = traces[2:]
+    even_ref[...] = traces[0:1]
+    odd_ref[...] = traces[1:2]
+    both_ref[...] = traces[2:3]
 
 
 def prepare(waveforms, event_mask, station_weight):
@@ -98,9 +100,9 @@
     vmem = pl.BlockSpec(memory_space=pltpu.VMEM)
     return pl.pallas_call(
         prepare_kernel,
-        out_shape=[jax.ShapeDtypeStruct((parts, events // 2, SUB, samples), F32) for parts in (3, 2, 1)],
+        out_shape=[jax.ShapeDtypeStruct((parts, events // 2, SUB, samples), F32) for parts in (3, 1, 1, 1)],
         in_specs=[hbm, hbm, pl.BlockSpec(memory_space=pltpu.SMEM)],
-        out_specs=[vmem] * 3,
+        out_specs=[vmem] * 4,
         scratch_shapes=[
             pltpu.VMEM(waves.shape, F32),
             pltpu.VMEM((stations, events), event_mask.dtype),
@@ -111,18 +113,18 @@
     )(waves, event_mask.T, station_weight)
 
 
-def fill_spectra(trace_refs, high_ref, low_ref, spectra_ref, part):
+def fill_spectra(trace_refs, table_ref, spectra_ref, part):
     pieces = [(ref, index) for ref in trace_refs for index in range(ref.shape[0])]
     _, twos, _, samples = trace_refs[0].shape
     low_half = lax.broadcasted_iota(jnp.int32, (twos, SUB, LANES), 1) < HALF
     for parity in range(2):
         ref, index = pieces[parity]
-        spectrum = split_dot(ref[index].reshape(twos * SUB, samples), high_ref, low_ref)
+        spectrum = split_dot(ref[index].reshape(twos * SUB, samples), table_ref)
         for block in range(4):
             tile = spectrum[:, block * LANES : (block + 1) * LANES].reshape(twos, SUB, LANES)
             spectra_ref[part, :twos, parity, block + block // 2] = tile
     ref, index = pieces[2]
-    spectrum = split_dot(ref[index].reshape(twos * SUB, samples), high_ref, low_ref)
+    spectrum = split_dot(ref[index].reshape(twos * SUB, samples), table_ref)
     for side in range(2):
         spot = 2 * side * LANES
         lower = spectrum[:, spot : spot + LANES].reshape(twos, SUB, LANES)
@@ -205,43 +207,36 @@
     return range(half * rounds // 2, (half + 1) * rounds // 2)
 
 
-def first_sums_kernel(outs, *refs):
-    scalar_refs, (own, sibling, across, high, low), refs = refs[:3], refs[3:8], refs[8:]
-    out_refs, (spectra_ref, sums_ref) = refs[: 2 * outs], refs[2 * outs :]
-    for part, traces in enumerate((own, sibling, across)):
-        fill_spectra([traces], high, low, spectra_ref, part)
-    for half in range(2):
-        turns = half_turns(scalar_refs[2].shape[0], half)
-        add_pairs(scalar_refs, turns, None, spectra_ref, None, out_refs[half * outs : (half + 1) * outs], sums_ref)
-
-
-def near_sums_kernel(outs, *refs):
-    scalar_refs, (own_a, own_b, sibling_a, sibling_b, high, low), refs = refs[:3], refs[3:9], refs[9:]
-    base_refs, refs = refs[: 2 * outs], refs[2 * outs :]
+def near_sums_kernel(count, outs, first, *refs):
+    scalar_refs, refs = refs[:3], refs[3:]
+    own_refs, sibling_refs, table_ref, refs = refs[:count], refs[count : 2 * count], refs[2 * count], refs[2 * count + 1 :]
+    base_refs, refs = ([None] * (2 * outs), refs) if first else (refs[: 2 * outs], refs[2 * outs :])
     spectra_ref, out_refs, sums_ref = refs[0], refs[1:-1], refs[-1]
-    fill_spectra([own_a, own_b], high, low, spectra_ref, 0)
-    fill_spectra([sibling_a, sibling_b], high, low, spectra_ref, 1)
+    fill_spectra(own_refs, table_ref, spectra_ref, 0)
+    fill_spectra(sibling_refs, table_ref, spectra_ref, 1)
     for half in range(2):
         turns = half_turns(scalar_refs[2].shape[0], half)
         some = slice(half * outs, (half + 1) * outs)
-        add_pairs(
-            scalar_refs, turns, lambda part: part < 2, spectra_ref, base_refs[some], out_refs[some], sums_ref
-        )
-
-
-def far_sums_kernel(outs, half, *refs):
-    scalar_refs, refs = refs[:3], refs[3:]
-    if half == 0:
-        (across_a, across_b, high, low), refs = refs[:4], refs[4:]
-    spectra_in, base_refs, refs = refs[0], refs[1 : 1 + outs], refs[1 + outs :]
-    if half == 0:
+        base = None if first else base_refs[some]
+        add_pairs(scalar_refs, turns, lambda part: part < 2, spectra_ref, base, out_refs[some], sums_ref)
+
+
+def far_sums_kernel(count, outs, first, halves, *refs):
+    scalar_refs, across_refs, refs = refs[:3], refs[3 : 3 + count], refs[3 + count :]
+    if count:
+        table_ref, refs = refs[0], refs[1:]
+    spectra_in, base_refs, refs = refs[0], refs[1 : 1 + outs * len(halves)], refs[1 + outs * len(halves) :]
+    if count:
         spectra_ref, refs = refs[0], refs[1:]
-        fill_spectra([across_a, across_b], high, low, spectra_ref, 2)
+        fill_spectra(across_refs, table_ref, spectra_ref, 2)
     else:
         spectra_ref = spectra_in
-    out_refs, (sums_ref,) = refs[:outs], refs[outs:]
-    turns = half_turns(scalar_refs[2].shape[0], half)
-    add_pairs(scalar_refs, turns, lambda part: part == 2, spectra_ref, base_refs, out_refs, sums_ref)
+    out_refs, sums_ref = refs[:-1], refs[-1]
+    for place, half in enumerate(halves):
+        turns = half_turns(scalar_refs[2].shape[0], half)
+        some = slice(place * outs, (place + 1) * outs)
+        base = None if first else base_refs[some]
+        add_pairs(scalar_refs, turns, lambda part: part == 2, spectra_ref, base, out_refs[some], sums_ref)
 
 
 def call_sums(kernel, name, scalars, arrays, updated, out_shapes, scratch, flops):
@@ -263,33 +258,21 @@
     )(*operands)
 
 
-def finish_kernel(channels, kept_ref, swapped_ref, weight_ref, high_ref, low_ref, *refs):
-    out_ref = refs[-1]
-    total = sum(weight_ref[station] for station in range(weight_ref.shape[0]))
-    scale = 1.0 / (channels * jnp.full((1, out_ref.shape[1]), total, F32))
-    out_ref[...] = split_dot(kept_ref[...] + swapped_ref[...], high_ref, low_ref) * scale
-
-
-def finish(channels, kept, swapped, station_weight, tables, half, result):
-    rows, lags = kept.shape
-    vmem = pl.BlockSpec(memory_space=pltpu.VMEM)
-    smem = pl.BlockSpec(memory_space=pltpu.SMEM)
-    operands = [kept, swapped, station_weight, *tables]
-    specs = [vmem, vmem, smem, vmem, vmem]
-    if result is not None:
-        operands.append(result)
-        specs.append(pl.BlockSpec(memory_space=pltpu.HBM))
+def finish_kernel(early_ref, early_swapped_ref, late_ref, late_swapped_ref, table_ref, out_ref):
+    rows = early_ref.shape[0]
+    out_ref[:rows] = split_dot(early_ref[...] + early_swapped_ref[...], table_ref)
+    out_ref[rows:] = split_dot(late_ref[...] + late_swapped_ref[...], table_ref)
+
+
+def finish(values, table):
+    rows, lags = values[0].shape
     return pl.pallas_call(
-        lambda *refs: finish_kernel(channels, *refs),
-        grid=(1,),
+        finish_kernel,
         out_shape=jax.ShapeDtypeStruct((2 * rows, lags), F32),
-        in_specs=specs,
-        out_specs=pl.BlockSpec((rows, lags), lambda i: (half, 0)),
-        input_output_aliases={} if result is None else {5: 0},
         compiler_params=pltpu.CompilerParams(vmem_limit_bytes=VMEM_BYTES),
         cost_estimate=pl.CostEstimate(flops=10**9, bytes_accessed=10**6, transcendentals=0),
         name="finish",
-    )(*operands)
+    )(*values, table)
 
 
 def on_device(waveforms, event_mask, station_weight, partners, pair_list, counts):
@@ -299,8 +282,8 @@
     length = lax.axis_size("station")
     assert (stations, channels, samples) == (HALF, 3, 2 * LANES)
     assert events % 2 == 0 and rounds % 2 == 0 and clusters % 2 == 0 and length % 4 == 0
-    forward = [jnp.asarray(table) for table in forward_table(samples)]
-    inverse = [jnp.asarray(table) for table in inverse_table(samples)]
+    forward = jnp.asarray(forward_table(samples))
+    inverse = jnp.asarray(inverse_table(samples))
     scalars = (partners, counts, jnp.transpose(pair_list, (0, 1, 3, 2)))
 
     def to_sibling(value):
@@ -315,71 +298,62 @@
     swap = length == 4
     outs = 2 if swap else 1
     half_shape = jax.ShapeDtypeStruct((rounds * all_pairs // 4 // outs, 2 * samples), F32)
-    spectra_shape = (3, events // 2 + 1, 2, 6, SUB, LANES)
+    spectra_shape = jax.ShapeDtypeStruct((3, events // 2 + 1, 2, 6, SUB, LANES), F32)
     sums = pltpu.VMEM((2, all_pairs // length * SUB, LANES), F32)
 
-    own, own_first, own_rest = prepare(waveforms, event_mask, station_weight)
-    mirror_first = to_mirror(own_first)
+    def near_sums(own, sibling, partial):
+        first = partial is None
+        return call_sums(
+            lambda *refs: near_sums_kernel(len(own), outs, first, *refs),
+            "near_sums",
+            scalars,
+            [*own, *sibling, forward],
+            [] if first else partial,
+            [spectra_shape] + [half_shape] * (2 * outs if first else 0),
+            [sums],
+            4 * 10**9,
+        )
+
+    def far_sums(across, spectra, partial, first, halves):
+        filled = [spectra] if across else []
+        return call_sums(
+            lambda *refs: far_sums_kernel(len(across), outs, first, halves, *refs),
+            "far_sums",
+            scalars,
+            [*across, forward] if across else [spectra],
+            [*filled, *partial],
+            [],
+            [sums],
+            2 * 10**9,
+        )
+
+    own, *pieces = prepare(waveforms, event_mask, station_weight)
+    mirror = [to_mirror(piece) for piece in pieces]
     across = to_across(own)
     sibling = to_sibling(own)
-    own_rest, mirror_first, across = lax.optimization_barrier((own_rest, mirror_first, across))
-    mirror_rest = to_mirror(own_rest)
-    far_first = to_across(mirror_first)
-    near_first = to_sibling(mirror_first)
-    partial = call_sums(
-        lambda *refs: first_sums_kernel(outs, *refs),
-        "first_sums",
-        scalars,
-        [own, sibling, across, *forward],
-        [],
-        [half_shape] * (2 * outs),
-        [pltpu.VMEM(spectra_shape, F32), sums],
-        4 * 10**9,
-    )
-    far_rest = to_across(mirror_rest)
-    near_rest = to_sibling(mirror_rest)
-    spectra, *partial = call_sums(
-        lambda *refs: near_sums_kernel(outs, *refs),
-        "near_sums",
-        scalars,
-        [mirror_first, mirror_rest, near_first, near_rest, *forward],
-        partial,
-        [jax.ShapeDtypeStruct(spectra_shape, F32)],
-        [sums],
-        3 * 10**9,
-    )
-    spectra, *early = call_sums(
-        lambda *refs: far_sums_kernel(outs, 0, *refs),
-        "far_sums",
-        scalars,
-        [far_first, far_rest, *forward],
-        [spectra, *partial[:outs]],
-        [],
-        [sums],
-        2 * 10**9,
-    )
-    late = call_sums(
-        lambda *refs: far_sums_kernel(outs, 1, *refs),
-        "far_sums",
-        scalars,
-        [spectra],
-        partial[outs:],
-        [],
-        [sums],
-        2 * 10**9,
-    )
-    result = None
-    for half, values in enumerate((early, late)):
+    spectra, *partial = near_sums([own], [sibling], None)
+    spectra, *partial = far_sums([across], spectra, partial, True, (0, 1))
+    mirror, partial = lax.optimization_barrier((mirror, partial))
+    far, near = [], []
+    for piece in mirror:
+        far.append(to_across(piece))
+        near.append(to_sibling(piece))
+    spectra, *partial = near_sums(mirror, near, partial)
+    spectra, *early = far_sums(far, spectra, partial[:outs], False, (0,))
+    late = far_sums([], spectra, partial[outs:], False, (1,))
+    values = []
+    for half in (early, late):
         if swap:
-            kept, sent = values
+            kept, sent = half
             received = lax.ppermute(sent, "station", [(i, i ^ 1) for i in range(length)])
         else:
             groups = np.arange(length).reshape(2, length // 2).tolist()
-            value = values[0].reshape(rounds // 2, all_pairs // 2, 2 * samples)
+            value = half[0].reshape(rounds // 2, all_pairs // 2, 2 * samples)
             kept = lax.psum_scatter(value, "station", scatter_dimension=1, axis_index_groups=groups, tiled=True)
             kept = kept.reshape(-1, 2 * samples)
             received = jnp.zeros_like(kept)
-        result = finish(channels, kept, received, station_weight, inverse, half, result)
+        values += [kept, received]
+    result = finish(values, inverse)
     return result.reshape(rounds, 1, all_pairs // length, 2 * samples)
 
 

time: 61.2 us -> 56.3 us (0.920)
  waiting for transfers between devices: 17.3 us -> 15.5 us
  starting transfers between devices: 19.2 us -> 17.5 us
  Pallas kernels: 17.5 us -> 16.6 us
  local copies, waits for them, and re-layouts: 6.29 us -> 5.43 us
    ppermute x2 -> x3, waiting for transfers between devices: 9.17 us -> 0.01 us  [to_mirror(): lax.ppermute(value, 'station', [(i, length - 1 - i) for i in range(length)])]
    ppermute x3 -> x4, waiting for transfers between devices: 0.04 us -> 4 us  [to_across(): lax.ppermute(value, 'cluster', [(i, (i + 1 if i % 2 else i - 1) % cluster...]
    ppermute x2, waiting for transfers between devices: 8.11 us -> 11.5 us  [on_device(): lax.ppermute(sent, 'station', [(i, i ^ 1) for i in range(length)])]
    ppermute x2, starting transfers between devices: 6.31 us -> 3.91 us  [on_device(): lax.ppermute(sent, 'station', [(i, i ^ 1) for i in range(length)])]
    pallas_call x2 -> x1, Pallas kernels: 3.25 us -> 1.39 us  [finish(): pl.pallas_call(finish_kernel, out_shape=jax.ShapeDtypeStruct((2 * rows, l...]
    pallas_call x4 -> x5, Pallas kernels: 12.9 us -> 13.9 us  [call_sums(): pl.pallas_call(kernel, out_shape=shapes, in_specs=[smem] * len(scalars) +...]
    unnamed x32 -> x24, local copies, waits for them, and re-layouts: 6.29 us -> 5.43 us
    ppermute x3 -> x4, starting transfers between devices: 0.4 us -> 1.17 us  [to_sibling(): return lax.ppermute(value, 'cluster', [(i, i ^ 1) for i in range(clusters)])]
  transfers between devices with their start and end apart: 10 -> 13, of which waited for: 4 -> 4; matrix products, arithmetic and copies ran while one was open for 0% -> 0% of each run, Pallas kernels for 20% -> 20%
where the time goes in v3:
time: 56.3 us; the launch traced here: 55.2 us
  starting transfers between devices  17.5 us (31%)
  Pallas kernels  16.6 us (29%)
  waiting for transfers between devices  15.5 us (28%)
  local copies, waits for them, and re-layouts  5.43 us (10%)
    pallas_call x5, Pallas kernels, call_sums(): pl.pallas_call(kernel, out_shape=shapes, in_specs=[smem] * len(scalars) +...  13.9 us
    ppermute x2, waiting for transfers between devices, on_device(): lax.ppermute(sent, 'station', [(i, i ^ 1) for i in range(length)])  11.5 us
    ppermute x3, starting transfers between devices, to_mirror(): lax.ppermute(value, 'station', [(i, length - 1 - i) for i in range(length)])  7.42 us
    unnamed x24, local copies, waits for them, and re-layouts  5.43 us
    ppermute x4, starting transfers between devices, to_across(): lax.ppermute(value, 'cluster', [(i, (i + 1 if i % 2 else i - 1) % cluster...  4.95 us
    ppermute x4, waiting for transfers between devices, to_across(): lax.ppermute(value, 'cluster', [(i, (i + 1 if i % 2 else i - 1) % cluster...  4 us
    ppermute x2, starting transfers between devices, on_device(): lax.ppermute(sent, 'station', [(i, i ^ 1) for i in range(length)])  3.91 us
    pallas_call x1, Pallas kernels, finish(): pl.pallas_call(finish_kernel, out_shape=jax.ShapeDtypeStruct((2 * rows, l...  1.39 us
  transfers between devices with their start and end apart: 13, of which 4 were waited for; matrix products, arithmetic and copies ran while one was open for 0% of the time, Pallas kernels for 20%

profile of v3, /device:TPU:0, one launch (start us, length us, event | category | flops | bytes accessed | tf_op | source)
XLA Modules:
  0.0 55.2 jit_solution(1977265380820768826)
XLA Ops:
  0.0 1.0 %copy-done = f32[32,4,3,256]{3,1,2,0:T(4,128)S(1)} copy-done((f32[32,4,3,256]{3,1,2,0:T(4,128)S(1)}, f32[32,4,3,256]{3,1,2,0:T(4,128)}, u32[]{:S(2)}) %copy-start) | copy-done | bytes 393240
  1.0 0.7 %copy-done.1 = s32[32,4]{0,1:T(4,128)S(1)} copy-done((s32[32,4]{0,1:T(4,128)S(1)}, s32[32,4]{0,1:T(4,128)}, u32[]{:S(2)}) %copy-start.1) | copy-done | bytes 536
  1.7 0.7 %copy-done.2 = f32[16]{0:T(128)S(1)} copy-done((f32[16]{0:T(128)S(1)}, f32[16]{0:T(128)}, u32[]{:S(2)}) %copy-start.2) | copy-done | bytes 88
  2.3 1.4 %prepare.1 = (f32[3,16,8,256]{3,2,1,0:T(8,128)S(1)}, f32[1,16,8,256]{3,2,1,0:T(8,128)S(1)}, f32[1,16,8,256]{3,2,1,0:T(8,128)S(1)}, f32[1,16,8,256]{3,2,1,0:T(8,128)S(1)}) custom-call(f32[16,2,3,4,256]{4,3,2,1,0:T(4,128)S(1)} %bitcast.8, s32[4,32]{1,0:T(4,128)S(1)} %bitcast.9, f32[16]{0:T(128)S(1)} %copy-done.2), custom_call_target="tpu_custom_call" | custom-call | tf_op jit(solution)/shard_map/prepare/pallas_call | solution.py:101
  3.7 0.5 collective-permute-start.4
  4.2 2.6 %collective-permute-start.3 = (f32[3,16,8,256]{3,2,1,0:T(8,128)S(1)}, f32[3,16,8,256]{3,2,1,0:T(8,128)S(1)}, u32[]{:S(2)}, u32[]{:S(2)}) collective-permute-start(f32[3,16,8,256]{3,2,1,0:T(8,128)S(1)} %get-tuple-element.38.refs_3_), channel_id=1, source_target_pairs={{0,12},{4,8},{8,4},{12,0},{1,13},{5,9},{9,5},{13,1},{2,14},{6,10},... | collective-permute-start | bytes 1179656 | tf_op jit(solution)/shard_map/ppermute | solution.py:293
  6.9 3.6 %collective-permute-start = (f32[1,16,8,256]{3,2,1,0:T(8,128)S(1)}, f32[1,16,8,256]{3,2,1,0:T(8,128)S(1)}, u32[]{:S(2)}, u32[]{:S(2)}) collective-permute-start(f32[1,16,8,256]{3,2,1,0:T(8,128)S(1)} %get-tuple-element.35), channel_id=1, source_target_pairs={{0,3},{1,2},{2,1},{3,0},{4,7},{5,6},{6,5},{7,4},{8,11},{9,10},{10,... | collective-permute-start | bytes 393224 | tf_op jit(solution)/shard_map/ppermute | solution.py:296
  10.5 0.2 collective-permute-start.1
  10.7 3.6 %collective-permute-start.2 = (f32[1,16,8,256]{3,2,1,0:T(8,128)S(1)}, f32[1,16,8,256]{3,2,1,0:T(8,128)S(1)}, u32[]{:S(2)}, u32[]{:S(2)}) collective-permute-start(f32[1,16,8,256]{3,2,1,0:T(8,128)S(1)} %get-tuple-element.37), channel_id=1, source_target_pairs={{0,3},{1,2},{2,1},{3,0},{4,7},{5,6},{6,5},{7,4},{8,11},{9,10},{10,... | collective-permute-start | bytes 393224 | tf_op jit(solution)/shard_map/ppermute | solution.py:296
  14.3 0.0 collective-permute-done.4.refs_4_
  14.3 0.7 %copy-done.3 = s32[4,1,256,2]{2,3,1,0:T(2,128)S(1)} copy-done((s32[4,1,256,2]{2,3,1,0:T(2,128)S(1)}, s32[4,1,256,2]{2,3,1,0:T(2,128)}, u32[]{:S(2)}) %copy-start.3) | copy-done | bytes 8216
  15.0 0.7 %copy-done.5 = s32[4,4]{1,0:T(4,128)S(1)} copy-done((s32[4,4]{1,0:T(4,128)S(1)}, s32[4,4]{1,0:T(4,128)}, u32[]{:S(2)}) %copy-start.5) | copy-done | bytes 88
  15.7 0.7 %copy-done.7 = s32[4]{0:T(128)S(1)} copy-done((s32[4]{0:T(128)S(1)}, s32[4]{0:T(128)}, u32[]{:S(2)}) %copy-start.7) | copy-done | bytes 40
  16.3 1.0 %copy-done.10 = bf16[2,256,512]{2,1,0:T(8,128)(2,1)S(1)} copy-done((bf16[2,256,512]{2,1,0:T(8,128)(2,1)S(1)}, bf16[2,256,512]{2,1,0:T(8,128)(2,1)}, u32[]{:S(2)}) %copy-start.10) | copy-done | bytes 524312
  17.4 4.3 %near_sums.2 = (f32[3,17,2,6,8,128]{5,4,3,2,1,0:T(8,128)S(1)}, f32[128,512]{1,0:T(8,128)S(1)}, f32[128,512]{1,0:T(8,128)S(1)}, f32[128,512]{1,0:T(8,128)S(1)}, f32[128,512]{1,0:T(8,128)S(1)}) custom-call(s32[4,4]{1,0:T(4,128)S(1)} %copy-done.5, s32[4]{0:T(128)S(1)} %copy-done.7, s32[4,1,2,256]{3,2,1,0:T(2,128)S(1)} %bitcast.10, ...), custom_call_target="tpu_custom_call" | custom-call | flops 4000000000 | bytes 1000000 | tf_op jit(solution)/shard_map/near_sums/pallas_call | solution.py:248
  21.7 0.0 collective-permute-done.3.refs_3_
  21.7 0.0 copy-done.6
  21.7 0.0 copy-done.11
  21.7 0.0 copy-start.4
  21.7 0.0 copy-start.8
  21.7 2.2 %far_sums.3 = (f32[3,17,2,6,8,128]{5,4,3,2,1,0:T(8,128)S(1)}, f32[128,512]{1,0:T(8,128)S(1)}, f32[128,512]{1,0:T(8,128)S(1)}, f32[128,512]{1,0:T(8,128)S(1)}, f32[128,512]{1,0:T(8,128)S(1)}) custom-call(s32[4,4]{1,0:T(4,128)S(1)} %copy-done.6, s32[4]{0:T(128)S(1)} %copy-done.7, ...), custom_call_target="tpu_custom_call", output_to_operand_aliasing={{0}: (5, {}), {1}: (6, {}), {2}: (7, {}), {3}: (8, {}), {4}... | custom-call | flops 2000000000 | bytes 1000000 | tf_op jit(solution)/shard_map/far_sums/pallas_call | solution.py:248
  23.9 0.0 collective-permute-done.refs_3_
  23.9 0.0 collective-permute-done.1.refs_4_
  23.9 0.0 collective-permute-done.2.refs_5_
  23.9 0.1 collective-permute-start.8
  24.0 0.5 collective-permute-start.9
  24.5 0.1 collective-permute-start.10
  24.6 0.6 %collective-permute-start.5 = (f32[1,16,8,256]{3,2,1,0:T(8,128)S(1)}, f32[1,16,8,256]{3,2,1,0:T(8,128)S(1)}, u32[]{:S(2)}, u32[]{:S(2)}) collective-permute-start(f32[1,16,8,256]{3,2,1,0:T(8,128)S(1)} %collective-permute-done.refs_3_), channel_id=1, source_target_pairs={{0,12},{4,8},{8,4},{12,0},{1,13},{5,9},{9,5},{13,1},{2,14},{6,10},... | collective-permute-start | bytes 393224 | tf_op jit(solution)/shard_map/ppermute | solution.py:293
  25.2 1.2 %collective-permute-start.6 = (f32[1,16,8,256]{3,2,1,0:T(8,128)S(1)}, f32[1,16,8,256]{3,2,1,0:T(8,128)S(1)}, u32[]{:S(2)}, u32[]{:S(2)}) collective-permute-start(f32[1,16,8,256]{3,2,1,0:T(8,128)S(1)} %collective-permute-done.1.refs_4_), channel_id=1, source_target_pairs={{0,12},{4,8},{8,4},{12,0},{1,13},{5,9},{9,5},{13,1},{2,14},{6,10},... | collective-permute-start | bytes 393224 | tf_op jit(solution)/shard_map/ppermute | solution.py:293
  26.3 0.0 collective-permute-done.8.refs_6_
  26.4 0.6 %collective-permute-start.7 = (f32[1,16,8,256]{3,2,1,0:T(8,128)S(1)}, f32[1,16,8,256]{3,2,1,0:T(8,128)S(1)}, u32[]{:S(2)}, u32[]{:S(2)}) collective-permute-start(f32[1,16,8,256]{3,2,1,0:T(8,128)S(1)} %collective-permute-done.2.refs_5_), channel_id=1, source_target_pairs={{0,12},{4,8},{8,4},{12,0},{1,13},{5,9},{9,5},{13,1},{2,14},{6,10},... | collective-permute-start | bytes 393224 | tf_op jit(solution)/shard_map/ppermute | solution.py:293
  26.9 0.0 collective-permute-done.9.refs_7_
  26.9 0.0 collective-permute-done.10.refs_8_
  26.9 0.0 copy-done.4
  27.0 0.0 copy-done.8
  27.0 4.5 %near_sums.3 = (f32[3,17,2,6,8,128]{5,4,3,2,1,0:T(8,128)S(1)}, f32[128,512]{1,0:T(8,128)S(1)}, f32[128,512]{1,0:T(8,128)S(1)}, f32[128,512]{1,0:T(8,128)S(1)}, f32[128,512]{1,0:T(8,128)S(1)}) custom-call(s32[4,4]{1,0:T(4,128)S(1)} %copy-done.6, s32[4]{0:T(128)S(1)} %copy-done.8, ...), custom_call_target="tpu_custom_call", output_to_operand_aliasing={{1}: (10, {}), {2}: (11, {}), {3}: (12, {}), {4}: (13, {})} | custom-call | flops 4000000000 | bytes 1000000 | tf_op jit(solution)/shard_map/near_sums/pallas_call | solution.py:248
  31.4 0.0 collective-permute-done.5.refs_3_
  31.5 1.2 %collective-permute-done.6.refs_4_ = f32[1,16,8,256]{3,2,1,0:T(8,128)S(1)} collective-permute-done((f32[1,16,8,256]{3,2,1,0:T(8,128)S(1)}, f32[1,16,8,256]{3,2,1,0:T(8,128)S(1)}, u32[]{:S(2)}, u32[]{:S(2)}) %collective-permute-start.6) | collective-permute-done | bytes 131104 | tf_op jit(solution)/shard_map/ppermute | solution.py:293
  32.6 2.8 %collective-permute-done.7.refs_5_ = f32[1,16,8,256]{3,2,1,0:T(8,128)S(1)} collective-permute-done((f32[1,16,8,256]{3,2,1,0:T(8,128)S(1)}, f32[1,16,8,256]{3,2,1,0:T(8,128)S(1)}, u32[]{:S(2)}, u32[]{:S(2)}) %collective-permute-start.7) | collective-permute-done | bytes 131104 | tf_op jit(solution)/shard_map/ppermute | solution.py:293
  35.4 1.2 %far_sums.4 = (f32[3,17,2,6,8,128]{5,4,3,2,1,0:T(8,128)S(1)}, f32[128,512]{1,0:T(8,128)S(1)}, f32[128,512]{1,0:T(8,128)S(1)}) custom-call(s32[4,4]{1,0:T(4,128)S(1)} %copy-done.6, s32[4]{0:T(128)S(1)} %copy-done.8, s32[4,1,2,256]{3,2,1,0:T(2,128)S(1)} %bitcast.13, ...), custom_call_target="tpu_custom_call", output_to_operand_aliasing={{0}: (7, {}), {1}: (8, {}), {2}: (9, {})} | custom-call | flops 2000000000 | bytes 1000000 | tf_op jit(solution)/shard_map/far_sums/pallas_call | solution.py:248
  36.6 0.0 copy-start.9
  36.7 1.7 %far_sums.5 = (f32[128,512]{1,0:T(8,128)S(1)}, f32[128,512]{1,0:T(8,128)S(1)}) custom-call(s32[4,4]{1,0:T(4,128)S(1)} %copy-done.6, s32[4]{0:T(128)S(1)} %copy-done.8, s32[4,1,2,256]{3,2,1,0:T(2,128)S(1)} %bitcast.14, f32[3,17,2,6,8,128]{5,4,3,2,1,0:T(8,128)S(1)} %get-tuple-element.60.refs_3_, ...), custom_call_target="tpu_custom_call", output_to_operand_aliasing={{0}: (4, {}), {1}: (5, {})} | custom-call | flops 2000000000 | bytes 1000000 | tf_op jit(solution)/shard_map/far_sums/pallas_call | solution.py:248
  38.4 3.8 %collective-permute-start.12 = (f32[128,512]{1,0:T(8,128)S(1)}, f32[128,512]{1,0:T(8,128)S(1)}, u32[]{:S(2)}, u32[]{:S(2)}) collective-permute-start(f32[128,512]{1,0:T(8,128)S(1)} %get-tuple-element.64), channel_id=1, source_target_pairs={{0,1},{1,0},{2,3},{3,2},{4,5},{5,4},{6,7},{7,6},{8,9},{9,8},{10,11... | collective-permute-start | bytes 786440 | tf_op jit(solution)/shard_map/ppermute | solution.py:348
  42.2 0.1 collective-permute-start.11
  42.3 7.1 %collective-permute-done.12.late_swapped_ref = f32[128,512]{1,0:T(8,128)S(1)} collective-permute-done((f32[128,512]{1,0:T(8,128)S(1)}, f32[128,512]{1,0:T(8,128)S(1)}, u32[]{:S(2)}, u32[]{:S(2)}) %collective-permute-start.12) | collective-permute-done | bytes 262176 | tf_op jit(solution)/shard_map/ppermute | solution.py:348
  49.4 4.4 %collective-permute-done.11.early_swapped_ref = f32[128,512]{1,0:T(8,128)S(1)} collective-permute-done((f32[128,512]{1,0:T(8,128)S(1)}, f32[128,512]{1,0:T(8,128)S(1)}, u32[]{:S(2)}, u32[]{:S(2)}) %collective-permute-start.11) | collective-permute-done | bytes 262176 | tf_op jit(solution)/shard_map/ppermute | solution.py:348
  53.8 0.0 copy-done.9
  53.8 1.4 %finish.1 = f32[256,512]{1,0:T(8,128)} custom-call(f32[128,512]{1,0:T(8,128)S(1)} %get-tuple-element.58.early_ref, f32[128,512]{1,0:T(8,128)S(1)} %collective-permute-done.11.early_swapped_ref, f32[128,512]{1,0:T(8,128)S(1)} %get-tuple-element.63.late_ref, f32[128,512]{1,0:T(8,128)S(1)} %collective-permute-done.12.late_swapped_ref, ...), custom_call_target="tpu_custom_call" | custom-call | flops 1000000000 | bytes 1000000 | tf_op jit(solution)/shard_map/finish/pallas_call | solution.py:269
  (9 shorter events, 0.0 us)
Async XLA Ops:
  0.0 1.0 %copy-start = (f32[32,4,3,256]{3,1,2,0:T(4,128)S(1)}, f32[32,4,3,256]{3,1,2,0:T(4,128)}, u32[]{:S(2)}) copy-start(f32[32,4,3,256]{3,1,2,0:T(4,128)} %param.8) | copy-start | bytes 1179652
  1.0 0.7 %copy-start.1 = (s32[32,4]{0,1:T(4,128)S(1)}, s32[32,4]{0,1:T(4,128)}, u32[]{:S(2)}) copy-start(s32[32,4]{0,1:T(4,128)} %param.9) | copy-start | bytes 1540
  1.7 0.7 %copy-start.2 = (f32[16]{0:T(128)S(1)}, f32[16]{0:T(128)}, u32[]{:S(2)}) copy-start(f32[16]{0:T(128)} %weight_ref.1) | copy-start | bytes 196
  3.7 10.6 %collective-permute-start.4 = (f32[3,16,8,256]{3,2,1,0:T(8,128)S(1)}, f32[3,16,8,256]{3,2,1,0:T(8,128)S(1)}, u32[]{:S(2)}, u32[]{:S(2)}) collective-permute-start(f32[3,16,8,256]{3,2,1,0:T(8,128)S(1)} %get-tuple-element.38.refs_3_), channel_id=1, source_target_pairs={{0,4},{4,0},{8,12},{12,8},{1,5},{5,1},{9,13},{13,9},{2,6},{6,2},{1... | collective-permute-start | bytes 1179656 | tf_op jit(solution)/shard_map/ppermute | solution.py:290
  4.2 17.5 %collective-permute-start.3 = (f32[3,16,8,256]{3,2,1,0:T(8,128)S(1)}, f32[3,16,8,256]{3,2,1,0:T(8,128)S(1)}, u32[]{:S(2)}, u32[]{:S(2)}) collective-permute-start(f32[3,16,8,256]{3,2,1,0:T(8,128)S(1)} %get-tuple-element.38.refs_3_), channel_id=1, source_target_pairs={{0,12},{4,8},{8,4},{12,0},{1,13},{5,9},{9,5},{13,1},{2,14},{6,10},... | collective-permute-start | bytes 1179656 | tf_op jit(solution)/shard_map/ppermute | solution.py:293
  6.9 17.1 %collective-permute-start = (f32[1,16,8,256]{3,2,1,0:T(8,128)S(1)}, f32[1,16,8,256]{3,2,1,0:T(8,128)S(1)}, u32[]{:S(2)}, u32[]{:S(2)}) collective-permute-start(f32[1,16,8,256]{3,2,1,0:T(8,128)S(1)} %get-tuple-element.35), channel_id=1, source_target_pairs={{0,3},{1,2},{2,1},{3,0},{4,7},{5,6},{6,5},{7,4},{8,11},{9,10},{10,... | collective-permute-start | bytes 393224 | tf_op jit(solution)/shard_map/ppermute | solution.py:296
  10.5 13.5 %collective-permute-start.1 = (f32[1,16,8,256]{3,2,1,0:T(8,128)S(1)}, f32[1,16,8,256]{3,2,1,0:T(8,128)S(1)}, u32[]{:S(2)}, u32[]{:S(2)}) collective-permute-start(f32[1,16,8,256]{3,2,1,0:T(8,128)S(1)} %get-tuple-element.36), channel_id=1, source_target_pairs={{0,3},{1,2},{2,1},{3,0},{4,7},{5,6},{6,5},{7,4},{8,11},{9,10},{10,... | collective-permute-start | bytes 393224 | tf_op jit(solution)/shard_map/ppermute | solution.py:296
  10.7 13.3 %collective-permute-start.2 = (f32[1,16,8,256]{3,2,1,0:T(8,128)S(1)}, f32[1,16,8,256]{3,2,1,0:T(8,128)S(1)}, u32[]{:S(2)}, u32[]{:S(2)}) collective-permute-start(f32[1,16,8,256]{3,2,1,0:T(8,128)S(1)} %get-tuple-element.37), channel_id=1, source_target_pairs={{0,3},{1,2},{2,1},{3,0},{4,7},{5,6},{6,5},{7,4},{8,11},{9,10},{10,... | collective-permute-start | bytes 393224 | tf_op jit(solution)/shard_map/ppermute | solution.py:296
  14.3 0.7 %copy-start.3 = (s32[4,1,256,2]{2,3,1,0:T(2,128)S(1)}, s32[4,1,256,2]{2,3,1,0:T(2,128)}, u32[]{:S(2)}) copy-start(s32[4,1,256,2]{2,3,1,0:T(2,128)} %param.12) | copy-start | bytes 24580
  15.0 0.7 %copy-start.5 = (s32[4,4]{1,0:T(4,128)S(1)}, s32[4,4]{1,0:T(4,128)}, u32[]{:S(2)}) copy-start(s32[4,4]{1,0:T(4,128)} %refs_0_.9) | copy-start | bytes 196
  15.7 0.7 %copy-start.7 = (s32[4]{0:T(128)S(1)}, s32[4]{0:T(128)}, u32[]{:S(2)}) copy-start(s32[4]{0:T(128)} %refs_1_.9) | copy-start | bytes 52
  16.3 1.0 %copy-start.10 = (bf16[2,256,512]{2,1,0:T(8,128)(2,1)S(1)}, bf16[2,256,512]{2,1,0:T(8,128)(2,1)}, u32[]{:S(2)}) copy-start(bf16[2,256,512]{2,1,0:T(8,128)(2,1)} %constant.4.clone.refs_5_.refs_4_.refs_9_.refs_6_) | copy-start | bytes 1572868
  17.4 4.3 %copy-start.6 = (s32[4,4]{1,0:T(4,128)S(1)}, s32[4,4]{1,0:T(4,128)}, u32[]{:S(2)}) copy-start(s32[4,4]{1,0:T(4,128)} %refs_0_.9) | copy-start | bytes 196
  17.4 4.4 %copy-start.11 = (bf16[2,256,512]{2,1,0:T(8,128)(2,1)S(1)}, bf16[2,256,512]{2,1,0:T(8,128)(2,1)}, u32[]{:S(2)}) copy-start(bf16[2,256,512]{2,1,0:T(8,128)(2,1)} %constant.4.clone.refs_5_.refs_4_.refs_9_.refs_6_) | copy-start | bytes 1572868
  21.7 5.2 %copy-start.4 = (s32[4,1,256,2]{2,3,1,0:T(2,128)S(1)}, s32[4,1,256,2]{2,3,1,0:T(2,128)}, u32[]{:S(2)}) copy-start(s32[4,1,256,2]{2,3,1,0:T(2,128)} %param.12) | copy-start | bytes 24580
  21.7 5.2 %copy-start.8 = (s32[4]{0:T(128)S(1)}, s32[4]{0:T(128)}, u32[]{:S(2)}) copy-start(s32[4]{0:T(128)} %refs_1_.9) | copy-start | bytes 52
  23.9 2.4 %collective-permute-start.8 = (f32[1,16,8,256]{3,2,1,0:T(8,128)S(1)}, f32[1,16,8,256]{3,2,1,0:T(8,128)S(1)}, u32[]{:S(2)}, u32[]{:S(2)}) collective-permute-start(f32[1,16,8,256]{3,2,1,0:T(8,128)S(1)} %collective-permute-done.refs_3_), channel_id=1, source_target_pairs={{0,4},{4,0},{8,12},{12,8},{1,5},{5,1},{9,13},{13,9},{2,6},{6,2},{1... | collective-permute-start | bytes 393224 | tf_op jit(solution)/shard_map/ppermute | solution.py:290
  24.0 2.9 %collective-permute-start.9 = (f32[1,16,8,256]{3,2,1,0:T(8,128)S(1)}, f32[1,16,8,256]{3,2,1,0:T(8,128)S(1)}, u32[]{:S(2)}, u32[]{:S(2)}) collective-permute-start(f32[1,16,8,256]{3,2,1,0:T(8,128)S(1)} %collective-permute-done.1.refs_4_), channel_id=1, source_target_pairs={{0,4},{4,0},{8,12},{12,8},{1,5},{5,1},{9,13},{13,9},{2,6},{6,2},{1... | collective-permute-start | bytes 393224 | tf_op jit(solution)/shard_map/ppermute | solution.py:290
  24.5 2.4 %collective-permute-start.10 = (f32[1,16,8,256]{3,2,1,0:T(8,128)S(1)}, f32[1,16,8,256]{3,2,1,0:T(8,128)S(1)}, u32[]{:S(2)}, u32[]{:S(2)}) collective-permute-start(f32[1,16,8,256]{3,2,1,0:T(8,128)S(1)} %collective-permute-done.2.refs_5_), channel_id=1, source_target_pairs={{0,4},{4,0},{8,12},{12,8},{1,5},{5,1},{9,13},{13,9},{2,6},{6,2},{1... | collective-permute-start | bytes 393224 | tf_op jit(solution)/shard_map/ppermute | solution.py:290
  24.6 6.8 %collective-permute-start.5 = (f32[1,16,8,256]{3,2,1,0:T(8,128)S(1)}, f32[1,16,8,256]{3,2,1,0:T(8,128)S(1)}, u32[]{:S(2)}, u32[]{:S(2)}) collective-permute-start(f32[1,16,8,256]{3,2,1,0:T(8,128)S(1)} %collective-permute-done.refs_3_), channel_id=1, source_target_pairs={{0,12},{4,8},{8,4},{12,0},{1,13},{5,9},{9,5},{13,1},{2,14},{6,10},... | collective-permute-start | bytes 393224 | tf_op jit(solution)/shard_map/ppermute | solution.py:293
  25.2 7.4 %collective-permute-start.6 = (f32[1,16,8,256]{3,2,1,0:T(8,128)S(1)}, f32[1,16,8,256]{3,2,1,0:T(8,128)S(1)}, u32[]{:S(2)}, u32[]{:S(2)}) collective-permute-start(f32[1,16,8,256]{3,2,1,0:T(8,128)S(1)} %collective-permute-done.1.refs_4_), channel_id=1, source_target_pairs={{0,12},{4,8},{8,4},{12,0},{1,13},{5,9},{9,5},{13,1},{2,14},{6,10},... | collective-permute-start | bytes 393224 | tf_op jit(solution)/shard_map/ppermute | solution.py:293
  26.4 9.1 %collective-permute-start.7 = (f32[1,16,8,256]{3,2,1,0:T(8,128)S(1)}, f32[1,16,8,256]{3,2,1,0:T(8,128)S(1)}, u32[]{:S(2)}, u32[]{:S(2)}) collective-permute-start(f32[1,16,8,256]{3,2,1,0:T(8,128)S(1)} %collective-permute-done.2.refs_5_), channel_id=1, source_target_pairs={{0,12},{4,8},{8,4},{12,0},{1,13},{5,9},{9,5},{13,1},{2,14},{6,10},... | collective-permute-start | bytes 393224 | tf_op jit(solution)/shard_map/ppermute | solution.py:293
  36.6 17.2 %copy-start.9 = (bf16[2,512,512]{2,1,0:T(8,128)(2,1)S(1)}, bf16[2,512,512]{2,1,0:T(8,128)(2,1)}, u32[]{:S(2)}) copy-start(bf16[2,512,512]{2,1,0:T(8,128)(2,1)} %constant.5.clone.table_ref) | copy-start | bytes 3145732
  38.4 11.0 %collective-permute-start.12 = (f32[128,512]{1,0:T(8,128)S(1)}, f32[128,512]{1,0:T(8,128)S(1)}, u32[]{:S(2)}, u32[]{:S(2)}) collective-permute-start(f32[128,512]{1,0:T(8,128)S(1)} %get-tuple-element.64), channel_id=1, source_target_pairs={{0,1},{1,0},{2,3},{3,2},{4,5},{5,4},{6,7},{7,6},{8,9},{9,8},{10,11... | collective-permute-start | bytes 786440 | tf_op jit(solution)/shard_map/ppermute | solution.py:348
  42.2 11.6 %collective-permute-start.11 = (f32[128,512]{1,0:T(8,128)S(1)}, f32[128,512]{1,0:T(8,128)S(1)}, u32[]{:S(2)}, u32[]{:S(2)}) collective-permute-start(f32[128,512]{1,0:T(8,128)S(1)} %get-tuple-element.59), channel_id=1, source_target_pairs={{0,1},{1,0},{2,3},{3,2},{4,5},{5,4},{6,7},{7,6},{8,9},{9,8},{10,11... | collective-permute-start | bytes 786440 | tf_op jit(solution)/shard_map/ppermute | solution.py:348

commit v4 on v3

v4 whole, which is shorter than its diff:
```python
import math

import jax
import jax.numpy as jnp
import ml_dtypes
import numpy as np
from jax import lax
from jax.experimental import pallas as pl
from jax.experimental.pallas import tpu as pltpu
from jax.sharding import PartitionSpec as P

epsilon = 1e-06
SUB, LANES = 8, 128
HALF = SUB // 2
VMEM_BYTES = 40 * 1024 * 1024
PREPARE_VMEM_BYTES = 62 * 1024 * 1024
F32 = jnp.float32
BF16 = jnp.bfloat16


def split_table(table):
    high = table.astype(ml_dtypes.bfloat16)
    low = (table - high.astype(np.float64)).astype(ml_dtypes.bfloat16)
    return np.stack([high, low])


def forward_table(samples):
    steps = np.arange(samples)
    angles = (steps[:, None] * steps[None, :] % (2 * samples)) * (math.pi / samples)
    return split_table(np.concatenate([np.cos(angles), -np.sin(angles)], axis=1))


def inverse_table(samples):
    record = 2 * samples
    bins = np.arange(samples)
    lags = (np.arange(record) + samples) % record
    angles = (bins[:, None] * lags[None, :] % record) * (math.pi / samples)
    gain = np.where(bins == 0, 1.0, 2.0)[:, None] / record
    return split_table(np.concatenate([gain * np.cos(angles), -gain * np.sin(angles)], axis=0))


def split_dot(value, table_ref):
    rows = value.shape[0]
    high = value.astype(BF16)
    low = (value - high.astype(F32)).astype(BF16)
    both = jnp.dot(jnp.concatenate([high, low], axis=0), table_ref[0], preferred_element_type=F32)
    return both[:rows] + (both[rows:] + jnp.dot(high, table_ref[1], preferred_element_type=F32))


def prepare_kernel(waves_hbm, mask_hbm, weight_hbm, all_ref, *refs):
    *piece_refs, waves_ref, mask_ref, weight_ref, sems = refs
    copies = [
        pltpu.make_async_copy(weight_hbm, weight_ref, sems.at[0]),
        pltpu.make_async_copy(mask_hbm, mask_ref, sems.at[1]),
        pltpu.make_async_copy(waves_hbm, waves_ref, sems.at[2]),
    ]
    for copy in copies:
        copy.start()
    twos, _, channels, stations, _ = waves_ref.shape
    events = 2 * twos
    rows = 3 * SUB * twos
    row = lax.broadcasted_iota(jnp.int32, (rows, events), 0)
    group, row_here = row // (SUB * twos), row % (SUB * twos)
    event_of_row = jnp.where(group < 2, 2 * (row_here // SUB) + group, row_here // HALF)
    at_event = (event_of_row == lax.broadcasted_iota(jnp.int32, (rows, events), 1)).astype(F32)
    row = lax.broadcasted_iota(jnp.int32, (rows, stations), 0)
    at_station = row % HALF == lax.broadcasted_iota(jnp.int32, (rows, stations), 1)
    station_id = lax.broadcasted_iota(jnp.int32, (stations, events), 0)
    first_weight = lax.axis_index("station") * stations
    copies[0].wait()
    network = channels * sum(weight_ref[station] for station in range(weight_ref.shape[0]))
    weight = jnp.zeros((stations, events), F32)
    for station in range(stations):
        weight = jnp.where(station_id == station, weight_ref[first_weight + station], weight)
    copies[1].wait()
    amplitude = mask_ref[...].astype(F32) * jnp.sqrt(weight / network)
    picked = lax.dot_general(
        at_event,
        amplitude,
        (((1,), (1,)), ((), ())),
        precision=lax.Precision.HIGHEST,
        preferred_element_type=F32,
    )
    factor = jnp.sum(jnp.where(at_station, picked, 0.0), axis=1, keepdims=True).reshape(3, twos, SUB, 1)
    copies[2].wait()
    for group in range(3):
        for side in range(2):
            part = waves_ref[:, group, side] if group < 2 else waves_ref[:, side, 2]
            all_ref[group, :, side * HALF : (side + 1) * HALF, :] = part
        traces = all_ref[group]
        energy = jnp.sum(traces * traces, axis=-1, keepdims=True)
        traces = traces * (lax.rsqrt(energy + epsilon) * factor[group])
        all_ref[group] = traces
        for piece, piece_ref in enumerate(piece_refs):
            piece_ref[group] = traces[piece * twos // 2 : (piece + 1) * twos // 2]


def prepare(waveforms, event_mask, station_weight):
    events, stations, channels, samples = waveforms.shape
    waves = jnp.transpose(waveforms, (0, 2, 1, 3)).reshape(events // 2, 2, channels, stations, samples)
    hbm = pl.BlockSpec(memory_space=pltpu.HBM)
    vmem = pl.BlockSpec(memory_space=pltpu.VMEM)
    return pl.pallas_call(
        prepare_kernel,
        out_shape=[jax.ShapeDtypeStruct((3, events // share, SUB, samples), F32) for share in (2, 4, 4)],
        in_specs=[hbm] * 3,
        out_specs=[vmem] * 3,
        scratch_shapes=[
            pltpu.VMEM(waves.shape, F32),
            pltpu.VMEM((stations, events), event_mask.dtype),
            pltpu.SMEM(station_weight.shape, F32),
            pltpu.SemaphoreType.DMA((3,)),
        ],
        compiler_params=pltpu.CompilerParams(vmem_limit_bytes=PREPARE_VMEM_BYTES),
        name="prepare",
    )(waves, event_mask.T, station_weight)


def index_kernel(events, partners_ref, counts_ref, pairs_ref, index_ref):
    rounds, _, _, all_pairs = pairs_ref.shape
    here = lax.axis_index("cluster")
    sibling = jnp.where(here % 2 == 0, here + 1, here - 1)
    own_count = counts_ref[here]
    for turn in range(rounds):
        partner = partners_ref[turn, here]
        part = jnp.where(partner == here, 0, jnp.where(partner == sibling, 1, 2))
        first, second = pairs_ref[turn, 0, 0:1], pairs_ref[turn, 0, 1:2]
        valid = (first < own_count) & (second < counts_ref[partner])
        index_ref[turn, 0:1] = jnp.where(valid, first, events)
        index_ref[turn, 1:2] = second + part * (events + 2)
        index_ref[turn, 2:3] = jnp.full((1, all_pairs), part, jnp.int32)


def pair_index(partners, counts, pair_list, events):
    rounds, _, all_pairs, _ = pair_list.shape
    vmem = pl.BlockSpec(memory_space=pltpu.VMEM)
    smem = pl.BlockSpec(memory_space=pltpu.SMEM)
    return pl.pallas_call(
        lambda *refs: index_kernel(events, *refs),
        out_shape=jax.ShapeDtypeStruct((rounds, 3, all_pairs), jnp.int32),
        in_specs=[smem, smem, vmem],
        out_specs=vmem,
        compiler_params=pltpu.CompilerParams(vmem_limit_bytes=VMEM_BYTES),
        name="pair_index",
    )(partners, counts, jnp.transpose(pair_list, (0, 1, 3, 2)))


def fill_spectra(traces_ref, part, piece, table_ref, spectra_ref):
    _, twos, _, samples = traces_ref.shape
    spot = pl.ds(piece * twos, twos)
    spectrum = split_dot(traces_ref[...].reshape(3 * twos * SUB, samples), table_ref)
    tiles = [
        spectrum[:, block * LANES : (block + 1) * LANES].reshape(3, twos, SUB, LANES) for block in range(4)
    ]
    for group in range(2):
        for block in range(4):
            spectra_ref[part, spot, group, block + block // 2] = tiles[block][group]
    low_half = lax.broadcasted_iota(jnp.int32, (twos, SUB, LANES), 1) < HALF
    for side in range(2):
        lower, upper = tiles[2 * side][2], tiles[2 * side + 1][2]
        turned_lower, turned_upper = pltpu.roll(lower, HALF, 1), pltpu.roll(upper, HALF, 1)
        spectra_ref[part, spot, 0, 3 * side + 2] = jnp.where(low_half, lower, turned_upper)
        spectra_ref[part, spot, 1, 3 * side + 2] = jnp.where(low_half, turned_lower, upper)


def clear_last(spectra_ref):
    spectra_ref[0, spectra_ref.shape[1] - 1] = jnp.zeros(spectra_ref.shape[2:], F32)


def spectra_kernel(places, first, *refs):
    trace_refs, table_ref, spectra_ref = refs[: len(places)], refs[len(places)], refs[-1]
    for (part, piece), traces_ref in zip(places, trace_refs, strict=True):
        fill_spectra(traces_ref, part, piece, table_ref, spectra_ref)
    if first:
        clear_last(spectra_ref)


def add_pairs(index_ref, turns, wanted, spectra_ref, base_refs, out_refs, sums_ref):
    _, _, all_pairs = index_ref.shape
    slots = 2 * spectra_ref.shape[1]
    length = lax.axis_size("station")
    station_here = lax.axis_index("station")
    blocks = length // 2
    block_pairs = all_pairs // length
    flat_ref = spectra_ref.reshape(spectra_ref.shape[0] * slots, 6, SUB, LANES)
    low_half = lax.broadcasted_iota(jnp.int32, (SUB, LANES), 0) < HALF

    def folded(lower, upper, both):
        turned = pltpu.roll(jnp.where(low_half, upper, lower), HALF, 0)
        return jnp.where(low_half, lower, upper) + turned + both

    def one_turn(place, turn):
        for block in range(blocks):
            if len(out_refs) == 2:
                source = station_here if block == 0 else station_here + 1 - 2 * (station_here % 2)
            else:
                source = station_here // blocks * blocks + block
            start = source * block_pairs

            def one_pair(pair, carry):
                left = flat_ref.at[index_ref[turn, 0, start + pair]]
                right = flat_ref.at[index_ref[turn, 1, start + pair]]
                real, imag = [], []
                for tile in range(3):
                    left_real, left_imag = left[tile], left[tile + 3]
                    right_real, right_imag = right[tile], right[tile + 3]
                    real.append(left_real * right_real + left_imag * right_imag)
                    imag.append(left_imag * right_real - left_real * right_imag)
                spot = pl.multiple_of(pair * SUB, SUB)
                sums_ref[0, pl.ds(spot, SUB), :] = folded(*real)
                sums_ref[1, pl.ds(spot, SUB), :] = folded(*imag)
                return carry

            lax.fori_loop(0, block_pairs, one_pair, 0, unroll=min(16, block_pairs))
            if len(out_refs) == 2:
                which, row = block, place * block_pairs
            else:
                which, row = 0, (place * blocks + block) * block_pairs
            for side in range(2):
                for half in range(2):
                    spot = pl.ds((2 * side + half) * LANES, LANES)
                    total = None if base_refs is None else base_refs[which][row : row + block_pairs, spot]
                    for lane_row in range(HALF):
                        piece = sums_ref[side, pl.ds(half * HALF + lane_row, block_pairs, stride=SUB), :]
                        total = piece if total is None else total + piece
                    out_refs[which][row : row + block_pairs, spot] = total

    for place, turn in enumerate(turns):
        pl.when(wanted(index_ref[turn, 2, 0]))(lambda: one_turn(place, turn))


def half_turns(rounds, half):
    return range(half * rounds // 2, (half + 1) * rounds // 2)


def first_near_kernel(outs, index_ref, own_ref, sibling_ref, table_ref, spectra_ref, *refs):
    out_refs, sums_ref = refs[:-1], refs[-1]
    fill_spectra(own_ref, 0, 0, table_ref, spectra_ref)
    fill_spectra(sibling_ref, 1, 0, table_ref, spectra_ref)
    clear_last(spectra_ref)
    for half in range(2):
        turns = half_turns(index_ref.shape[0], half)
        some = out_refs[half * outs : (half + 1) * outs]
        add_pairs(index_ref, turns, lambda part: part < 2, spectra_ref, None, some, sums_ref)


def first_far_kernel(outs, index_ref, across_ref, table_ref, *refs):
    spectra_ref, out_refs, sums_ref = refs[2 * outs + 1], refs[2 * outs + 2 : -1], refs[-1]
    fill_spectra(across_ref, 2, 0, table_ref, spectra_ref)
    for half in range(2):
        turns = half_turns(index_ref.shape[0], half)
        some = out_refs[half * outs : (half + 1) * outs]
        add_pairs(index_ref, turns, lambda part: part == 2, spectra_ref, None, some, sums_ref)


def near_kernel(outs, index_ref, sibling_ref, table_ref, *refs):
    base_refs, refs = refs[1 : 2 * outs + 1], refs[2 * outs + 1 :]
    spectra_ref, out_refs, sums_ref = refs[0], refs[1:-1], refs[-1]
    fill_spectra(sibling_ref, 1, 1, table_ref, spectra_ref)
    for half in range(2):
        turns = half_turns(index_ref.shape[0], half)
        some = slice(half * outs, (half + 1) * outs)
        add_pairs(index_ref, turns, lambda part: part < 2, spectra_ref, base_refs[some], out_refs[some], sums_ref)


def far_kernel(outs, half, index_ref, *refs):
    if half == 0:
        across_ref, table_ref, _, *refs = refs
        base_refs, spectra_ref, refs = refs[:outs], refs[outs], refs[outs + 1 :]
        fill_spectra(across_ref, 2, 1, table_ref, spectra_ref)
    else:
        spectra_ref, base_refs, refs = refs[0], refs[1 : outs + 1], refs[outs + 1 :]
    out_refs, sums_ref = refs[:-1], refs[-1]
    turns = half_turns(index_ref.shape[0], half)
    add_pairs(index_ref, turns, lambda part: part == 2, spectra_ref, base_refs, out_refs, sums_ref)


def call_kernel(kernel, name, operands, specs, updated, out_shapes, scratch, flops):
    vmem = pl.BlockSpec(memory_space=pltpu.VMEM)
    operands = [*operands, *updated]
    shapes = [*(jax.ShapeDtypeStruct(value.shape, value.dtype) for value in updated), *out_shapes]
    first_in = len(operands) - len(updated)
    in_specs = [vmem] * len(operands)
    out_specs = [vmem] * len(shapes)
    for place, spec in specs.items():
        in_specs[place] = spec
        if place >= first_in:
            out_specs[place - first_in] = spec
    return pl.pallas_call(
        kernel,
        out_shape=shapes,
        in_specs=in_specs,
        out_specs=out_specs,
        scratch_shapes=scratch,
        input_output_aliases={first_in + i: i for i in range(len(updated))},
        compiler_params=pltpu.CompilerParams(vmem_limit_bytes=VMEM_BYTES),
        cost_estimate=pl.CostEstimate(flops=flops, bytes_accessed=flops // 1000, transcendentals=0),
        name=name,
    )(*operands)


def finish_kernel(early_ref, early_swapped_ref, late_ref, late_swapped_ref, table_ref, out_ref):
    rows = early_ref.shape[0]
    out_ref[:rows] = split_dot(early_ref[...] + early_swapped_ref[...], table_ref)
    out_ref[rows:] = split_dot(late_ref[...] + late_swapped_ref[...], table_ref)


def finish(values, table):
    rows, lags = values[0].shape
    return pl.pallas_call(
        finish_kernel,
        out_shape=jax.ShapeDtypeStruct((2 * rows, lags), F32),
        compiler_params=pltpu.CompilerParams(vmem_limit_bytes=VMEM_BYTES),
        cost_estimate=pl.CostEstimate(flops=10**9, bytes_accessed=10**6, transcendentals=0),
        name="finish",
    )(*values, table)


def on_device(waveforms, event_mask, station_weight, partners, pair_list, counts):
    events, stations, channels, samples = waveforms.shape
    rounds, _, all_pairs, _ = pair_list.shape
    clusters = lax.axis_size("cluster")
    length = lax.axis_size("station")
    assert (stations, channels, samples) == (HALF, 3, 2 * LANES)
    assert events % 4 == 0 and rounds % 2 == 0 and clusters % 2 == 0 and length % 4 == 0
    forward = jnp.asarray(forward_table(samples))
    inverse = jnp.asarray(inverse_table(samples))

    def to_sibling(value):
        return lax.ppermute(value, "cluster", [(i, i ^ 1) for i in range(clusters)])

    def to_across(value):
        return lax.ppermute(value, "cluster", [(i, (i + 1 if i % 2 else i - 1) % clusters) for i in range(clusters)])

    def to_mirror(value):
        return lax.ppermute(value, "station", [(i, length - 1 - i) for i in range(length)])

    swap = length == 4
    outs = 2 if swap else 1
    half_shape = jax.ShapeDtypeStruct((rounds * all_pairs // 4 // outs, 2 * samples), F32)
    spectra_shape = jax.ShapeDtypeStruct((3, events // 2 + 1, 2, 6, SUB, LANES), F32)
    sums = pltpu.VMEM((2, all_pairs // length * SUB, LANES), F32)

    smem = {0: pl.BlockSpec(memory_space=pltpu.SMEM)}

    def add_spectra(traces, places, spectra, flops):
        return call_kernel(
            lambda *refs: spectra_kernel(places, not spectra, *refs),
            "add_spectra",
            [*traces, forward],
            {},
            spectra,
            [] if spectra else [spectra_shape],
            [],
            flops,
        )

    own, first_piece, last_piece = prepare(waveforms, event_mask, station_weight)
    index = pair_index(partners, counts, pair_list, events)
    mirror_first = to_mirror(first_piece)
    mirror_last = to_mirror(last_piece)
    across = to_across(own)
    sibling = to_sibling(own)
    spectra, *partial = call_kernel(
        lambda *refs: first_near_kernel(outs, *refs),
        "first_near",
        [index, own, sibling, forward],
        smem,
        [],
        [spectra_shape] + [half_shape] * (2 * outs),
        [sums],
        1,
    )
    _, *partial = call_kernel(
        lambda *refs: first_far_kernel(outs, *refs),
        "first_far",
        [index, across, forward],
        smem,
        [spectra, *partial],
        [],
        [sums],
        1,
    )
    mirror_first, *partial = lax.optimization_barrier((mirror_first, *partial))
    far_first, near_first = to_across(mirror_first), to_sibling(mirror_first)
    (other,) = add_spectra([mirror_first], [(0, 0)], [], 1)
    mirror_last, other = lax.optimization_barrier((mirror_last, other))
    far_last, near_last = to_across(mirror_last), to_sibling(mirror_last)
    (other,) = add_spectra([mirror_last, near_first, far_first], [(0, 1), (1, 0), (2, 0)], [other], 1)
    other, *partial = call_kernel(
        lambda *refs: near_kernel(outs, *refs),
        "near_sums",
        [index, near_last, forward],
        smem,
        [other, *partial],
        [],
        [sums],
        1,
    )
    other, *early = call_kernel(
        lambda *refs: far_kernel(outs, 0, *refs),
        "far_sums",
        [index, far_last, forward],
        smem,
        [other, *partial[:outs]],
        [],
        [sums],
        1,
    )
    late = call_kernel(
        lambda *refs: far_kernel(outs, 1, *refs),
        "far_sums",
        [index, other],
        smem,
        partial[outs:],
        [],
        [sums],
        2 * 10**9,
    )
    values = []
    for half in (early, late):
        if swap:
            kept, sent = half
            received = lax.ppermute(sent, "station", [(i, i ^ 1) for i in range(length)])
        else:
            groups = np.arange(length).reshape(2, length // 2).tolist()
            value = half[0].reshape(rounds // 2, all_pairs // 2, 2 * samples)
            kept = lax.psum_scatter(value, "station", scatter_dimension=1, axis_index_groups=groups, tiled=True)
            kept = kept.reshape(-1, 2 * samples)
            received = jnp.zeros_like(kept)
        values += [kept, received]
    result = finish(values, inverse)
    return result.reshape(rounds, 1, all_pairs // length, 2 * samples)


def solution(mesh):
    return jax.shard_map(
        on_device,
        mesh=mesh,
        in_specs=(
            P(("groups", "cluster"), "station", None, None),
            P(("groups", "cluster"), "station"),
            P("groups"),
            P(None, "groups"),
            P(None, ("groups", "cluster"), None, None),
            P("groups"),
        ),
        out_specs=P(None, ("groups", "cluster"), "station", None),
        check_vma=False,
    )
```

time: 56.3 us -> 49.6 us (0.88); the launches traced: 55.2 us -> 49.2 us
  starting transfers between devices: 17.5 us -> 11.5 us
  Pallas kernels: 16.6 us -> 17.3 us
    ppermute x3 -> x2, starting transfers between devices: 7.42 us -> 3.82 us  [to_mirror(): lax.ppermute(value, 'station', [(i, length - 1 - i) for i in range(length)])]
    ppermute x2, starting transfers between devices: 3.91 us -> 2.16 us  [on_device(): lax.ppermute(sent, 'station', [(i, i ^ 1) for i in range(length)])]
    ppermute x2, waiting for transfers between devices: 11.5 us -> 10.6 us  [on_device(): lax.ppermute(sent, 'station', [(i, i ^ 1) for i in range(length)])]
    pallas_call x6 -> x9, Pallas kernels: 15.2 us -> 15.9 us  [the longest x7 13.2 us: call_kernel(): pl.pallas_call(kernel, out_shape=shapes, in_specs=in_specs, out_specs=out...]
    ppermute x4 -> x3, starting transfers between devices: 4.95 us -> 4.37 us  [to_across(): lax.ppermute(value, 'cluster', [(i, (i + 1 if i % 2 else i - 1) % cluster...]
    ppermute x4 -> x3, waiting for transfers between devices: 4 us -> 4.53 us  [to_across(): lax.ppermute(value, 'cluster', [(i, (i + 1 if i % 2 else i - 1) % cluster...]
    unnamed x24 -> x16, local copies, waits for them, and re-layouts: 5.43 us -> 5.11 us
    ppermute x4 -> x3, starting transfers between devices: 1.17 us -> 1.16 us  [to_sibling(): return lax.ppermute(value, 'cluster', [(i, i ^ 1) for i in range(clusters)])]
  transfers between devices with their start and end apart: 13 -> 10, of which waited for: 4 -> 3; matrix products, arithmetic and copies ran while one was open for 0% -> 0% of each run, Pallas kernels for 20% -> 26%
where the time goes in v4:
time: 49.6 us; the launch traced here: 49.2 us
  Pallas kernels  17.3 us (35%)
  waiting for transfers between devices  15.2 us (31%)
  starting transfers between devices  11.5 us (23%)
  local copies, waits for them, and re-layouts  5.11 us (10%)
    pallas_call x7, Pallas kernels, call_kernel(): pl.pallas_call(kernel, out_shape=shapes, in_specs=in_specs, out_specs=out...  13.2 us
    ppermute x2, waiting for transfers between devices, on_device(): lax.ppermute(sent, 'station', [(i, i ^ 1) for i in range(length)])  10.6 us
    unnamed x16, local copies, waits for them, and re-layouts  5.11 us
    ppermute x3, waiting for transfers between devices, to_across(): lax.ppermute(value, 'cluster', [(i, (i + 1 if i % 2 else i - 1) % cluster...  4.53 us
    ppermute x3, starting transfers between devices, to_across(): lax.ppermute(value, 'cluster', [(i, (i + 1 if i % 2 else i - 1) % cluster...  4.37 us
    ppermute x2, starting transfers between devices, to_mirror(): lax.ppermute(value, 'station', [(i, length - 1 - i) for i in range(length)])  3.82 us
    ppermute x2, starting transfers between devices, on_device(): lax.ppermute(sent, 'station', [(i, i ^ 1) for i in range(length)])  2.16 us
    pallas_call x1, Pallas kernels, prepare(): pl.pallas_call(prepare_kernel, out_shape=[jax.ShapeDtypeStruct((3, events...  2.1 us
  transfers between devices with their start and end apart: 10, of which 3 were waited for; matrix products, arithmetic and copies ran while one was open for 0% of the time, Pallas kernels for 26%

profile of v4, /device:TPU:0, one launch (start us, length us, event | category | flops | bytes accessed | tf_op | source)
XLA Modules:
  0.0 49.2 jit_solution(13568606090326648313)
XLA Ops:
  0.0 2.1 %prepare.1 = (f32[3,16,8,256]{3,2,1,0:T(8,128)}, f32[3,8,8,256]{3,2,1,0:T(8,128)}, f32[3,8,8,256]{3,2,1,0:T(8,128)}) custom-call(f32[16,2,3,4,256]{4,3,2,1,0:T(4,128)} %bitcast.9, s32[4,32]{1,0:T(4,128)} %bitcast.10, f32[16]{0:T(128)} %weight_hbm.1), custom_call_target="tpu_custom_call" | custom-call | tf_op jit(solution)/shard_map/prepare/pallas_call | solution.py:103
  2.1 0.5 %collective-permute-start.3 = (f32[3,16,8,256]{3,2,1,0:T(8,128)}, f32[3,16,8,256]{3,2,1,0:T(8,128)S(1)}, u32[]{:S(2)}, u32[]{:S(2)}) collective-permute-start(f32[3,16,8,256]{3,2,1,0:T(8,128)} %get-tuple-element.36.refs_1_), channel_id=1, source_target_pairs={{0,4},{4,0},{8,12},{12,8},{1,5},{5,1},{9,13},{13,9},{2,6},{6,2},{1... | collective-permute-start | bytes 1179656 | tf_op jit(solution)/shard_map/ppermute | solution.py:330
  2.6 2.6 %collective-permute-start.2 = (f32[3,16,8,256]{3,2,1,0:T(8,128)}, f32[3,16,8,256]{3,2,1,0:T(8,128)S(1)}, u32[]{:S(2)}, u32[]{:S(2)}) collective-permute-start(f32[3,16,8,256]{3,2,1,0:T(8,128)} %get-tuple-element.36.refs_1_), channel_id=1, source_target_pairs={{0,12},{4,8},{8,4},{12,0},{1,13},{5,9},{9,5},{13,1},{2,14},{6,10},... | collective-permute-start | bytes 1179656 | tf_op jit(solution)/shard_map/ppermute | solution.py:333
  5.2 3.6 %collective-permute-start.1 = (f32[3,8,8,256]{3,2,1,0:T(8,128)}, f32[3,8,8,256]{3,2,1,0:T(8,128)S(1)}, u32[]{:S(2)}, u32[]{:S(2)}) collective-permute-start(f32[3,8,8,256]{3,2,1,0:T(8,128)} %get-tuple-element.35), channel_id=1, source_target_pairs={{0,3},{1,2},{2,1},{3,0},{4,7},{5,6},{6,5},{7,4},{8,11},{9,10},{10,... | collective-permute-start | bytes 589832 | tf_op jit(solution)/shard_map/ppermute | solution.py:336
  8.8 0.2 collective-permute-start
  9.1 0.0 copy-start.4
  9.1 0.7 %copy-done.4 = s32[4,1,256,2]{2,3,1,0:T(2,128)S(1)} copy-done((s32[4,1,256,2]{2,3,1,0:T(2,128)S(1)}, s32[4,1,256,2]{2,3,1,0:T(2,128)}, u32[]{:S(2)}) %copy-start.4) | copy-done | bytes 8216
  9.8 0.0 copy-start.5
  9.8 0.7 %copy-done.5 = s32[4,4]{1,0:T(4,128)S(1)} copy-done((s32[4,4]{1,0:T(4,128)S(1)}, s32[4,4]{1,0:T(4,128)}, u32[]{:S(2)}) %copy-start.5) | copy-done | bytes 88
  10.4 0.0 copy-start.6
  10.5 0.7 %copy-done.6 = s32[4]{0:T(128)S(1)} copy-done((s32[4]{0:T(128)S(1)}, s32[4]{0:T(128)}, u32[]{:S(2)}) %copy-start.6) | copy-done | bytes 40
  11.1 0.6 %pair_index.1.refs_0_ = s32[4,3,256]{2,1,0:T(4,128)S(1)} custom-call(s32[4,4]{1,0:T(4,128)S(1)} %copy-done.5, s32[4]{0:T(128)S(1)} %copy-done.6, s32[4,1,2,256]{3,2,1,0:T(2,128)S(1)} %bitcast.8), custom_call_target="tpu_custom_call" | custom-call | tf_op jit(solution)/shard_map/pair_index/pallas_call | solution.py:138
  11.7 0.0 collective-permute-done.3.refs_2_
  11.7 0.0 copy-start
  11.7 1.0 %copy-done = bf16[2,256,512]{2,1,0:T(8,128)(2,1)S(1)} copy-done((bf16[2,256,512]{2,1,0:T(8,128)(2,1)S(1)}, bf16[2,256,512]{2,1,0:T(8,128)(2,1)}, u32[]{:S(2)}) %copy-start) | copy-done | bytes 524312
  12.8 0.0 copy-start.3
  12.8 1.0 %copy-done.3 = f32[3,16,8,256]{3,2,1,0:T(8,128)S(1)} copy-done((f32[3,16,8,256]{3,2,1,0:T(8,128)S(1)}, f32[3,16,8,256]{3,2,1,0:T(8,128)}, u32[]{:S(2)}) %copy-start.3) | copy-done | bytes 393240
  13.8 0.0 copy-start.2
  13.8 4.7 %first_near.1 = (f32[3,17,2,6,8,128]{5,4,3,2,1,0:T(8,128)S(1)}, f32[128,512]{1,0:T(8,128)S(1)}, f32[128,512]{1,0:T(8,128)S(1)}, f32[128,512]{1,0:T(8,128)S(1)}, f32[128,512]{1,0:T(8,128)S(1)}) custom-call(s32[4,3,256]{2,1,0:T(4,128)S(1)} %pair_index.1.refs_0_, f32[3,16,8,256]{3,2,1,0:T(8,128)S(1)} %copy-done.3, ...), custom_call_target="tpu_custom_call" | custom-call | flops 1 | tf_op jit(solution)/shard_map/first_near/pallas_call | solution.py:289
  18.4 0.0 collective-permute-done.2.refs_1_
  18.4 0.0 copy-start.1
  18.5 1.0 %copy-done.1 = bf16[2,256,512]{2,1,0:T(8,128)(2,1)S(1)} copy-done((bf16[2,256,512]{2,1,0:T(8,128)(2,1)S(1)}, bf16[2,256,512]{2,1,0:T(8,128)(2,1)}, u32[]{:S(2)}) %copy-start.1) | copy-done | bytes 524312
  19.5 1.3 %first_far.1 = (f32[3,17,2,6,8,128]{5,4,3,2,1,0:T(8,128)S(1)}, f32[128,512]{1,0:T(8,128)S(1)}, f32[128,512]{1,0:T(8,128)S(1)}, f32[128,512]{1,0:T(8,128)S(1)}, f32[128,512]{1,0:T(8,128)S(1)}) custom-call(s32[4,3,256]{2,1,0:T(4,128)S(1)} %pair_index.1.refs_0_, ...), custom_call_target="tpu_custom_call", output_to_operand_aliasing={{0}: (3, {}), {1}: (4, {}), {2}: (5, {}), {3}: (6, {}), {4}... | custom-call | flops 1 | tf_op jit(solution)/shard_map/first_far/pallas_call | solution.py:289
  20.8 0.0 collective-permute-done.1.refs_0_
  20.8 0.1 collective-permute-start.7
  20.9 0.5 collective-permute-start.6
  21.3 0.0 copy-done.2
  21.3 0.3 add_spectra.2.refs_4_
  21.7 0.0 collective-permute-done.refs_0_
  21.7 0.2 collective-permute-start.5
  21.9 1.7 %collective-permute-start.4 = (f32[3,8,8,256]{3,2,1,0:T(8,128)S(1)}, f32[3,8,8,256]{3,2,1,0:T(8,128)S(1)}, u32[]{:S(2)}, u32[]{:S(2)}) collective-permute-start(f32[3,8,8,256]{3,2,1,0:T(8,128)S(1)} %collective-permute-done.refs_0_), channel_id=1, source_target_pairs={{0,12},{4,8},{8,4},{12,0},{1,13},{5,9},{9,5},{13,1},{2,14},{6,10},... | collective-permute-start | bytes 589832 | tf_op jit(solution)/shard_map/ppermute | solution.py:333
  23.5 4.5 %collective-permute-done.7.refs_2_ = f32[3,8,8,256]{3,2,1,0:T(8,128)S(1)} collective-permute-done((f32[3,8,8,256]{3,2,1,0:T(8,128)S(1)}, f32[3,8,8,256]{3,2,1,0:T(8,128)S(1)}, u32[]{:S(2)}, u32[]{:S(2)}) %collective-permute-start.7) | collective-permute-done | bytes 196640 | tf_op jit(solution)/shard_map/ppermute | solution.py:333
  28.1 0.0 collective-permute-done.6.refs_1_
  28.1 0.6 %add_spectra.3.refs_3_ = f32[3,17,2,6,8,128]{5,4,3,2,1,0:T(8,128)S(1)} custom-call(f32[3,8,8,256]{3,2,1,0:T(8,128)S(1)} %collective-permute-done.refs_0_, f32[3,8,8,256]{3,2,1,0:T(8,128)S(1)} %collective-permute-done.6.refs_1_, f32[3,8,8,256]{3,2,1,0:T(8,128)S(1)} %collective-permute-done.7.refs_2_, ...), custom_call_target="tpu_custom_call", output_to_operand_aliasing={{}: (4, {})} | custom-call | flops 1 | tf_op jit(solution)/shard_map/add_spectra/pallas_call | solution.py:289
  28.7 0.0 collective-permute-done.5.refs_1_
  28.7 4.4 %near_sums.1 = (f32[3,17,2,6,8,128]{5,4,3,2,1,0:T(8,128)S(1)}, f32[128,512]{1,0:T(8,128)S(1)}, f32[128,512]{1,0:T(8,128)S(1)}, f32[128,512]{1,0:T(8,128)S(1)}, f32[128,512]{1,0:T(8,128)S(1)}) custom-call(s32[4,3,256]{2,1,0:T(4,128)S(1)} %pair_index.1.refs_0_, ...), custom_call_target="tpu_custom_call", output_to_operand_aliasing={{0}: (3, {}), {1}: (4, {}), {2}: (5, {}), {3}: (6, {}), {4}... | custom-call | flops 1 | tf_op jit(solution)/shard_map/near_sums/pallas_call | solution.py:289
  33.1 0.0 collective-permute-done.4.refs_1_
  33.1 1.1 %far_sums.2 = (f32[3,17,2,6,8,128]{5,4,3,2,1,0:T(8,128)S(1)}, f32[128,512]{1,0:T(8,128)S(1)}, f32[128,512]{1,0:T(8,128)S(1)}) custom-call(s32[4,3,256]{2,1,0:T(4,128)S(1)} %pair_index.1.refs_0_, f32[3,8,8,256]{3,2,1,0:T(8,128)S(1)} %collective-permute-done.4.refs_1_, ...), custom_call_target="tpu_custom_call", output_to_operand_aliasing={{0}: (3, {}), {1}: (4, {}), {2}: (5, {})} | custom-call | flops 1 | tf_op jit(solution)/shard_map/far_sums/pallas_call | solution.py:289
  34.3 1.5 %collective-permute-start.8 = (f32[128,512]{1,0:T(8,128)S(1)}, f32[128,512]{1,0:T(8,128)S(1)}, u32[]{:S(2)}, u32[]{:S(2)}) collective-permute-start(f32[128,512]{1,0:T(8,128)S(1)} %get-tuple-element.57), channel_id=1, source_target_pairs={{0,1},{1,0},{2,3},{3,2},{4,5},{5,4},{6,7},{7,6},{8,9},{9,8},{10,11... | collective-permute-start | bytes 786440 | tf_op jit(solution)/shard_map/ppermute | solution.py:424
  35.8 0.0 copy-start.7
  35.8 0.8 %far_sums.3 = (f32[128,512]{1,0:T(8,128)S(1)}, f32[128,512]{1,0:T(8,128)S(1)}) custom-call(s32[4,3,256]{2,1,0:T(4,128)S(1)} %pair_index.1.refs_0_, f32[3,17,2,6,8,128]{5,4,3,2,1,0:T(8,128)S(1)} %get-tuple-element.58.refs_1_, f32[128,512]{1,0:T(8,128)S(1)} %get-tuple-element.59.refs_2_, ...), custom_call_target="tpu_custom_call", output_to_operand_aliasing={{0}: (2, {}), {1}: (3, {})} | custom-call | flops 2000000000 | bytes 2000000 | tf_op jit(solution)/shard_map/far_sums/pallas_call | solution.py:289
  36.6 0.7 %collective-permute-start.9 = (f32[128,512]{1,0:T(8,128)S(1)}, f32[128,512]{1,0:T(8,128)S(1)}, u32[]{:S(2)}, u32[]{:S(2)}) collective-permute-start(f32[128,512]{1,0:T(8,128)S(1)} %get-tuple-element.62), channel_id=1, source_target_pairs={{0,1},{1,0},{2,3},{3,2},{4,5},{5,4},{6,7},{7,6},{8,9},{9,8},{10,11... | collective-permute-start | bytes 786440 | tf_op jit(solution)/shard_map/ppermute | solution.py:424
  37.2 6.3 %collective-permute-done.8.early_swapped_ref = f32[128,512]{1,0:T(8,128)S(1)} collective-permute-done((f32[128,512]{1,0:T(8,128)S(1)}, f32[128,512]{1,0:T(8,128)S(1)}, u32[]{:S(2)}, u32[]{:S(2)}) %collective-permute-start.8) | collective-permute-done | bytes 262176 | tf_op jit(solution)/shard_map/ppermute | solution.py:424
  43.5 4.3 %collective-permute-done.9.late_swapped_ref = f32[128,512]{1,0:T(8,128)S(1)} collective-permute-done((f32[128,512]{1,0:T(8,128)S(1)}, f32[128,512]{1,0:T(8,128)S(1)}, u32[]{:S(2)}, u32[]{:S(2)}) %collective-permute-start.9) | collective-permute-done | bytes 262176 | tf_op jit(solution)/shard_map/ppermute | solution.py:424
  47.9 0.0 copy-done.7
  47.9 1.4 %finish.1 = f32[256,512]{1,0:T(8,128)} custom-call(f32[128,512]{1,0:T(8,128)S(1)} %get-tuple-element.56.early_ref, f32[128,512]{1,0:T(8,128)S(1)} %collective-permute-done.8.early_swapped_ref, f32[128,512]{1,0:T(8,128)S(1)} %get-tuple-element.61.late_ref, f32[128,512]{1,0:T(8,128)S(1)} %collective-permute-done.9.late_swapped_ref, ...), custom_call_target="tpu_custom_call" | custom-call | flops 1000000000 | bytes 1000000 | tf_op jit(solution)/shard_map/finish/pallas_call | solution.py:310
Async XLA Ops:
  2.1 9.6 %collective-permute-start.3 = (f32[3,16,8,256]{3,2,1,0:T(8,128)}, f32[3,16,8,256]{3,2,1,0:T(8,128)S(1)}, u32[]{:S(2)}, u32[]{:S(2)}) collective-permute-start(f32[3,16,8,256]{3,2,1,0:T(8,128)} %get-tuple-element.36.refs_1_), channel_id=1, source_target_pairs={{0,4},{4,0},{8,12},{12,8},{1,5},{5,1},{9,13},{13,9},{2,6},{6,2},{1... | collective-permute-start | bytes 1179656 | tf_op jit(solution)/shard_map/ppermute | solution.py:330
  2.6 15.8 %collective-permute-start.2 = (f32[3,16,8,256]{3,2,1,0:T(8,128)}, f32[3,16,8,256]{3,2,1,0:T(8,128)S(1)}, u32[]{:S(2)}, u32[]{:S(2)}) collective-permute-start(f32[3,16,8,256]{3,2,1,0:T(8,128)} %get-tuple-element.36.refs_1_), channel_id=1, source_target_pairs={{0,12},{4,8},{8,4},{12,0},{1,13},{5,9},{9,5},{13,1},{2,14},{6,10},... | collective-permute-start | bytes 1179656 | tf_op jit(solution)/shard_map/ppermute | solution.py:333
  5.2 15.5 %collective-permute-start.1 = (f32[3,8,8,256]{3,2,1,0:T(8,128)}, f32[3,8,8,256]{3,2,1,0:T(8,128)S(1)}, u32[]{:S(2)}, u32[]{:S(2)}) collective-permute-start(f32[3,8,8,256]{3,2,1,0:T(8,128)} %get-tuple-element.35), channel_id=1, source_target_pairs={{0,3},{1,2},{2,1},{3,0},{4,7},{5,6},{6,5},{7,4},{8,11},{9,10},{10,... | collective-permute-start | bytes 589832 | tf_op jit(solution)/shard_map/ppermute | solution.py:336
  8.8 12.8 %collective-permute-start = (f32[3,8,8,256]{3,2,1,0:T(8,128)}, f32[3,8,8,256]{3,2,1,0:T(8,128)S(1)}, u32[]{:S(2)}, u32[]{:S(2)}) collective-permute-start(f32[3,8,8,256]{3,2,1,0:T(8,128)} %get-tuple-element.34), channel_id=1, source_target_pairs={{0,3},{1,2},{2,1},{3,0},{4,7},{5,6},{6,5},{7,4},{8,11},{9,10},{10,... | collective-permute-start | bytes 589832 | tf_op jit(solution)/shard_map/ppermute | solution.py:336
  9.1 0.7 %copy-start.4 = (s32[4,1,256,2]{2,3,1,0:T(2,128)S(1)}, s32[4,1,256,2]{2,3,1,0:T(2,128)}, u32[]{:S(2)}) copy-start(s32[4,1,256,2]{2,3,1,0:T(2,128)} %param.12) | copy-start | bytes 24580
  9.8 0.7 %copy-start.5 = (s32[4,4]{1,0:T(4,128)S(1)}, s32[4,4]{1,0:T(4,128)}, u32[]{:S(2)}) copy-start(s32[4,4]{1,0:T(4,128)} %refs_0_.1) | copy-start | bytes 196
  10.4 0.7 %copy-start.6 = (s32[4]{0:T(128)S(1)}, s32[4]{0:T(128)}, u32[]{:S(2)}) copy-start(s32[4]{0:T(128)} %refs_1_.2) | copy-start | bytes 52
  11.7 1.0 %copy-start = (bf16[2,256,512]{2,1,0:T(8,128)(2,1)S(1)}, bf16[2,256,512]{2,1,0:T(8,128)(2,1)}, u32[]{:S(2)}) copy-start(bf16[2,256,512]{2,1,0:T(8,128)(2,1)} %constant.4.clone.refs_3_.refs_2_.refs_1_) | copy-start | bytes 1572868
  12.8 1.0 %copy-start.3 = (f32[3,16,8,256]{3,2,1,0:T(8,128)S(1)}, f32[3,16,8,256]{3,2,1,0:T(8,128)}, u32[]{:S(2)}) copy-start(f32[3,16,8,256]{3,2,1,0:T(8,128)} %get-tuple-element.36.refs_1_) | copy-start | bytes 1179652
  13.8 7.6 %copy-start.2 = (bf16[2,256,512]{2,1,0:T(8,128)(2,1)S(1)}, bf16[2,256,512]{2,1,0:T(8,128)(2,1)}, u32[]{:S(2)}) copy-start(bf16[2,256,512]{2,1,0:T(8,128)(2,1)} %constant.4.clone.refs_3_.refs_2_.refs_1_) | copy-start | bytes 1572868
  18.4 1.0 %copy-start.1 = (bf16[2,256,512]{2,1,0:T(8,128)(2,1)S(1)}, bf16[2,256,512]{2,1,0:T(8,128)(2,1)}, u32[]{:S(2)}) copy-start(bf16[2,256,512]{2,1,0:T(8,128)(2,1)} %constant.4.clone.refs_3_.refs_2_.refs_1_) | copy-start | bytes 1572868
  20.8 7.3 %collective-permute-start.7 = (f32[3,8,8,256]{3,2,1,0:T(8,128)S(1)}, f32[3,8,8,256]{3,2,1,0:T(8,128)S(1)}, u32[]{:S(2)}, u32[]{:S(2)}) collective-permute-start(f32[3,8,8,256]{3,2,1,0:T(8,128)S(1)} %collective-permute-done.1.refs_0_), channel_id=1, source_target_pairs={{0,12},{4,8},{8,4},{12,0},{1,13},{5,9},{9,5},{13,1},{2,14},{6,10},... | collective-permute-start | bytes 589832 | tf_op jit(solution)/shard_map/ppermute | solution.py:333
  20.9 7.2 %collective-permute-start.6 = (f32[3,8,8,256]{3,2,1,0:T(8,128)S(1)}, f32[3,8,8,256]{3,2,1,0:T(8,128)S(1)}, u32[]{:S(2)}, u32[]{:S(2)}) collective-permute-start(f32[3,8,8,256]{3,2,1,0:T(8,128)S(1)} %collective-permute-done.1.refs_0_), channel_id=1, source_target_pairs={{0,4},{4,0},{8,12},{12,8},{1,5},{5,1},{9,13},{13,9},{2,6},{6,2},{1... | collective-permute-start | bytes 589832 | tf_op jit(solution)/shard_map/ppermute | solution.py:330
  21.7 7.0 %collective-permute-start.5 = (f32[3,8,8,256]{3,2,1,0:T(8,128)S(1)}, f32[3,8,8,256]{3,2,1,0:T(8,128)S(1)}, u32[]{:S(2)}, u32[]{:S(2)}) collective-permute-start(f32[3,8,8,256]{3,2,1,0:T(8,128)S(1)} %collective-permute-done.refs_0_), channel_id=1, source_target_pairs={{0,4},{4,0},{8,12},{12,8},{1,5},{5,1},{9,13},{13,9},{2,6},{6,2},{1... | collective-permute-start | bytes 589832 | tf_op jit(solution)/shard_map/ppermute | solution.py:330
  21.9 11.3 %collective-permute-start.4 = (f32[3,8,8,256]{3,2,1,0:T(8,128)S(1)}, f32[3,8,8,256]{3,2,1,0:T(8,128)S(1)}, u32[]{:S(2)}, u32[]{:S(2)}) collective-permute-start(f32[3,8,8,256]{3,2,1,0:T(8,128)S(1)} %collective-permute-done.refs_0_), channel_id=1, source_target_pairs={{0,12},{4,8},{8,4},{12,0},{1,13},{5,9},{9,5},{13,1},{2,14},{6,10},... | collective-permute-start | bytes 589832 | tf_op jit(solution)/shard_map/ppermute | solution.py:333
  34.3 9.3 %collective-permute-start.8 = (f32[128,512]{1,0:T(8,128)S(1)}, f32[128,512]{1,0:T(8,128)S(1)}, u32[]{:S(2)}, u32[]{:S(2)}) collective-permute-start(f32[128,512]{1,0:T(8,128)S(1)} %get-tuple-element.57), channel_id=1, source_target_pairs={{0,1},{1,0},{2,3},{3,2},{4,5},{5,4},{6,7},{7,6},{8,9},{9,8},{10,11... | collective-permute-start | bytes 786440 | tf_op jit(solution)/shard_map/ppermute | solution.py:424
  35.8 12.1 %copy-start.7 = (bf16[2,512,512]{2,1,0:T(8,128)(2,1)S(1)}, bf16[2,512,512]{2,1,0:T(8,128)(2,1)}, u32[]{:S(2)}) copy-start(bf16[2,512,512]{2,1,0:T(8,128)(2,1)} %constant.5.clone.table_ref) | copy-start | bytes 3145732
  36.6 11.3 %collective-permute-start.9 = (f32[128,512]{1,0:T(8,128)S(1)}, f32[128,512]{1,0:T(8,128)S(1)}, u32[]{:S(2)}, u32[]{:S(2)}) collective-permute-start(f32[128,512]{1,0:T(8,128)S(1)} %get-tuple-element.62), channel_id=1, source_target_pairs={{0,1},{1,0},{2,3},{3,2},{4,5},{5,4},{6,7},{7,6},{8,9},{9,8},{10,11... | collective-permute-start | bytes 786440 | tf_op jit(solution)/shard_map/ppermute | solution.py:424

commit v5 on v4

--- a/solution.py
+++ b/solution.py
@@ -12,7 +12,7 @@
 epsilon = 1e-06
 SUB, LANES = 8, 128
 HALF = SUB // 2
-VMEM_BYTES = 40 * 1024 * 1024
+VMEM_BYTES = 16 * 1024 * 1024
 PREPARE_VMEM_BYTES = 62 * 1024 * 1024
 F32 = jnp.float32
 BF16 = jnp.bfloat16
@@ -116,19 +116,28 @@
     )(waves, event_mask.T, station_weight)
 
 
-def index_kernel(events, partners_ref, counts_ref, pairs_ref, index_ref):
+def index_kernel(events, partners_ref, counts_ref, pairs_ref, index_ref, order_ref):
     rounds, _, _, all_pairs = pairs_ref.shape
     here = lax.axis_index("cluster")
     sibling = jnp.where(here % 2 == 0, here + 1, here - 1)
     own_count = counts_ref[here]
+    partners = [partners_ref[turn, here] for turn in range(rounds)]
+    parts = [jnp.where(partner == here, 0, jnp.where(partner == sibling, 1, 2)) for partner in partners]
+    across = jnp.int32(0)
     for turn in range(rounds):
-        partner = partners_ref[turn, here]
-        part = jnp.where(partner == here, 0, jnp.where(partner == sibling, 1, 2))
+        part = parts[turn]
+        across += (part == 2).astype(jnp.int32)
+        place = jnp.int32(0)
+        for other in range(rounds):
+            ahead = parts[other] <= part if other < turn else parts[other] < part
+            place += ahead.astype(jnp.int32)
+        order_ref[place] = jnp.int32(turn)
         first, second = pairs_ref[turn, 0, 0:1], pairs_ref[turn, 0, 1:2]
-        valid = (first < own_count) & (second < counts_ref[partner])
-        index_ref[turn, 0:1] = jnp.where(valid, first, events)
-        index_ref[turn, 1:2] = second + part * (events + 2)
-        index_ref[turn, 2:3] = jnp.full((1, all_pairs), part, jnp.int32)
+        valid = (first < own_count) & (second < counts_ref[partners[turn]])
+        index_ref[place, 0:1] = jnp.where(valid, first, events)
+        index_ref[place, 1:2] = second + part * (events + 2)
+        index_ref[place, 2:3] = jnp.full((1, all_pairs), part, jnp.int32)
+    order_ref[rounds] = across
 
 
 def pair_index(partners, counts, pair_list, events):
@@ -137,9 +146,12 @@
     smem = pl.BlockSpec(memory_space=pltpu.SMEM)
     return pl.pallas_call(
         lambda *refs: index_kernel(events, *refs),
-        out_shape=jax.ShapeDtypeStruct((rounds, 3, all_pairs), jnp.int32),
+        out_shape=[
+            jax.ShapeDtypeStruct((rounds, 3, all_pairs), jnp.int32),
+            jax.ShapeDtypeStruct((rounds + 1,), jnp.int32),
+        ],
         in_specs=[smem, smem, vmem],
-        out_specs=vmem,
+        out_specs=[vmem, smem],
         compiler_params=pltpu.CompilerParams(vmem_limit_bytes=VMEM_BYTES),
         name="pair_index",
     )(partners, counts, jnp.transpose(pair_list, (0, 1, 3, 2)))
@@ -233,46 +245,58 @@
     return range(half * rounds // 2, (half + 1) * rounds // 2)
 
 
-def first_near_kernel(outs, index_ref, own_ref, sibling_ref, table_ref, spectra_ref, *refs):
-    out_refs, sums_ref = refs[:-1], refs[-1]
+def index_copy(index_hbm, index_ref, sem):
+    copy = pltpu.make_async_copy(index_hbm, index_ref, sem)
+    copy.start()
+    return copy
+
+
+def first_near_kernel(outs, index_hbm, own_ref, sibling_ref, table_ref, spectra_ref, *refs):
+    *out_refs, sums_ref, index_ref, sem = refs
+    copy = index_copy(index_hbm, index_ref, sem)
     fill_spectra(own_ref, 0, 0, table_ref, spectra_ref)
     fill_spectra(sibling_ref, 1, 0, table_ref, spectra_ref)
     clear_last(spectra_ref)
+    copy.wait()
     for half in range(2):
         turns = half_turns(index_ref.shape[0], half)
         some = out_refs[half * outs : (half + 1) * outs]
         add_pairs(index_ref, turns, lambda part: part < 2, spectra_ref, None, some, sums_ref)
 
 
-def first_far_kernel(outs, index_ref, across_ref, table_ref, *refs):
-    spectra_ref, out_refs, sums_ref = refs[2 * outs + 1], refs[2 * outs + 2 : -1], refs[-1]
-    fill_spectra(across_ref, 2, 0, table_ref, spectra_ref)
+def first_far_kernel(outs, index_hbm, first_ref, last_ref, table_ref, *refs):
+    spectra_ref, *out_refs, sums_ref, index_ref, sem = refs[2 * outs + 1 :]
+    copy = index_copy(index_hbm, index_ref, sem)
+    fill_spectra(first_ref, 2, 0, table_ref, spectra_ref)
+    fill_spectra(last_ref, 2, 1, table_ref, spectra_ref)
+    copy.wait()
     for half in range(2):
         turns = half_turns(index_ref.shape[0], half)
         some = out_refs[half * outs : (half + 1) * outs]
         add_pairs(index_ref, turns, lambda part: part == 2, spectra_ref, None, some, sums_ref)
 
 
-def near_kernel(outs, index_ref, sibling_ref, table_ref, *refs):
-    base_refs, refs = refs[1 : 2 * outs + 1], refs[2 * outs + 1 :]
-    spectra_ref, out_refs, sums_ref = refs[0], refs[1:-1], refs[-1]
-    fill_spectra(sibling_ref, 1, 1, table_ref, spectra_ref)
-    for half in range(2):
-        turns = half_turns(index_ref.shape[0], half)
-        some = slice(half * outs, (half + 1) * outs)
-        add_pairs(index_ref, turns, lambda part: part < 2, spectra_ref, base_refs[some], out_refs[some], sums_ref)
-
-
-def far_kernel(outs, half, index_ref, *refs):
-    if half == 0:
-        across_ref, table_ref, _, *refs = refs
-        base_refs, spectra_ref, refs = refs[:outs], refs[outs], refs[outs + 1 :]
-        fill_spectra(across_ref, 2, 1, table_ref, spectra_ref)
-    else:
-        spectra_ref, base_refs, refs = refs[0], refs[1 : outs + 1], refs[outs + 1 :]
-    out_refs, sums_ref = refs[:-1], refs[-1]
+def more_kernel(outs, places, half, parts, has_base, *refs):
+    count = len(places)
+    index_hbm, trace_refs, refs = refs[0], refs[1 : 1 + count], refs[1 + count :]
+    if count:
+        table_ref, refs = refs[0], refs[1:]
+    base_refs, refs = (refs[1 : 1 + outs], refs[1 + outs :]) if has_base else (None, refs[1:])
+    spectra_ref, *out_refs, sums_ref, index_ref, sem = refs
+    copy = index_copy(index_hbm, index_ref, sem)
+    for (traces_part, piece), traces_ref in zip(places, trace_refs, strict=True):
+        fill_spectra(traces_ref, traces_part, piece, table_ref, spectra_ref)
+    if not has_base:
+        for out_ref in out_refs:
+            out_ref[...] = jnp.zeros(out_ref.shape, F32)
+    copy.wait()
     turns = half_turns(index_ref.shape[0], half)
-    add_pairs(index_ref, turns, lambda part: part == 2, spectra_ref, base_refs, out_refs, sums_ref)
+    low, high = parts
+
+    def wanted(part):
+        return (part >= low) & (part <= high)
+
+    add_pairs(index_ref, turns, wanted, spectra_ref, base_refs, out_refs, sums_ref)
 
 
 def call_kernel(kernel, name, operands, specs, updated, out_shapes, scratch, flops):
@@ -299,21 +323,47 @@
     )(*operands)
 
 
-def finish_kernel(early_ref, early_swapped_ref, late_ref, late_swapped_ref, table_ref, out_ref):
-    rows = early_ref.shape[0]
-    out_ref[:rows] = split_dot(early_ref[...] + early_swapped_ref[...], table_ref)
-    out_ref[rows:] = split_dot(late_ref[...] + late_swapped_ref[...], table_ref)
-
-
-def finish(values, table):
-    rows, lags = values[0].shape
+def finish_kernel(half, order_ref, kept_ref, swapped_ref, table_ref, *refs):
+    out_hbm, result_ref, order_smem, sems = refs[-4:]
+    copy = index_copy(order_ref, order_smem, sems.at[0])
+    places = half_turns(order_ref.shape[0] - 1, half)
+    rows = kept_ref.shape[0] // len(places)
+    result_ref[...] = split_dot(kept_ref[...] + swapped_ref[...], table_ref)
+    copy.wait()
+    copies = [
+        pltpu.make_async_copy(
+            result_ref.at[pl.ds(number * rows, rows)],
+            out_hbm.at[pl.ds(pl.multiple_of(order_smem[place] * rows, SUB), rows)],
+            sems.at[number],
+        )
+        for number, place in enumerate(places)
+    ]
+    for copy in copies:
+        copy.start()
+    for copy in copies:
+        copy.wait()
+
+
+def finish(order, kept, swapped, table, half, result):
+    rows, lags = kept.shape
+    vmem = pl.BlockSpec(memory_space=pltpu.VMEM)
+    hbm = pl.BlockSpec(memory_space=pltpu.HBM)
+    operands = [order, kept, swapped, table] + ([] if result is None else [result])
     return pl.pallas_call(
-        finish_kernel,
+        lambda *refs: finish_kernel(half, *refs),
         out_shape=jax.ShapeDtypeStruct((2 * rows, lags), F32),
+        in_specs=[pl.BlockSpec(memory_space=pl.ANY), vmem, vmem, vmem] + [hbm] * (len(operands) - 4),
+        out_specs=hbm,
+        scratch_shapes=[
+            pltpu.VMEM((rows, lags), F32),
+            pltpu.SMEM(order.shape, order.dtype),
+            pltpu.SemaphoreType.DMA((order.shape[0] // 2,)),
+        ],
+        input_output_aliases={} if result is None else {4: 0},
         compiler_params=pltpu.CompilerParams(vmem_limit_bytes=VMEM_BYTES),
-        cost_estimate=pl.CostEstimate(flops=10**9, bytes_accessed=10**6, transcendentals=0),
+        cost_estimate=pl.CostEstimate(flops=1, bytes_accessed=1, transcendentals=0),
         name="finish",
-    )(*values, table)
+    )(*operands)
 
 
 def on_device(waveforms, event_mask, station_weight, partners, pair_list, counts):
@@ -335,13 +385,27 @@
     def to_mirror(value):
         return lax.ppermute(value, "station", [(i, length - 1 - i) for i in range(length)])
 
+    def swap_stations(value):
+        return lax.ppermute(value, "station", [(i, i ^ 1) for i in range(length)])
+
+    def spread(value):
+        groups = np.arange(length).reshape(2, length // 2).tolist()
+        value = value.reshape(rounds // 2, all_pairs // 2, 2 * samples)
+        kept = lax.psum_scatter(value, "station", scatter_dimension=1, axis_index_groups=groups, tiled=True)
+        kept = kept.reshape(-1, 2 * samples)
+        return kept, jnp.zeros_like(kept)
+
     swap = length == 4
     outs = 2 if swap else 1
     half_shape = jax.ShapeDtypeStruct((rounds * all_pairs // 4 // outs, 2 * samples), F32)
     spectra_shape = jax.ShapeDtypeStruct((3, events // 2 + 1, 2, 6, SUB, LANES), F32)
-    sums = pltpu.VMEM((2, all_pairs // length * SUB, LANES), F32)
-
-    smem = {0: pl.BlockSpec(memory_space=pltpu.SMEM)}
+    scratch = [
+        pltpu.VMEM((2, all_pairs // length * SUB, LANES), F32),
+        pltpu.SMEM((rounds, 3, all_pairs), jnp.int32),
+        pltpu.SemaphoreType.DMA,
+    ]
+
+    anywhere = {0: pl.BlockSpec(memory_space=pl.ANY)}
 
     def add_spectra(traces, places, spectra, flops):
         return call_kernel(
@@ -355,81 +419,70 @@
             flops,
         )
 
+    def more_sums(name, traces, places, half, parts, spectra, base):
+        return call_kernel(
+            lambda *refs: more_kernel(outs, places, half, parts, bool(base), *refs),
+            name,
+            [index, *traces, forward] if traces else [index],
+            anywhere,
+            [spectra, *base],
+            [] if base else [half_shape] * outs,
+            scratch,
+            1,
+        )
+
     own, first_piece, last_piece = prepare(waveforms, event_mask, station_weight)
-    index = pair_index(partners, counts, pair_list, events)
-    mirror_first = to_mirror(first_piece)
-    mirror_last = to_mirror(last_piece)
-    across = to_across(own)
+    index, order = pair_index(partners, counts, pair_list, events)
+    mirror_first, mirror_last = to_mirror(first_piece), to_mirror(last_piece)
+    across = [to_across(first_piece), to_across(last_piece)]
     sibling = to_sibling(own)
     spectra, *partial = call_kernel(
         lambda *refs: first_near_kernel(outs, *refs),
         "first_near",
         [index, own, sibling, forward],
-        smem,
+        anywhere,
         [],
         [spectra_shape] + [half_shape] * (2 * outs),
-        [sums],
-        1,
-    )
-    _, *partial = call_kernel(
-        lambda *refs: first_far_kernel(outs, *refs),
-        "first_far",
-        [index, across, forward],
-        smem,
-        [spectra, *partial],
-        [],
-        [sums],
+        scratch,
         1,
     )
     mirror_first, *partial = lax.optimization_barrier((mirror_first, *partial))
     far_first, near_first = to_across(mirror_first), to_sibling(mirror_first)
     (other,) = add_spectra([mirror_first], [(0, 0)], [], 1)
-    mirror_last, other = lax.optimization_barrier((mirror_last, other))
-    far_last, near_last = to_across(mirror_last), to_sibling(mirror_last)
-    (other,) = add_spectra([mirror_last, near_first, far_first], [(0, 1), (1, 0), (2, 0)], [other], 1)
-    other, *partial = call_kernel(
-        lambda *refs: near_kernel(outs, *refs),
-        "near_sums",
-        [index, near_last, forward],
-        smem,
-        [other, *partial],
+    other, *partial = lax.optimization_barrier((other, *partial))
+    _, *partial = call_kernel(
+        lambda *refs: first_far_kernel(outs, *refs),
+        "first_far",
+        [index, *across, forward],
+        anywhere,
+        [spectra, *partial],
         [],
-        [sums],
+        scratch,
         1,
     )
-    other, *early = call_kernel(
-        lambda *refs: far_kernel(outs, 0, *refs),
-        "far_sums",
-        [index, far_last, forward],
-        smem,
-        [other, *partial[:outs]],
-        [],
-        [sums],
-        1,
-    )
-    late = call_kernel(
-        lambda *refs: far_kernel(outs, 1, *refs),
-        "far_sums",
-        [index, other],
-        smem,
-        partial[outs:],
-        [],
-        [sums],
-        2 * 10**9,
-    )
-    values = []
-    for half in (early, late):
-        if swap:
-            kept, sent = half
-            received = lax.ppermute(sent, "station", [(i, i ^ 1) for i in range(length)])
-        else:
-            groups = np.arange(length).reshape(2, length // 2).tolist()
-            value = half[0].reshape(rounds // 2, all_pairs // 2, 2 * samples)
-            kept = lax.psum_scatter(value, "station", scatter_dimension=1, axis_index_groups=groups, tiled=True)
-            kept = kept.reshape(-1, 2 * samples)
-            received = jnp.zeros_like(kept)
-        values += [kept, received]
-    result = finish(values, inverse)
+    mirror_last, other, *partial = lax.optimization_barrier((mirror_last, other, *partial))
+    far_last, near_last = to_across(mirror_last), to_sibling(mirror_last)
+    early, late = partial[:outs], partial[outs:]
+    other, *early = more_sums("own_sums", [mirror_last], [(0, 1)], 0, (0, 0), other, early)
+    (other,) = add_spectra([near_first, far_first], [(1, 0), (2, 0)], [other], 1)
+    other, *early = more_sums("sibling_sums", [near_last], [(1, 1)], 0, (1, 1), other, early)
+    if swap:
+        early.append(swap_stations(early.pop()))
+    other, *late = more_sums("near_sums", [], [], 1, (0, 1), other, late)
+    other, *late = more_sums("across_sums", [far_last], [(2, 1)], 1, (2, 2), other, late)
+    if swap:
+        late.append(swap_stations(late.pop()))
+
+        def with_across(spectra, kept):
+            _, more_kept, more_sent = more_sums("across_sums", [], [], 0, (2, 2), spectra, [])
+            return kept + more_kept + swap_stations(more_sent)
+
+        early[0] = lax.cond(order[rounds] > rounds // 2, with_across, lambda _, kept: kept, other, early[0])
+    else:
+        _, *early = more_sums("across_sums", [], [], 0, (2, 2), other, early)
+        early, late = spread(early[0]), spread(late[0])
+    result = finish(order, *early, inverse, 0, None)
+    result = finish(order, *late, inverse, 1, result)
     return result.reshape(rounds, 1, all_pairs // length, 2 * samples)
 
 

time: 49.6 us -> 44.8 us (0.903)
  waiting for transfers between devices: 15.2 us -> 8.01 us
  starting transfers between devices: 11.5 us -> 13.2 us
  Pallas kernels: 17.3 us -> 18 us
  between operations: 0.15 us -> 0.84 us
    ppermute x2, waiting for transfers between devices: 10.6 us -> 6.25 us  [swap_stations(): return lax.ppermute(value, 'station', [(i, i ^ 1) for i in range(length)])]
    ppermute x3 -> x4, waiting for transfers between devices: 4.53 us -> 1.75 us  [to_across(): lax.ppermute(value, 'cluster', [(i, (i + 1 if i % 2 else i - 1) % cluster...]
    pallas_call x2 -> x3, Pallas kernels: 1.96 us -> 3.74 us  [the longest x2 2.54 us: finish(): pl.pallas_call(lambda *refs: finish_kernel(half, *refs), out_shape=jax.Sh...]
    ppermute x2, starting transfers between devices: 2.16 us -> 3.36 us  [swap_stations(): return lax.ppermute(value, 'station', [(i, i ^ 1) for i in range(length)])]
    pallas_call x7 -> x8, Pallas kernels: 13.2 us -> 12.2 us  [call_kernel(): pl.pallas_call(kernel, out_shape=shapes, in_specs=in_specs, out_specs=out...]
    unnamed x16 -> x14, local copies, waits for them, and re-layouts: 5.11 us -> 4.08 us
    ppermute x2, starting transfers between devices: 3.82 us -> 4.77 us  [to_mirror(): lax.ppermute(value, 'station', [(i, length - 1 - i) for i in range(length)])]
    ppermute x3 -> x4, starting transfers between devices: 4.37 us -> 3.56 us  [to_across(): lax.ppermute(value, 'cluster', [(i, (i + 1 if i % 2 else i - 1) % cluster...]
  transfers between devices with their start and end apart: 10 -> 11, of which waited for: 3 -> 3; matrix products, arithmetic and copies ran while one was open for 0% -> 1% of each run, Pallas kernels for 26% -> 33%
where the time goes in v5:
time: 44.8 us; the launch traced here: 44.7 us
  Pallas kernels  18 us (40%)
  starting transfers between devices  13.2 us (29%)
  waiting for transfers between devices  8.01 us (18%)
  local copies, waits for them, and re-layouts  4.66 us (10%)
  between operations  0.84 us (2%)
    pallas_call x8, Pallas kernels, call_kernel(): pl.pallas_call(kernel, out_shape=shapes, in_specs=in_specs, out_specs=out...  12.2 us
    ppermute x2, waiting for transfers between devices, swap_stations(): return lax.ppermute(value, 'station', [(i, i ^ 1) for i in range(length)])  6.25 us
    ppermute x2, starting transfers between devices, to_mirror(): lax.ppermute(value, 'station', [(i, length - 1 - i) for i in range(length)])  4.77 us
    unnamed x14, local copies, waits for them, and re-layouts  4.08 us
    ppermute x4, starting transfers between devices, to_across(): lax.ppermute(value, 'cluster', [(i, (i + 1 if i % 2 else i - 1) % cluster...  3.56 us
    ppermute x2, starting transfers between devices, swap_stations(): return lax.ppermute(value, 'station', [(i, i ^ 1) for i in range(length)])  3.36 us
    pallas_call x2, Pallas kernels, finish(): pl.pallas_call(lambda *refs: finish_kernel(half, *refs), out_shape=jax.Sh...  2.54 us
    pallas_call x1, Pallas kernels, prepare(): pl.pallas_call(prepare_kernel, out_shape=[jax.ShapeDtypeStruct((3, events...  2.1 us
  transfers between devices with their start and end apart: 11, of which 3 were waited for; matrix products, arithmetic and copies ran while one was open for 1% of the time, Pallas kernels for 33%

profile of v5, /device:TPU:0, one launch (start us, length us, event | category | flops | bytes accessed | tf_op | source)
XLA Modules:
  0.0 44.7 jit_solution(17091482917163662156)
XLA Ops:
  0.0 2.1 %prepare.1 = (f32[3,16,8,256]{3,2,1,0:T(8,128)}, f32[3,8,8,256]{3,2,1,0:T(8,128)}, f32[3,8,8,256]{3,2,1,0:T(8,128)}) custom-call(f32[16,2,3,4,256]{4,3,2,1,0:T(4,128)} %bitcast.10, s32[4,32]{1,0:T(4,128)} %bitcast.11, f32[16]{0:T(128)} %weight_hbm.1), custom_call_target="tpu_custom_call" | custom-call | tf_op jit(solution)/shard_map/prepare/pallas_call | solution.py:103
  2.1 0.5 %collective-permute-start.3 = (f32[3,16,8,256]{3,2,1,0:T(8,128)}, f32[3,16,8,256]{3,2,1,0:T(8,128)S(1)}, u32[]{:S(2)}, u32[]{:S(2)}) collective-permute-start(f32[3,16,8,256]{3,2,1,0:T(8,128)} %get-tuple-element.66.refs_1_), channel_id=1, source_target_pairs={{0,4},{4,0},{8,12},{12,8},{1,5},{5,1},{9,13},{13,9},{2,6},{6,2},{1... | collective-permute-start | bytes 1179656 | tf_op jit(solution)/shard_map/ppermute | solution.py:380
  2.6 4.7 %collective-permute-start.2 = (f32[3,8,8,256]{3,2,1,0:T(8,128)}, f32[3,8,8,256]{3,2,1,0:T(8,128)S(1)}, u32[]{:S(2)}, u32[]{:S(2)}) collective-permute-start(f32[3,8,8,256]{3,2,1,0:T(8,128)} %get-tuple-element.65), channel_id=1, source_target_pairs={{0,3},{1,2},{2,1},{3,0},{4,7},{5,6},{6,5},{7,4},{8,11},{9,10},{10,... | collective-permute-start | bytes 589832 | tf_op jit(solution)/shard_map/ppermute | solution.py:386
  7.3 1.3 %collective-permute-start.4 = (f32[3,8,8,256]{3,2,1,0:T(8,128)}, f32[3,8,8,256]{3,2,1,0:T(8,128)S(1)}, u32[]{:S(2)}, u32[]{:S(2)}) collective-permute-start(f32[3,8,8,256]{3,2,1,0:T(8,128)} %get-tuple-element.65), channel_id=1, source_target_pairs={{0,12},{4,8},{8,4},{12,0},{1,13},{5,9},{9,5},{13,1},{2,14},{6,10},... | collective-permute-start | bytes 589832 | tf_op jit(solution)/shard_map/ppermute | solution.py:383
  8.6 0.5 %collective-permute-start.5 = (f32[3,8,8,256]{3,2,1,0:T(8,128)}, f32[3,8,8,256]{3,2,1,0:T(8,128)S(1)}, u32[]{:S(2)}, u32[]{:S(2)}) collective-permute-start(f32[3,8,8,256]{3,2,1,0:T(8,128)} %get-tuple-element.64), channel_id=1, source_target_pairs={{0,12},{4,8},{8,4},{12,0},{1,13},{5,9},{9,5},{13,1},{2,14},{6,10},... | collective-permute-start | bytes 589832 | tf_op jit(solution)/shard_map/ppermute | solution.py:383
  9.1 0.1 collective-permute-start.1
  9.1 0.0 copy-start.4
  9.1 0.7 %copy-done.4 = s32[4,1,256,2]{2,3,1,0:T(2,128)S(1)} copy-done((s32[4,1,256,2]{2,3,1,0:T(2,128)S(1)}, s32[4,1,256,2]{2,3,1,0:T(2,128)}, u32[]{:S(2)}) %copy-start.4) | copy-done | bytes 8216
  9.8 0.0 copy-start.5
  9.8 0.7 %copy-done.5 = s32[4,4]{1,0:T(4,128)S(1)} copy-done((s32[4,4]{1,0:T(4,128)S(1)}, s32[4,4]{1,0:T(4,128)}, u32[]{:S(2)}) %copy-start.5) | copy-done | bytes 88
  10.5 0.0 copy-start.6
  10.5 0.7 %copy-done.6 = s32[4]{0:T(128)S(1)} copy-done((s32[4]{0:T(128)S(1)}, s32[4]{0:T(128)}, u32[]{:S(2)}) %copy-start.6) | copy-done | bytes 40
  11.2 1.2 %pair_index.1 = (s32[4,3,256]{2,1,0:T(4,128)S(1)}, s32[5]{0:T(128)S(1)}) custom-call(s32[4,4]{1,0:T(4,128)S(1)} %copy-done.5, s32[4]{0:T(128)S(1)} %copy-done.6, s32[4,1,2,256]{3,2,1,0:T(2,128)S(1)} %bitcast.9), custom_call_target="tpu_custom_call" | custom-call | tf_op jit(solution)/shard_map/pair_index/pallas_call | solution.py:147
  12.4 0.0 collective-permute-done.3.refs_2_
  12.4 0.0 copy-start
  12.4 1.0 %copy-done = bf16[2,256,512]{2,1,0:T(8,128)(2,1)S(1)} copy-done((bf16[2,256,512]{2,1,0:T(8,128)(2,1)S(1)}, bf16[2,256,512]{2,1,0:T(8,128)(2,1)}, u32[]{:S(2)}) %copy-start) | copy-done | bytes 524312
  13.4 0.0 copy-start.3
  13.5 1.0 %copy-done.3 = f32[3,16,8,256]{3,2,1,0:T(8,128)S(1)} copy-done((f32[3,16,8,256]{3,2,1,0:T(8,128)S(1)}, f32[3,16,8,256]{3,2,1,0:T(8,128)}, u32[]{:S(2)}) %copy-start.3) | copy-done | bytes 393240
  14.4 3.1 %first_near.1 = (f32[3,17,2,6,8,128]{5,4,3,2,1,0:T(8,128)S(1)}, f32[128,512]{1,0:T(8,128)S(1)}, f32[128,512]{1,0:T(8,128)S(1)}, f32[128,512]{1,0:T(8,128)S(1)}, f32[128,512]{1,0:T(8,128)S(1)}) custom-call(s32[4,3,256]{2,1,0:T(4,128)S(1)} %get-tuple-element.63.refs_0_, f32[3,16,8,256]{3,2,1,0:T(8,128)S(1)} %copy-done.3, ...), custom_call_target="tpu_custom_call" | custom-call | flops 1 | tf_op jit(solution)/shard_map/first_near/pallas_call | solution.py:313
  17.6 0.0 collective-permute-done.2.refs_0_
  17.6 0.3 add_spectra.2.refs_3_
  17.9 0.9 %collective-permute-start.8 = (f32[3,8,8,256]{3,2,1,0:T(8,128)S(1)}, f32[3,8,8,256]{3,2,1,0:T(8,128)S(1)}, u32[]{:S(2)}, u32[]{:S(2)}) collective-permute-start(f32[3,8,8,256]{3,2,1,0:T(8,128)S(1)} %collective-permute-done.2.refs_0_), channel_id=1, source_target_pairs={{0,4},{4,0},{8,12},{12,8},{1,5},{5,1},{9,13},{13,9},{2,6},{6,2},{1... | collective-permute-start | bytes 589832 | tf_op jit(solution)/shard_map/ppermute | solution.py:380
  18.9 1.7 %collective-permute-start.9 = (f32[3,8,8,256]{3,2,1,0:T(8,128)S(1)}, f32[3,8,8,256]{3,2,1,0:T(8,128)S(1)}, u32[]{:S(2)}, u32[]{:S(2)}) collective-permute-start(f32[3,8,8,256]{3,2,1,0:T(8,128)S(1)} %collective-permute-done.2.refs_0_), channel_id=1, source_target_pairs={{0,12},{4,8},{8,4},{12,0},{1,13},{5,9},{9,5},{13,1},{2,14},{6,10},... | collective-permute-start | bytes 589832 | tf_op jit(solution)/shard_map/ppermute | solution.py:383
  20.5 0.0 collective-permute-done.4.refs_1_
  20.5 0.0 collective-permute-done.5.refs_2_
  20.5 0.0 copy-done.1
  20.5 1.6 %first_far.1 = (f32[3,17,2,6,8,128]{5,4,3,2,1,0:T(8,128)S(1)}, f32[128,512]{1,0:T(8,128)S(1)}, f32[128,512]{1,0:T(8,128)S(1)}, f32[128,512]{1,0:T(8,128)S(1)}, f32[128,512]{1,0:T(8,128)S(1)}) custom-call(s32[4,3,256]{2,1,0:T(4,128)S(1)} %get-tuple-element.63.refs_0_, ...), custom_call_target="tpu_custom_call", output_to_operand_aliasing={{0}: (4, {}), {1}: (5, {}), {2}: (6, {}), {3}: (7, {}), {4}... | custom-call | flops 1 | tf_op jit(solution)/shard_map/first_far/pallas_call | solution.py:313
  22.2 0.0 collective-permute-done.1.refs_1_
  22.2 0.1 collective-permute-start.7
  22.3 0.1 collective-permute-start.6
  22.4 1.6 %own_sums.1 = (f32[3,17,2,6,8,128]{5,4,3,2,1,0:T(8,128)S(1)}, f32[128,512]{1,0:T(8,128)S(1)}, f32[128,512]{1,0:T(8,128)S(1)}) custom-call(s32[4,3,256]{2,1,0:T(4,128)S(1)} %get-tuple-element.63.refs_0_, f32[3,8,8,256]{3,2,1,0:T(8,128)S(1)} %collective-permute-done.1.refs_1_, ...), custom_call_target="tpu_custom_call", output_to_operand_aliasing={{0}: (3, {}), {1}: (4, {}), {2}: (5, {})} | custom-call | flops 1 | tf_op jit(solution)/shard_map/own_sums/pallas_call | solution.py:313
  24.0 0.0 collective-permute-done.8.refs_0_
  24.1 1.7 %collective-permute-done.9.refs_1_ = f32[3,8,8,256]{3,2,1,0:T(8,128)S(1)} collective-permute-done((f32[3,8,8,256]{3,2,1,0:T(8,128)S(1)}, f32[3,8,8,256]{3,2,1,0:T(8,128)S(1)}, u32[]{:S(2)}, u32[]{:S(2)}) %collective-permute-start.9) | collective-permute-done | bytes 196640 | tf_op jit(solution)/shard_map/ppermute | solution.py:383
  25.8 0.5 %add_spectra.3.refs_3_ = f32[3,17,2,6,8,128]{5,4,3,2,1,0:T(8,128)S(1)} custom-call(f32[3,8,8,256]{3,2,1,0:T(8,128)S(1)} %collective-permute-done.8.refs_0_, f32[3,8,8,256]{3,2,1,0:T(8,128)S(1)} %collective-permute-done.9.refs_1_, bf16[2,256,512]{2,1,0:T(8,128)(2,1)S(1)} %copy-done.1, ...), custom_call_target="tpu_custom_call", output_to_operand_aliasing={{}: (3, {})} | custom-call | flops 1 | tf_op jit(solution)/shard_map/add_spectra/pallas_call | solution.py:313
  26.3 0.0 collective-permute-done.7.refs_1_
  26.3 1.7 %sibling_sums.1 = (f32[3,17,2,6,8,128]{5,4,3,2,1,0:T(8,128)S(1)}, f32[128,512]{1,0:T(8,128)S(1)}, f32[128,512]{1,0:T(8,128)S(1)}) custom-call(s32[4,3,256]{2,1,0:T(4,128)S(1)} %get-tuple-element.63.refs_0_, f32[3,8,8,256]{3,2,1,0:T(8,128)S(1)} %collective-permute-done.7.refs_1_, ...), custom_call_target="tpu_custom_call", output_to_operand_aliasing={{0}: (3, {}), {1}: (4, {}), {2}: (5, {})} | custom-call | flops 1 | tf_op jit(solution)/shard_map/sibling_sums/pallas_call | solution.py:313
  28.0 3.1 %collective-permute-start.11 = (f32[128,512]{1,0:T(8,128)S(1)}, f32[128,512]{1,0:T(8,128)S(1)}, u32[]{:S(2)}, u32[]{:S(2)}) collective-permute-start(f32[128,512]{1,0:T(8,128)S(1)} %get-tuple-element.103), channel_id=1, source_target_pairs={{0,1},{1,0},{2,3},{3,2},{4,5},{5,4},{6,7},{7,6},{8,9},{9,8},{10,11... | collective-permute-start | bytes 786440 | tf_op jit(solution)/shard_map/ppermute | solution.py:389
  31.1 1.7 %near_sums.1 = (f32[3,17,2,6,8,128]{5,4,3,2,1,0:T(8,128)S(1)}, f32[128,512]{1,0:T(8,128)S(1)}, f32[128,512]{1,0:T(8,128)S(1)}) custom-call(s32[4,3,256]{2,1,0:T(4,128)S(1)} %get-tuple-element.63.refs_0_, f32[3,17,2,6,8,128]{5,4,3,2,1,0:T(8,128)S(1)} %get-tuple-element.93.refs_1_, ...), custom_call_target="tpu_custom_call", output_to_operand_aliasing={{0}: (1, {}), {1}: (2, {}), {2}: (3, {})} | custom-call | flops 1 | tf_op jit(solution)/shard_map/near_sums/pallas_call | solution.py:313
  32.7 0.0 collective-permute-done.6.refs_1_
  32.8 1.7 %across_sums.3 = (f32[3,17,2,6,8,128]{5,4,3,2,1,0:T(8,128)S(1)}, f32[128,512]{1,0:T(8,128)S(1)}, f32[128,512]{1,0:T(8,128)S(1)}) custom-call(s32[4,3,256]{2,1,0:T(4,128)S(1)} %get-tuple-element.63.refs_0_, f32[3,8,8,256]{3,2,1,0:T(8,128)S(1)} %collective-permute-done.6.refs_1_, ...), custom_call_target="tpu_custom_call", output_to_operand_aliasing={{0}: (3, {}), {1}: (4, {}), {2}: (5, {})} | custom-call | flops 1 | tf_op jit(solution)/shard_map/across_sums/pallas_call | solution.py:313
  34.4 0.0 copy-start.2
  34.5 0.2 collective-permute-start.10
  34.7 0.6 %slice.3 = s32[1]{0:T(128)} slice(s32[5]{0:T(128)S(1)} %get-tuple-element.62.refs_0_), slice={[4:5]} | slice | bytes 8 | tf_op jit(solution)/shard_map/slice | solution.py:480
  35.9 2.2 %collective-permute-done.11.refs_2_ = f32[128,512]{1,0:T(8,128)S(1)} collective-permute-done((f32[128,512]{1,0:T(8,128)S(1)}, f32[128,512]{1,0:T(8,128)S(1)}, u32[]{:S(2)}, u32[]{:S(2)}) %collective-permute-start.11) | collective-permute-done | bytes 262176 | tf_op jit(solution)/shard_map/ppermute | solution.py:389
  38.2 0.0 copy-done.2
  38.2 1.3 %finish.2.refs_4_ = f32[256,512]{1,0:T(8,128)} custom-call(s32[5]{0:T(128)S(1)} %get-tuple-element.62.refs_0_, f32[128,512]{1,0:T(8,128)S(1)} %get-tuple-element.104.refs_1_, f32[128,512]{1,0:T(8,128)S(1)} %collective-permute-done.11.refs_2_, bf16[2,512,512]{2,1,0:T(8,128)(2,1)S(1)} %copy-done.2), custom_call_target="tpu_custom_call" | custom-call | flops 1 | bytes 1 | tf_op jit(solution)/shard_map/finish/pallas_call | solution.py:352
  39.5 4.0 %collective-permute-done.10.refs_2_ = f32[128,512]{1,0:T(8,128)S(1)} collective-permute-done((f32[128,512]{1,0:T(8,128)S(1)}, f32[128,512]{1,0:T(8,128)S(1)}, u32[]{:S(2)}, u32[]{:S(2)}) %collective-permute-start.10) | collective-permute-done | bytes 262176 | tf_op jit(solution)/shard_map/ppermute | solution.py:389
  43.5 1.3 %finish.3 = f32[256,512]{1,0:T(8,128)} custom-call(s32[5]{0:T(128)S(1)} %get-tuple-element.62.refs_0_, f32[128,512]{1,0:T(8,128)S(1)} %get-tuple-element.99.refs_1_, f32[128,512]{1,0:T(8,128)S(1)} %collective-permute-done.10.refs_2_, bf16[2,512,512]{2,1,0:T(8,128)(2,1)S(1)} %copy-done.2, f32[256,512]{1,0:T(8,128)} %finish.2.refs_4_), custom_call_target="tpu_custom_call", output_to_operand_aliasing={{}: (4, {})} | custom-call | flops 1 | bytes 1 | tf_op jit(solution)/shard_map/finish/pallas_call | solution.py:352
  (2 shorter events, 0.0 us)
Async XLA Ops:
  2.1 10.3 %collective-permute-start.3 = (f32[3,16,8,256]{3,2,1,0:T(8,128)}, f32[3,16,8,256]{3,2,1,0:T(8,128)S(1)}, u32[]{:S(2)}, u32[]{:S(2)}) collective-permute-start(f32[3,16,8,256]{3,2,1,0:T(8,128)} %get-tuple-element.66.refs_1_), channel_id=1, source_target_pairs={{0,4},{4,0},{8,12},{12,8},{1,5},{5,1},{9,13},{13,9},{2,6},{6,2},{1... | collective-permute-start | bytes 1179656 | tf_op jit(solution)/shard_map/ppermute | solution.py:380
  2.6 15.0 %collective-permute-start.2 = (f32[3,8,8,256]{3,2,1,0:T(8,128)}, f32[3,8,8,256]{3,2,1,0:T(8,128)S(1)}, u32[]{:S(2)}, u32[]{:S(2)}) collective-permute-start(f32[3,8,8,256]{3,2,1,0:T(8,128)} %get-tuple-element.65), channel_id=1, source_target_pairs={{0,3},{1,2},{2,1},{3,0},{4,7},{5,6},{6,5},{7,4},{8,11},{9,10},{10,... | collective-permute-start | bytes 589832 | tf_op jit(solution)/shard_map/ppermute | solution.py:386
  7.3 13.2 %collective-permute-start.4 = (f32[3,8,8,256]{3,2,1,0:T(8,128)}, f32[3,8,8,256]{3,2,1,0:T(8,128)S(1)}, u32[]{:S(2)}, u32[]{:S(2)}) collective-permute-start(f32[3,8,8,256]{3,2,1,0:T(8,128)} %get-tuple-element.65), channel_id=1, source_target_pairs={{0,12},{4,8},{8,4},{12,0},{1,13},{5,9},{9,5},{13,1},{2,14},{6,10},... | collective-permute-start | bytes 589832 | tf_op jit(solution)/shard_map/ppermute | solution.py:383
  8.6 12.0 %collective-permute-start.5 = (f32[3,8,8,256]{3,2,1,0:T(8,128)}, f32[3,8,8,256]{3,2,1,0:T(8,128)S(1)}, u32[]{:S(2)}, u32[]{:S(2)}) collective-permute-start(f32[3,8,8,256]{3,2,1,0:T(8,128)} %get-tuple-element.64), channel_id=1, source_target_pairs={{0,12},{4,8},{8,4},{12,0},{1,13},{5,9},{9,5},{13,1},{2,14},{6,10},... | collective-permute-start | bytes 589832 | tf_op jit(solution)/shard_map/ppermute | solution.py:383
  9.1 13.1 %collective-permute-start.1 = (f32[3,8,8,256]{3,2,1,0:T(8,128)}, f32[3,8,8,256]{3,2,1,0:T(8,128)S(1)}, u32[]{:S(2)}, u32[]{:S(2)}) collective-permute-start(f32[3,8,8,256]{3,2,1,0:T(8,128)} %get-tuple-element.64), channel_id=1, source_target_pairs={{0,3},{1,2},{2,1},{3,0},{4,7},{5,6},{6,5},{7,4},{8,11},{9,10},{10,... | collective-permute-start | bytes 589832 | tf_op jit(solution)/shard_map/ppermute | solution.py:386
  9.1 0.7 %copy-start.4 = (s32[4,1,256,2]{2,3,1,0:T(2,128)S(1)}, s32[4,1,256,2]{2,3,1,0:T(2,128)}, u32[]{:S(2)}) copy-start(s32[4,1,256,2]{2,3,1,0:T(2,128)} %param.14) | copy-start | bytes 24580
  9.8 0.7 %copy-start.5 = (s32[4,4]{1,0:T(4,128)S(1)}, s32[4,4]{1,0:T(4,128)}, u32[]{:S(2)}) copy-start(s32[4,4]{1,0:T(4,128)} %refs_0_.1) | copy-start | bytes 196
  10.5 0.7 %copy-start.6 = (s32[4]{0:T(128)S(1)}, s32[4]{0:T(128)}, u32[]{:S(2)}) copy-start(s32[4]{0:T(128)} %refs_1_.2) | copy-start | bytes 52
  12.4 1.0 %copy-start = (bf16[2,256,512]{2,1,0:T(8,128)(2,1)S(1)}, bf16[2,256,512]{2,1,0:T(8,128)(2,1)}, u32[]{:S(2)}) copy-start(bf16[2,256,512]{2,1,0:T(8,128)(2,1)} %constant.7.clone.refs_3_.refs_1_.refs_2_) | copy-start | bytes 1572868
  13.4 1.0 %copy-start.3 = (f32[3,16,8,256]{3,2,1,0:T(8,128)S(1)}, f32[3,16,8,256]{3,2,1,0:T(8,128)}, u32[]{:S(2)}) copy-start(f32[3,16,8,256]{3,2,1,0:T(8,128)} %get-tuple-element.66.refs_1_) | copy-start | bytes 1179652
  14.4 6.1 %copy-start.1 = (bf16[2,256,512]{2,1,0:T(8,128)(2,1)S(1)}, bf16[2,256,512]{2,1,0:T(8,128)(2,1)}, u32[]{:S(2)}) copy-start(bf16[2,256,512]{2,1,0:T(8,128)(2,1)} %constant.7.clone.refs_3_.refs_1_.refs_2_) | copy-start | bytes 1572868
  17.9 6.1 %collective-permute-start.8 = (f32[3,8,8,256]{3,2,1,0:T(8,128)S(1)}, f32[3,8,8,256]{3,2,1,0:T(8,128)S(1)}, u32[]{:S(2)}, u32[]{:S(2)}) collective-permute-start(f32[3,8,8,256]{3,2,1,0:T(8,128)S(1)} %collective-permute-done.2.refs_0_), channel_id=1, source_target_pairs={{0,4},{4,0},{8,12},{12,8},{1,5},{5,1},{9,13},{13,9},{2,6},{6,2},{1... | collective-permute-start | bytes 589832 | tf_op jit(solution)/shard_map/ppermute | solution.py:380
  18.9 6.9 %collective-permute-start.9 = (f32[3,8,8,256]{3,2,1,0:T(8,128)S(1)}, f32[3,8,8,256]{3,2,1,0:T(8,128)S(1)}, u32[]{:S(2)}, u32[]{:S(2)}) collective-permute-start(f32[3,8,8,256]{3,2,1,0:T(8,128)S(1)} %collective-permute-done.2.refs_0_), channel_id=1, source_target_pairs={{0,12},{4,8},{8,4},{12,0},{1,13},{5,9},{9,5},{13,1},{2,14},{6,10},... | collective-permute-start | bytes 589832 | tf_op jit(solution)/shard_map/ppermute | solution.py:383
  22.2 4.1 %collective-permute-start.7 = (f32[3,8,8,256]{3,2,1,0:T(8,128)S(1)}, f32[3,8,8,256]{3,2,1,0:T(8,128)S(1)}, u32[]{:S(2)}, u32[]{:S(2)}) collective-permute-start(f32[3,8,8,256]{3,2,1,0:T(8,128)S(1)} %collective-permute-done.1.refs_1_), channel_id=1, source_target_pairs={{0,4},{4,0},{8,12},{12,8},{1,5},{5,1},{9,13},{13,9},{2,6},{6,2},{1... | collective-permute-start | bytes 589832 | tf_op jit(solution)/shard_map/ppermute | solution.py:380
  22.3 10.5 %collective-permute-start.6 = (f32[3,8,8,256]{3,2,1,0:T(8,128)S(1)}, f32[3,8,8,256]{3,2,1,0:T(8,128)S(1)}, u32[]{:S(2)}, u32[]{:S(2)}) collective-permute-start(f32[3,8,8,256]{3,2,1,0:T(8,128)S(1)} %collective-permute-done.1.refs_1_), channel_id=1, source_target_pairs={{0,12},{4,8},{8,4},{12,0},{1,13},{5,9},{9,5},{13,1},{2,14},{6,10},... | collective-permute-start | bytes 589832 | tf_op jit(solution)/shard_map/ppermute | solution.py:383
  28.0 10.2 %collective-permute-start.11 = (f32[128,512]{1,0:T(8,128)S(1)}, f32[128,512]{1,0:T(8,128)S(1)}, u32[]{:S(2)}, u32[]{:S(2)}) collective-permute-start(f32[128,512]{1,0:T(8,128)S(1)} %get-tuple-element.103), channel_id=1, source_target_pairs={{0,1},{1,0},{2,3},{3,2},{4,5},{5,4},{6,7},{7,6},{8,9},{9,8},{10,11... | collective-permute-start | bytes 786440 | tf_op jit(solution)/shard_map/ppermute | solution.py:389
  34.4 3.7 %copy-start.2 = (bf16[2,512,512]{2,1,0:T(8,128)(2,1)S(1)}, bf16[2,512,512]{2,1,0:T(8,128)(2,1)}, u32[]{:S(2)}) copy-start(bf16[2,512,512]{2,1,0:T(8,128)(2,1)} %constant.8.clone.refs_3_) | copy-start | bytes 3145732
  34.5 9.0 %collective-permute-start.10 = (f32[128,512]{1,0:T(8,128)S(1)}, f32[128,512]{1,0:T(8,128)S(1)}, u32[]{:S(2)}, u32[]{:S(2)}) collective-permute-start(f32[128,512]{1,0:T(8,128)S(1)} %get-tuple-element.100), channel_id=1, source_target_pairs={{0,1},{1,0},{2,3},{3,2},{4,5},{5,4},{6,7},{7,6},{8,9},{9,8},{10,11... | collective-permute-start | bytes 786440 | tf_op jit(solution)/shard_map/ppermute | solution.py:389

commit v6 on v5

v6 whole, which is shorter than its diff:
```python
import math

import jax
import jax.numpy as jnp
import ml_dtypes
import numpy as np
from jax import lax
from jax.experimental import pallas as pl
from jax.experimental.pallas import tpu as pltpu
from jax.sharding import PartitionSpec as P

epsilon = 1e-06
SUB, LANES = 8, 128
HALF = SUB // 2
TILES = 6
ENTRIES = 3
UNROLL = 4
FIRST_SHARE = 9
VMEM_BYTES = 16 * 1024 * 1024
PREPARE_VMEM_BYTES = 62 * 1024 * 1024
F32 = jnp.float32
BF16 = jnp.bfloat16


def split_table(table):
    high = table.astype(ml_dtypes.bfloat16)
    low = (table - high.astype(np.float64)).astype(ml_dtypes.bfloat16)
    return np.stack([high, low])


def forward_table(samples):
    steps = np.arange(samples)
    angles = (steps[:, None] * steps[None, :] % (2 * samples)) * (math.pi / samples)
    return split_table(np.concatenate([np.cos(angles), -np.sin(angles)], axis=1))


def inverse_table(samples):
    record = 2 * samples
    bins = np.arange(samples)
    lags = (np.arange(record) + samples) % record
    angles = (bins[:, None] * lags[None, :] % record) * (math.pi / samples)
    gain = np.where(bins == 0, 1.0, 2.0)[:, None] / record
    return split_table(np.concatenate([gain * np.cos(angles), -gain * np.sin(angles)], axis=0))


def split_dot(value, table_ref):
    rows = value.shape[0]
    high = value.astype(BF16)
    low = (value - high.astype(F32)).astype(BF16)
    both = jnp.dot(jnp.concatenate([high, low], axis=0), table_ref[0], preferred_element_type=F32)
    return both[:rows] + (both[rows:] + jnp.dot(high, table_ref[1], preferred_element_type=F32))


def piece_spots(twos):
    count = twos * FIRST_SHARE // 16
    return [(0, count), (count, twos - count)]


def prepare_kernel(waves_hbm, mask_hbm, weight_hbm, *refs):
    all_hbm, *out_hbms, waves_ref, mask_ref, weight_ref, result_ref, sems = refs
    pieces = len(out_hbms)
    twos, _, channels, stations, _ = waves_ref.shape
    spots = piece_spots(twos)
    copies = [
        pltpu.make_async_copy(weight_hbm, weight_ref, sems.at[0]),
        pltpu.make_async_copy(mask_hbm, mask_ref, sems.at[1]),
    ]
    for piece, (first, count) in enumerate(spots):
        spot = pl.ds(first, count)
        copies.append(pltpu.make_async_copy(waves_hbm.at[spot], waves_ref.at[spot], sems.at[2 + piece]))
    for copy in copies:
        copy.start()
    events = 2 * twos
    rows = 3 * SUB * twos
    row = lax.broadcasted_iota(jnp.int32, (rows, events), 0)
    group, row_here = row // (SUB * twos), row % (SUB * twos)
    event_of_row = jnp.where(group < 2, 2 * (row_here // SUB) + group, row_here // HALF)
    at_event = (event_of_row == lax.broadcasted_iota(jnp.int32, (rows, events), 1)).astype(F32)
    row = lax.broadcasted_iota(jnp.int32, (rows, stations), 0)
    at_station = row % HALF == lax.broadcasted_iota(jnp.int32, (rows, stations), 1)
    station_id = lax.broadcasted_iota(jnp.int32, (stations, events), 0)
    first_weight = lax.axis_index("station") * stations
    copies[0].wait()
    network = channels * sum(weight_ref[station] for station in range(weight_ref.shape[0]))
    weight = jnp.zeros((stations, events), F32)
    for station in range(stations):
        weight = jnp.where(station_id == station, weight_ref[first_weight + station], weight)
    copies[1].wait()
    amplitude = mask_ref[...].astype(F32) * jnp.sqrt(weight / network)
    picked = lax.dot_general(
        at_event,
        amplitude,
        (((1,), (1,)), ((), ())),
        precision=lax.Precision.HIGHEST,
        preferred_element_type=F32,
    )
    factor = jnp.sum(jnp.where(at_station, picked, 0.0), axis=1, keepdims=True).reshape(3, twos, SUB, 1)
    results = []
    for piece, (first, count) in enumerate(spots):
        copies[2 + piece].wait()
        spot = slice(first, first + count)
        for group in range(3):
            for side in range(2):
                part = waves_ref[spot, group, side] if group < 2 else waves_ref[spot, side, 2]
                result_ref[group, spot, side * HALF : (side + 1) * HALF, :] = part
            traces = result_ref[group, spot]
            energy = jnp.sum(traces * traces, axis=-1, keepdims=True)
            result_ref[group, spot] = traces * (lax.rsqrt(energy + epsilon) * factor[group, spot])
        for number, target in enumerate((out_hbms[piece], all_hbm.at[:, pl.ds(first, count)])):
            sem = sems.at[2 + pieces + 2 * piece + number]
            results.append(pltpu.make_async_copy(result_ref.at[:, pl.ds(first, count)], target, sem))
            results[-1].start()
    for copy in results:
        copy.wait()


def prepare(waveforms, event_mask, station_weight):
    events, stations, channels, samples = waveforms.shape
    waves = jnp.transpose(waveforms, (0, 2, 1, 3)).reshape(events // 2, 2, channels, stations, samples)
    hbm = pl.BlockSpec(memory_space=pltpu.HBM)
    spots = piece_spots(events // 2)
    pieces = len(spots)
    shape = (3, events // 2, SUB, samples)
    return pl.pallas_call(
        prepare_kernel,
        out_shape=[jax.ShapeDtypeStruct(shape, F32)]
        + [jax.ShapeDtypeStruct((3, count, SUB, samples), F32) for _, count in spots],
        in_specs=[hbm] * 3,
        out_specs=[hbm] * (1 + pieces),
        scratch_shapes=[
            pltpu.VMEM(waves.shape, F32),
            pltpu.VMEM((stations, events), event_mask.dtype),
            pltpu.SMEM(station_weight.shape, F32),
            pltpu.VMEM(shape, F32),
            pltpu.SemaphoreType.DMA((2 + 3 * pieces,)),
        ],
        compiler_params=pltpu.CompilerParams(vmem_limit_bytes=PREPARE_VMEM_BYTES),
        name="prepare",
    )(waves, event_mask.T, station_weight)


def index_kernel(events, partners_ref, counts_ref, pairs_ref, index_ref, order_ref):
    rounds, _, _, all_pairs = pairs_ref.shape
    here = lax.axis_index("cluster")
    sibling = jnp.where(here % 2 == 0, here + 1, here - 1)
    own_count = counts_ref[here]
    partners = [partners_ref[turn, here] for turn in range(rounds)]
    parts = [jnp.where(partner == here, 0, jnp.where(partner == sibling, 1, 2)) for partner in partners]
    across = jnp.int32(0)
    lane = lax.broadcasted_iota(jnp.int32, (1, LANES), 1)
    order = jnp.zeros((1, LANES), jnp.int32)
    for turn in range(rounds):
        part = parts[turn]
        across += (part == 2).astype(jnp.int32)
        place = jnp.int32(0)
        for other in range(rounds):
            ahead = parts[other] <= part if other < turn else parts[other] < part
            place += ahead.astype(jnp.int32)
        order = jnp.where(lane == place, turn, order)
        first, second = pairs_ref[turn, 0, 0:1], pairs_ref[turn, 0, 1:2]
        valid = (first < own_count) & (second < counts_ref[partners[turn]])
        entries = (
            TILES * jnp.where(valid, first, events),
            TILES * (second + part * (events + 2)),
            jnp.full((1, all_pairs), part, jnp.int32),
        )
        for kind, entry in enumerate(entries):
            for row in range(all_pairs // LANES):
                spot = (ENTRIES * place + kind) * (all_pairs // LANES) + row
                index_ref[pl.ds(spot, 1)] = entry[:, row * LANES : (row + 1) * LANES]
    order_ref[...] = jnp.where(lane == rounds, across, order)


def pair_index(partners, counts, pair_list, events):
    rounds, _, all_pairs, _ = pair_list.shape
    vmem = pl.BlockSpec(memory_space=pltpu.VMEM)
    smem = pl.BlockSpec(memory_space=pltpu.SMEM)
    return pl.pallas_call(
        lambda *refs: index_kernel(events, *refs),
        out_shape=[
            jax.ShapeDtypeStruct((rounds * ENTRIES * all_pairs // LANES, LANES), jnp.int32),
            jax.ShapeDtypeStruct((1, LANES), jnp.int32),
        ],
        in_specs=[smem, smem, vmem],
        out_specs=[vmem, vmem],
        compiler_params=pltpu.CompilerParams(vmem_limit_bytes=VMEM_BYTES),
        name="pair_index",
    )(partners, counts, jnp.transpose(pair_list, (0, 1, 3, 2)))


def fill_spectra(traces_ref, part, first, table_ref, spectra_ref):
    _, twos, _, samples = traces_ref.shape
    spot = pl.ds(first, twos)
    spectrum = split_dot(traces_ref[...].reshape(3 * twos * SUB, samples), table_ref)
    tiles = [
        spectrum[:, block * LANES : (block + 1) * LANES].reshape(3, twos, SUB, LANES) for block in range(4)
    ]
    low_half = lax.broadcasted_iota(jnp.int32, (twos, SUB, LANES), 1) < HALF
    for group in range(3):
        for side in range(2):
            lower, upper = tiles[2 * side][group], tiles[2 * side + 1][group]
            first = jnp.where(low_half, lower, pltpu.roll(upper, HALF, 1))
            second = jnp.where(low_half, pltpu.roll(lower, HALF, 1), upper)
            if group < 2:
                spectra_ref[part, spot, group, 3 * side] = first
                spectra_ref[part, spot, group, 3 * side + 1] = second
            else:
                spectra_ref[part, spot, 0, 3 * side + 2] = first
                spectra_ref[part, spot, 1, 3 * side + 2] = second


def clear_last(spectra_ref):
    spectra_ref[0, spectra_ref.shape[1] - 1] = jnp.zeros(spectra_ref.shape[2:], F32)


def spectra_kernel(places, first, *refs):
    trace_refs, table_ref, spectra_ref = refs[: len(places)], refs[len(places)], refs[-1]
    for (part, pair), traces_ref in zip(places, trace_refs, strict=True):
        fill_spectra(traces_ref, part, pair, table_ref, spectra_ref)
    if first:
        clear_last(spectra_ref)


def add_pairs(index_ref, all_pairs, turns, wanted, blocks, spectra_ref, base_refs, out_refs):
    slots = 2 * spectra_ref.shape[1]
    length = lax.axis_size("station")
    station_here = lax.axis_index("station")
    swap = length == 4
    block_pairs = all_pairs // length
    flat_ref = spectra_ref.reshape(spectra_ref.shape[0] * slots * TILES, SUB, LANES)
    row_id = lax.broadcasted_iota(jnp.int32, (SUB, LANES), 0)
    in_four, in_two, in_one = row_id < 4, row_id % 4 < 2, row_id % 2 < 1

    def down(value, rows):
        return pltpu.roll(value, rows % SUB, 0)

    def fold_four(sums):
        even, odd = (
            jnp.where(in_two, one + down(one, -2), other + down(other, 2)) for one, other in (sums[0::2], sums[1::2])
        )
        return jnp.where(in_one, even + down(even, -1), odd + down(odd, 1))

    def fold_eight(sums):
        one, other = fold_four(sums[:4]), fold_four(sums[4:])
        return jnp.where(in_four, one, down(other, 4)), jnp.where(in_four, down(one, 4), other)

    def one_turn(place, turn):
        for number, block in enumerate(blocks):
            if swap:
                source = station_here if block == 0 else station_here + 1 - 2 * (station_here % 2)
                which, row = number, place * block_pairs
            else:
                source = station_here // len(blocks) * len(blocks) + block
                which, row = 0, (place * len(blocks) + block) * block_pairs
            start = source * block_pairs

            def eight_pairs(group, carry):
                real, imag = [], []
                first = start + group * SUB
                for spot in range(SUB):
                    entry = ENTRIES * turn * all_pairs + spot
                    left = flat_ref[pl.ds(index_ref[entry + first], TILES)]
                    right = flat_ref[pl.ds(index_ref[entry + all_pairs + first], TILES)]
                    reals, imags = [], []
                    for tile in range(3):
                        left_real, left_imag = left[tile], left[tile + 3]
                        right_real, right_imag = right[tile], right[tile + 3]
                        reals.append(left_real * right_real + left_imag * right_imag)
                        imags.append(left_imag * right_real - left_real * right_imag)
                    real.append(reals[0] + reals[1] + reals[2])
                    imag.append(imags[0] + imags[1] + imags[2])
                rows = pl.ds(pl.multiple_of(row + group * SUB, SUB), SUB)
                for column, total in enumerate((*fold_eight(real), *fold_eight(imag))):
                    spot = pl.ds(column * LANES, LANES)
                    if base_refs is not None:
                        total += base_refs[which][rows, spot]
                    out_refs[which][rows, spot] = total
                return carry

            lax.fori_loop(0, block_pairs // SUB, eight_pairs, 0, unroll=min(UNROLL, block_pairs // SUB))

    for place, turn in enumerate(turns):
        pl.when(wanted(index_ref[(ENTRIES * turn + 2) * all_pairs]))(lambda: one_turn(place, turn))


def half_turns(rounds, half):
    return range(half * rounds // 2, (half + 1) * rounds // 2)


def index_copy(index_hbm, index_ref, sem):
    copy = pltpu.make_async_copy(index_hbm, index_ref, sem)
    copy.start()
    return copy


def first_near_kernel(blocks, rounds, all_pairs, index_hbm, own_ref, sibling_ref, table_ref, spectra_ref, *refs):
    *out_refs, index_ref, sem = refs
    copy = index_copy(index_hbm, index_ref, sem)
    fill_spectra(own_ref, 0, 0, table_ref, spectra_ref)
    fill_spectra(sibling_ref, 1, 0, table_ref, spectra_ref)
    clear_last(spectra_ref)
    copy.wait()
    for half in range(2):
        turns = half_turns(rounds, half)
        some = out_refs[half * len(out_refs) // 2 : (half + 1) * len(out_refs) // 2]
        add_pairs(index_ref, all_pairs, turns, lambda part: part < 2, blocks, spectra_ref, None, some)


def first_far_kernel(blocks, rounds, all_pairs, index_hbm, first_ref, last_ref, table_ref, *refs):
    spectra_ref, *out_refs, index_ref, sem = refs[len(refs) // 2 - 1 :]
    copy = index_copy(index_hbm, index_ref, sem)
    fill_spectra(first_ref, 2, 0, table_ref, spectra_ref)
    fill_spectra(last_ref, 2, first_ref.shape[1], table_ref, spectra_ref)
    copy.wait()
    for half in range(2):
        turns = half_turns(rounds, half)
        some = out_refs[half * len(out_refs) // 2 : (half + 1) * len(out_refs) // 2]
        add_pairs(index_ref, all_pairs, turns, lambda part: part == 2, blocks, spectra_ref, None, some)


def more_kernel(rounds, all_pairs, places, jobs, has_base, *refs):
    count = len(places)
    index_hbm, trace_refs, refs = refs[0], refs[1 : 1 + count], refs[1 + count :]
    if count:
        table_ref, refs = refs[0], refs[1:]
    *refs, index_ref, sem = refs
    arrays = len(refs) // 2 - 1 if has_base else len(refs) - 2
    base_refs, (spectra_ref, *out_refs) = refs[1 : 1 + arrays] if has_base else None, refs[-1 - arrays :]
    copy = index_copy(index_hbm, index_ref, sem)
    for (part, pair), traces_ref in zip(places, trace_refs, strict=True):
        fill_spectra(traces_ref, part, pair, table_ref, spectra_ref)
    if not has_base:
        for out_ref in out_refs:
            out_ref[...] = jnp.zeros(out_ref.shape, F32)
    copy.wait()
    for half, parts, blocks, first, last in jobs:

        def wanted(part, parts=parts):
            return (part >= parts[0]) & (part <= parts[-1])

        turns = half_turns(rounds, half)
        base = base_refs[first:last] if has_base else None
        add_pairs(index_ref, all_pairs, turns, wanted, blocks, spectra_ref, base, out_refs[first:last])


def call_kernel(kernel, name, operands, specs, updated, out_shapes, scratch, flops):
    vmem = pl.BlockSpec(memory_space=pltpu.VMEM)
    operands = [*operands, *updated]
    shapes = [*(jax.ShapeDtypeStruct(value.shape, value.dtype) for value in updated), *out_shapes]
    first_in = len(operands) - len(updated)
    in_specs = [vmem] * len(operands)
    out_specs = [vmem] * len(shapes)
    for place, spec in specs.items():
        in_specs[place] = spec
        if place >= first_in:
            out_specs[place - first_in] = spec
    return pl.pallas_call(
        kernel,
        out_shape=shapes,
        in_specs=in_specs,
        out_specs=out_specs,
        scratch_shapes=scratch,
        input_output_aliases={first_in + i: i for i in range(len(updated))},
        compiler_params=pltpu.CompilerParams(vmem_limit_bytes=VMEM_BYTES),
        cost_estimate=pl.CostEstimate(flops=flops, bytes_accessed=flops // 1000, transcendentals=0),
        name=name,
    )(*operands)


def invert_kernel(cross_ref, table_ref, out_ref):
    out_ref[...] = split_dot(cross_ref[...], table_ref)


def finish_kernel(turns, invert, order_ref, kept_ref, swapped_ref, table_ref, *refs):
    out_hbm, result_ref, sems = refs[-3:]
    rows = kept_ref.shape[0] // len(turns)
    lane = lax.broadcasted_iota(jnp.int32, (1, LANES), 1)
    order = order_ref[...].astype(F32)
    targets = [jnp.sum(jnp.where(lane == turn, order, 0.0)).astype(jnp.int32) for turn in turns]
    total = kept_ref[...] + swapped_ref[...]
    result_ref[...] = split_dot(total, table_ref) if invert else total
    copies = [
        pltpu.make_async_copy(
            result_ref.at[pl.ds(number * rows, rows)],
            out_hbm.at[pl.ds(pl.multiple_of(target * rows, SUB), rows)],
            sems.at[number],
        )
        for number, target in enumerate(targets)
    ]
    for copy in copies:
        copy.start()
    for copy in copies:
        copy.wait()


def finish(order, kept, swapped, table, turns, invert, result):
    rows, lags = kept.shape
    vmem = pl.BlockSpec(memory_space=pltpu.VMEM)
    hbm = pl.BlockSpec(memory_space=pltpu.HBM)
    operands = [order, kept, swapped, table] + ([] if result is None else [result])
    return pl.pallas_call(
        lambda *refs: finish_kernel(turns, invert, *refs),
        out_shape=jax.ShapeDtypeStruct((2 * rows, lags), F32),
        in_specs=[vmem] * 4 + [hbm] * (len(operands) - 4),
        out_specs=hbm,
        scratch_shapes=[
            pltpu.VMEM((rows, lags), F32),
            pltpu.SemaphoreType.DMA((len(turns),)),
        ],
        input_output_aliases={} if result is None else {4: 0},
        compiler_params=pltpu.CompilerParams(vmem_limit_bytes=VMEM_BYTES),
        cost_estimate=pl.CostEstimate(flops=1, bytes_accessed=1, transcendentals=0),
        name="finish",
    )(*operands)


def on_device(waveforms, event_mask, station_weight, partners, pair_list, counts):
    events, stations, channels, samples = waveforms.shape
    rounds, _, all_pairs, _ = pair_list.shape
    clusters = lax.axis_size("cluster")
    length = lax.axis_size("station")
    assert (stations, channels, samples) == (HALF, 3, 2 * LANES)
    assert events % 4 == 0 and rounds % 2 == 0 and clusters % 2 == 0 and length % 4 == 0
    forward = jnp.asarray(forward_table(samples))
    inverse = jnp.asarray(inverse_table(samples))

    def to_sibling(value):
        return lax.ppermute(value, "cluster", [(i, i ^ 1) for i in range(clusters)])

    def to_across(value):
        return lax.ppermute(value, "cluster", [(i, (i + 1 if i % 2 else i - 1) % clusters) for i in range(clusters)])

    def to_mirror(value):
        return lax.ppermute(value, "station", [(i, length - 1 - i) for i in range(length)])

    def swap_stations(value):
        return lax.ppermute(value, "station", [(i, i ^ 1) for i in range(length)])

    def spread(value):
        groups = np.arange(length).reshape(2, length // 2).tolist()
        value = value.reshape(rounds // 2, all_pairs // 2, 2 * samples)
        kept = lax.psum_scatter(value, "station", scatter_dimension=1, axis_index_groups=groups, tiled=True)
        kept = kept.reshape(-1, 2 * samples)
        return kept, jnp.zeros_like(kept)

    def invert(cross, table):
        return call_kernel(invert_kernel, "invert", [cross, table], {}, [], [half_shape], [], 1)[0]

    swap = length == 4
    blocks = list(range(length // 2))
    outs = 2 if swap else 1
    half_shape = jax.ShapeDtypeStruct((rounds * all_pairs // 4 // outs, 2 * samples), F32)
    spectra_shape = jax.ShapeDtypeStruct((3, events // 2 + 1, 2, TILES, SUB, LANES), F32)
    scratch = [
        pltpu.SMEM((rounds * ENTRIES * all_pairs,), jnp.int32),
        pltpu.SemaphoreType.DMA,
    ]

    anywhere = {0: pl.BlockSpec(memory_space=pl.ANY)}

    def add_spectra(traces, places, spectra, flops):
        return call_kernel(
            lambda *refs: spectra_kernel(places, not spectra, *refs),
            "add_spectra",
            [*traces, forward],
            {},
            spectra,
            [] if spectra else [spectra_shape],
            [],
            flops,
        )

    def more_sums(name, traces, places, jobs, spectra, base):
        return call_kernel(
            lambda *refs: more_kernel(rounds, all_pairs, places, jobs, bool(base), *refs),
            name,
            [index, *traces, forward] if traces else [index],
            anywhere,
            [spectra, *base],
            [] if base else [half_shape] * outs,
            scratch,
            1,
        )

    own, *pieces = prepare(waveforms, event_mask, station_weight)
    index, order = pair_index(partners, counts, pair_list, events)
    index = index.reshape(-1)
    mirror_first, mirror_last = (to_mirror(piece) for piece in pieces)
    across = [to_across(piece) for piece in pieces]
    sibling = to_sibling(own)
    spectra, *partial = call_kernel(
        lambda *refs: first_near_kernel(blocks, rounds, all_pairs, *refs),
        "first_near",
        [index, own, sibling, forward],
        anywhere,
        [],
        [spectra_shape] + [half_shape] * (2 * outs),
        scratch,
        1,
    )
    mirror_first, *partial = lax.optimization_barrier((mirror_first, *partial))
    far_first, near_first = to_across(mirror_first), to_sibling(mirror_first)
    (other,) = add_spectra([mirror_first], [(0, 0)], [], 1)
    other, *partial = lax.optimization_barrier((other, *partial))
    _, *partial = call_kernel(
        lambda *refs: first_far_kernel(blocks, rounds, all_pairs, *refs),
        "first_far",
        [index, *across, forward],
        anywhere,
        [spectra, *partial],
        [],
        scratch,
        1,
    )
    mirror_last, other, *partial = lax.optimization_barrier((mirror_last, other, *partial))
    far_last, near_last = to_across(mirror_last), to_sibling(mirror_last)
    early, late = partial[:outs], partial[outs:]
    later = piece_spots(events // 2)[1][0]
    sent = blocks[1:] if swap else blocks
    *early_kept, early_sent = early
    *late_kept, late_sent = late

    def add_sent(name, traces, places, half, parts, spectra, value):
        return more_sums(name, traces, places, [(half, parts, sent, 0, 1)], spectra, [value])

    other, early_sent = add_sent("own_sums", [mirror_last], [(0, later)], 0, (0,), other, early_sent)
    (other,) = add_spectra([near_first], [(1, 0)], [other], 1)
    other, early_sent = add_sent("sibling_sums", [near_last], [(1, later)], 0, (1,), other, early_sent)
    if not swap:
        other, late_sent = add_sent("near_sums", [far_first], [(2, 0)], 1, (0, 1), other, late_sent)
        other, late_sent = add_sent("across_sums", [far_last], [(2, later)], 1, (2,), other, late_sent)
        other, early_sent = add_sent("across_sums", [], [], 0, (2,), other, early_sent)
        early, late = spread(early_sent), spread(late_sent)
    else:
        early_received = swap_stations(early_sent)
        other, late_sent = add_sent("near_sums", [far_first], [(2, 0)], 1, (0, 1), other, late_sent)
        other, late_sent = add_sent("across_sums", [far_last], [(2, later)], 1, (2,), other, late_sent)
        late_received = swap_stations(invert(late_sent, inverse))
        jobs = [(0, (0, 1), blocks[:1], 0, 1), (1, (0, 2), blocks[:1], 1, 2)]
        other, early_kept, late_kept = more_sums("kept_sums", [], [], jobs, other, early_kept + late_kept)

        def with_across(spectra, kept):
            jobs = [(0, (2,), blocks, 0, 2)]
            _, more_kept, more_sent = more_sums("across_sums", [], [], jobs, spectra, [])
            return kept + more_kept + swap_stations(more_sent)

        early_kept = lax.cond(order[0, rounds] > rounds // 2, with_across, lambda _, kept: kept, other, early_kept)
        early, late = (early_kept, early_received), (invert(late_kept, inverse), late_received)
    result = finish(order, *early, inverse, half_turns(rounds, 0), True, None)
    result = finish(order, *late, inverse, half_turns(rounds, 1), not swap, result)
    return result.reshape(rounds, 1, all_pairs // length, 2 * samples)


def solution(mesh):
    return jax.shard_map(
        on_device,
        mesh=mesh,
        in_specs=(
            P(("groups", "cluster"), "station", None, None),
            P(("groups", "cluster"), "station"),
            P("groups"),
            P(None, "groups"),
            P(None, ("groups", "cluster"), None, None),
            P("groups"),
        ),
        out_specs=P(None, ("groups", "cluster"), "station", None),
        check_vma=False,
    )
```

time: 44.8 us -> 43.1 us (0.962)
  waiting for transfers between devices: 8.01 us -> 2.12 us
  starting transfers between devices: 13.2 us -> 18.3 us
  Pallas kernels: 18 us -> 16.8 us
    ppermute x2, starting transfers between devices: 3.36 us -> 7.57 us  [swap_stations(): return lax.ppermute(value, 'station', [(i, i ^ 1) for i in range(length)])]
    ppermute x2, waiting for transfers between devices: 6.25 us -> 2.09 us  [swap_stations(): return lax.ppermute(value, 'station', [(i, i ^ 1) for i in range(length)])]
    ppermute x4, waiting for transfers between devices: 1.75 us -> 0.01 us  [to_across(): lax.ppermute(value, 'cluster', [(i, (i + 1 if i % 2 else i - 1) % cluster...]
    ppermute x4, starting transfers between devices: 3.56 us -> 4.59 us  [to_across(): lax.ppermute(value, 'cluster', [(i, (i + 1 if i % 2 else i - 1) % cluster...]
    pallas_call x1, Pallas kernels: 1.21 us -> 0.61 us  [pair_index(): pl.pallas_call(lambda *refs: index_kernel(events, *refs), out_shape=[jax....]
    pallas_call x3, Pallas kernels: 4.64 us -> 4.08 us  [the longest x1 2.15 us: prepare(): pl.pallas_call(prepare_kernel, out_shape=[jax.ShapeDtypeStruct(shape, F32...]
    pallas_call x8 -> x11, Pallas kernels: 12.2 us -> 12.1 us  [call_kernel(): pl.pallas_call(kernel, out_shape=shapes, in_specs=in_specs, out_specs=out...]
  transfers between devices with their start and end apart: 11 -> 11, of which waited for: 3 -> 1; matrix products, arithmetic and copies ran while one was open for 1% -> 1% of each run, Pallas kernels for 33% -> 32%
where the time goes in v6:
time: 43.1 us; the launch traced here: 42.8 us
  starting transfers between devices  18.3 us (42%)
  Pallas kernels  16.8 us (39%)
  local copies, waits for them, and re-layouts  4.66 us (11%)
  waiting for transfers between devices  2.12 us (5%)
  between operations  0.89 us (2%)
    pallas_call x11, Pallas kernels, call_kernel(): pl.pallas_call(kernel, out_shape=shapes, in_specs=in_specs, out_specs=out...  12.1 us
    ppermute x2, starting transfers between devices, swap_stations(): return lax.ppermute(value, 'station', [(i, i ^ 1) for i in range(length)])  7.57 us
    ppermute x2, starting transfers between devices, to_mirror(): lax.ppermute(value, 'station', [(i, length - 1 - i) for i in range(length)])  4.77 us
    ppermute x4, starting transfers between devices, to_across(): lax.ppermute(value, 'cluster', [(i, (i + 1 if i % 2 else i - 1) % cluster...  4.59 us
    unnamed x14, local copies, waits for them, and re-layouts  4.08 us
    pallas_call x1, Pallas kernels, prepare(): pl.pallas_call(prepare_kernel, out_shape=[jax.ShapeDtypeStruct(shape, F32...  2.15 us
    ppermute x2, waiting for transfers between devices, swap_stations(): return lax.ppermute(value, 'station', [(i, i ^ 1) for i in range(length)])  2.09 us
    pallas_call x2, Pallas kernels, finish(): pl.pallas_call(lambda *refs: finish_kernel(turns, invert, *refs), out_sha...  1.94 us
  transfers between devices with their start and end apart: 11, of which 1 were waited for; matrix products, arithmetic and copies ran while one was open for 1% of the time, Pallas kernels for 32%

profile of v6, /device:TPU:0, one launch (start us, length us, event | category | flops | bytes accessed | tf_op | source)
XLA Modules:
  0.0 42.8 jit_solution(6687769653841874472)
XLA Ops:
  0.0 2.1 %prepare.1 = (f32[3,16,8,256]{3,2,1,0:T(8,128)}, f32[3,9,8,256]{3,2,1,0:T(8,128)}, f32[3,7,8,256]{3,2,1,0:T(8,128)}) custom-call(f32[16,2,3,4,256]{4,3,2,1,0:T(4,128)} %bitcast.19, s32[4,32]{1,0:T(4,128)} %bitcast.20, f32[16]{0:T(128)} %weight_hbm.1), custom_call_target="tpu_custom_call" | custom-call | tf_op jit(solution)/shard_map/prepare/pallas_call | solution.py:124
  2.2 0.5 %collective-permute-start.3 = (f32[3,16,8,256]{3,2,1,0:T(8,128)}, f32[3,16,8,256]{3,2,1,0:T(8,128)S(1)}, u32[]{:S(2)}, u32[]{:S(2)}) collective-permute-start(f32[3,16,8,256]{3,2,1,0:T(8,128)} %get-tuple-element.65.refs_1_), channel_id=1, source_target_pairs={{0,4},{4,0},{8,12},{12,8},{1,5},{5,1},{9,13},{13,9},{2,6},{6,2},{1... | collective-permute-start | bytes 1179656 | tf_op jit(solution)/shard_map/ppermute | solution.py:428
  2.7 4.7 %collective-permute-start.2 = (f32[3,9,8,256]{3,2,1,0:T(8,128)}, f32[3,9,8,256]{3,2,1,0:T(8,128)S(1)}, u32[]{:S(2)}, u32[]{:S(2)}) collective-permute-start(f32[3,9,8,256]{3,2,1,0:T(8,128)} %get-tuple-element.64), channel_id=1, source_target_pairs={{0,3},{1,2},{2,1},{3,0},{4,7},{5,6},{6,5},{7,4},{8,11},{9,10},{10,... | collective-permute-start | bytes 663560 | tf_op jit(solution)/shard_map/ppermute | solution.py:434
  7.4 1.3 %collective-permute-start.4 = (f32[3,9,8,256]{3,2,1,0:T(8,128)}, f32[3,9,8,256]{3,2,1,0:T(8,128)S(1)}, u32[]{:S(2)}, u32[]{:S(2)}) collective-permute-start(f32[3,9,8,256]{3,2,1,0:T(8,128)} %get-tuple-element.64), channel_id=1, source_target_pairs={{0,12},{4,8},{8,4},{12,0},{1,13},{5,9},{9,5},{13,1},{2,14},{6,10},... | collective-permute-start | bytes 663560 | tf_op jit(solution)/shard_map/ppermute | solution.py:431
  8.6 0.5 %collective-permute-start.5 = (f32[3,7,8,256]{3,2,1,0:T(8,128)}, f32[3,7,8,256]{3,2,1,0:T(8,128)S(1)}, u32[]{:S(2)}, u32[]{:S(2)}) collective-permute-start(f32[3,7,8,256]{3,2,1,0:T(8,128)} %get-tuple-element.63), channel_id=1, source_target_pairs={{0,12},{4,8},{8,4},{12,0},{1,13},{5,9},{9,5},{13,1},{2,14},{6,10},... | collective-permute-start | bytes 516104 | tf_op jit(solution)/shard_map/ppermute | solution.py:431
  9.1 0.1 collective-permute-start.1
  9.2 0.0 copy-start.4
  9.2 0.7 %copy-done.4 = s32[4,1,256,2]{2,3,1,0:T(2,128)S(1)} copy-done((s32[4,1,256,2]{2,3,1,0:T(2,128)S(1)}, s32[4,1,256,2]{2,3,1,0:T(2,128)}, u32[]{:S(2)}) %copy-start.4) | copy-done | bytes 8216
  9.9 0.7 %copy-done.5 = s32[4,4]{1,0:T(4,128)S(1)} copy-done((s32[4,4]{1,0:T(4,128)S(1)}, s32[4,4]{1,0:T(4,128)}, u32[]{:S(2)}) %copy-start.5) | copy-done | bytes 88
  10.6 0.7 %copy-done.6 = s32[4]{0:T(128)S(1)} copy-done((s32[4]{0:T(128)S(1)}, s32[4]{0:T(128)}, u32[]{:S(2)}) %copy-start.6) | copy-done | bytes 40
  11.2 0.6 %pair_index.1 = (s32[24,128]{1,0:T(8,128)S(1)}, s32[1,128]{1,0:T(1,128)S(1)}) custom-call(s32[4,4]{1,0:T(4,128)S(1)} %copy-done.5, s32[4]{0:T(128)S(1)} %copy-done.6, s32[4,1,2,256]{3,2,1,0:T(2,128)S(1)} %bitcast.10), custom_call_target="tpu_custom_call" | custom-call | tf_op jit(solution)/shard_map/pair_index/pallas_call | solution.py:178
  11.8 0.0 collective-permute-done.3.refs_2_
  11.9 0.0 copy-start
  11.9 1.0 %copy-done = bf16[2,256,512]{2,1,0:T(8,128)(2,1)S(1)} copy-done((bf16[2,256,512]{2,1,0:T(8,128)(2,1)S(1)}, bf16[2,256,512]{2,1,0:T(8,128)(2,1)}, u32[]{:S(2)}) %copy-start) | copy-done | bytes 524312
  12.9 1.0 %copy-done.3 = f32[3,16,8,256]{3,2,1,0:T(8,128)S(1)} copy-done((f32[3,16,8,256]{3,2,1,0:T(8,128)S(1)}, f32[3,16,8,256]{3,2,1,0:T(8,128)}, u32[]{:S(2)}) %copy-start.3) | copy-done | bytes 393240
  13.9 2.1 %first_near.1 = (f32[3,17,2,6,8,128]{5,4,3,2,1,0:T(8,128)S(1)}, f32[128,512]{1,0:T(8,128)S(1)}, f32[128,512]{1,0:T(8,128)S(1)}, f32[128,512]{1,0:T(8,128)S(1)}, f32[128,512]{1,0:T(8,128)S(1)}) custom-call(s32[3072]{0:T(1024)S(1)} %bitcast.11, f32[3,16,8,256]{3,2,1,0:T(8,128)S(1)} %copy-done.3, f32[3,16,8,256]{3,2,1,0:T(8,128)S(1)} %collective-permute-done.3.refs_2_, ...), custom_call_target="tpu_custom_call" | custom-call | flops 1 | tf_op jit(solution)/shard_map/first_near/pallas_call | solution.py:357
  16.0 0.0 collective-permute-done.2.refs_0_
  16.0 0.8 %collective-permute-start.9 = (f32[3,9,8,256]{3,2,1,0:T(8,128)S(1)}, f32[3,9,8,256]{3,2,1,0:T(8,128)S(1)}, u32[]{:S(2)}, u32[]{:S(2)}) collective-permute-start(f32[3,9,8,256]{3,2,1,0:T(8,128)S(1)} %collective-permute-done.2.refs_0_), channel_id=1, source_target_pairs={{0,4},{4,0},{8,12},{12,8},{1,5},{5,1},{9,13},{13,9},{2,6},{6,2},{1... | collective-permute-start | bytes 663560 | tf_op jit(solution)/shard_map/ppermute | solution.py:428
  16.8 1.7 %collective-permute-start.7 = (f32[3,9,8,256]{3,2,1,0:T(8,128)S(1)}, f32[3,9,8,256]{3,2,1,0:T(8,128)S(1)}, u32[]{:S(2)}, u32[]{:S(2)}) collective-permute-start(f32[3,9,8,256]{3,2,1,0:T(8,128)S(1)} %collective-permute-done.2.refs_0_), channel_id=1, source_target_pairs={{0,12},{4,8},{8,4},{12,0},{1,13},{5,9},{9,5},{13,1},{2,14},{6,10},... | collective-permute-start | bytes 663560 | tf_op jit(solution)/shard_map/ppermute | solution.py:431
  18.5 0.3 add_spectra.2.refs_3_
  18.8 0.0 collective-permute-done.5.refs_2_
  18.8 0.0 collective-permute-done.4.refs_1_
  18.8 0.0 copy-done.1
  18.8 2.3 %first_far.1 = (f32[3,17,2,6,8,128]{5,4,3,2,1,0:T(8,128)S(1)}, f32[128,512]{1,0:T(8,128)S(1)}, f32[128,512]{1,0:T(8,128)S(1)}, f32[128,512]{1,0:T(8,128)S(1)}, f32[128,512]{1,0:T(8,128)S(1)}) custom-call(s32[3072]{0:T(1024)S(1)} %bitcast.12, ...), custom_call_target="tpu_custom_call", output_to_operand_aliasing={{0}: (4, {}), {1}: (5, {}), {2}: (6, {}), {3}: (7, {}), {4}... | custom-call | flops 1 | tf_op jit(solution)/shard_map/first_far/pallas_call | solution.py:357
  21.2 0.0 collective-permute-done.1.refs_1_
  21.2 0.1 collective-permute-start.8
  21.2 1.2 %collective-permute-start.6 = (f32[3,7,8,256]{3,2,1,0:T(8,128)S(1)}, f32[3,7,8,256]{3,2,1,0:T(8,128)S(1)}, u32[]{:S(2)}, u32[]{:S(2)}) collective-permute-start(f32[3,7,8,256]{3,2,1,0:T(8,128)S(1)} %collective-permute-done.1.refs_1_), channel_id=1, source_target_pairs={{0,12},{4,8},{8,4},{12,0},{1,13},{5,9},{9,5},{13,1},{2,14},{6,10},... | collective-permute-start | bytes 516104 | tf_op jit(solution)/shard_map/ppermute | solution.py:431
  22.4 1.4 %own_sums.1 = (f32[3,17,2,6,8,128]{5,4,3,2,1,0:T(8,128)S(1)}, f32[128,512]{1,0:T(8,128)S(1)}) custom-call(s32[3072]{0:T(1024)S(1)} %bitcast.13, f32[3,7,8,256]{3,2,1,0:T(8,128)S(1)} %collective-permute-done.1.refs_1_, bf16[2,256,512]{2,1,0:T(8,128)(2,1)S(1)} %copy-done.1, ...), custom_call_target="tpu_custom_call", output_to_operand_aliasing={{0}: (3, {}), {1}: (4, {})} | custom-call | flops 1 | tf_op jit(solution)/shard_map/own_sums/pallas_call | solution.py:357
  23.8 0.0 collective-permute-done.9.refs_0_
  23.8 0.3 add_spectra.3.refs_3_
  24.2 0.0 collective-permute-done.8.refs_1_
  24.2 0.8 %sibling_sums.1 = (f32[3,17,2,6,8,128]{5,4,3,2,1,0:T(8,128)S(1)}, f32[128,512]{1,0:T(8,128)S(1)}) custom-call(s32[3072]{0:T(1024)S(1)} %bitcast.14, f32[3,7,8,256]{3,2,1,0:T(8,128)S(1)} %collective-permute-done.8.refs_1_, bf16[2,256,512]{2,1,0:T(8,128)(2,1)S(1)} %copy-done.1, ...), custom_call_target="tpu_custom_call", output_to_operand_aliasing={{0}: (3, {}), {1}: (4, {})} | custom-call | flops 1 | tf_op jit(solution)/shard_map/sibling_sums/pallas_call | solution.py:357
  25.0 4.7 %collective-permute-start.11 = (f32[128,512]{1,0:T(8,128)S(1)}, f32[128,512]{1,0:T(8,128)S(1)}, u32[]{:S(2)}, u32[]{:S(2)}) collective-permute-start(f32[128,512]{1,0:T(8,128)S(1)} %get-tuple-element.101), channel_id=1, source_target_pairs={{0,1},{1,0},{2,3},{3,2},{4,5},{5,4},{6,7},{7,6},{8,9},{9,8},{10,11... | collective-permute-start | bytes 786440 | tf_op jit(solution)/shard_map/ppermute | solution.py:437
  29.6 0.0 collective-permute-done.7.refs_1_
  29.6 0.8 %near_sums.1 = (f32[3,17,2,6,8,128]{5,4,3,2,1,0:T(8,128)S(1)}, f32[128,512]{1,0:T(8,128)S(1)}) custom-call(s32[3072]{0:T(1024)S(1)} %bitcast.15, f32[3,9,8,256]{3,2,1,0:T(8,128)S(1)} %collective-permute-done.7.refs_1_, bf16[2,256,512]{2,1,0:T(8,128)(2,1)S(1)} %copy-done.1, ...), custom_call_target="tpu_custom_call", output_to_operand_aliasing={{0}: (3, {}), {1}: (4, {})} | custom-call | flops 1 | tf_op jit(solution)/shard_map/near_sums/pallas_call | solution.py:357
  30.4 0.0 copy-start.2
  30.4 0.0 collective-permute-done.6.refs_1_
  30.5 1.4 %across_sums.3 = (f32[3,17,2,6,8,128]{5,4,3,2,1,0:T(8,128)S(1)}, f32[128,512]{1,0:T(8,128)S(1)}) custom-call(s32[3072]{0:T(1024)S(1)} %bitcast.16, f32[3,7,8,256]{3,2,1,0:T(8,128)S(1)} %collective-permute-done.6.refs_1_, bf16[2,256,512]{2,1,0:T(8,128)(2,1)S(1)} %copy-done.1, ...), custom_call_target="tpu_custom_call", output_to_operand_aliasing={{0}: (3, {}), {1}: (4, {})} | custom-call | flops 1 | tf_op jit(solution)/shard_map/across_sums/pallas_call | solution.py:357
  31.8 0.0 copy-done.2
  31.9 0.4 invert.3
  32.2 2.9 %collective-permute-start.10 = (f32[128,512]{1,0:T(8,128)S(1)}, f32[128,512]{1,0:T(8,128)S(1)}, u32[]{:S(2)}, u32[]{:S(2)}) collective-permute-start(f32[128,512]{1,0:T(8,128)S(1)} %invert.3), channel_id=1, source_target_pairs={{0,1},{1,0},{2,3},{3,2},{4,5},{5,4},{6,7},{7,6},{8,9},{9,8},{10,11... | collective-permute-start | bytes 786440 | tf_op jit(solution)/shard_map/ppermute | solution.py:437
  35.1 0.6 %slice.3 = s32[1,1]{1,0:T(1,128)} slice(s32[1,128]{1,0:T(1,128)S(1)} %get-tuple-element.61.refs_0_), slice={[0:1], [4:5]} | slice | bytes 8 | tf_op jit(solution)/shard_map/slice | solution.py:547
  36.3 2.0 %kept_sums.1 = (f32[3,17,2,6,8,128]{5,4,3,2,1,0:T(8,128)S(1)}, f32[128,512]{1,0:T(8,128)S(1)}, f32[128,512]{1,0:T(8,128)S(1)}) custom-call(s32[3072]{0:T(1024)S(1)} %bitcast.17, f32[3,17,2,6,8,128]{5,4,3,2,1,0:T(8,128)S(1)} %get-tuple-element.94.refs_1_, ...), custom_call_target="tpu_custom_call", output_to_operand_aliasing={{0}: (1, {}), {1}: (2, {}), {2}: (3, {})} | custom-call | flops 1 | tf_op jit(solution)/shard_map/kept_sums/pallas_call | solution.py:357
  38.4 0.4 invert.2.refs_1_
  38.7 0.0 collective-permute-done.11.refs_2_
  38.8 1.1 %finish.2.refs_4_ = f32[256,512]{1,0:T(8,128)} custom-call(s32[1,128]{1,0:T(1,128)S(1)} %get-tuple-element.61.refs_0_, f32[128,512]{1,0:T(8,128)S(1)} %get-tuple-element.102.refs_1_, f32[128,512]{1,0:T(8,128)S(1)} %collective-permute-done.11.refs_2_, bf16[2,512,512]{2,1,0:T(8,128)(2,1)S(1)} %copy-done.2), custom_call_target="tpu_custom_call" | custom-call | flops 1 | bytes 1 | tf_op jit(solution)/shard_map/finish/pallas_call | solution.py:401
  39.9 2.1 %collective-permute-done.10.refs_2_ = f32[128,512]{1,0:T(8,128)S(1)} collective-permute-done((f32[128,512]{1,0:T(8,128)S(1)}, f32[128,512]{1,0:T(8,128)S(1)}, u32[]{:S(2)}, u32[]{:S(2)}) %collective-permute-start.10) | collective-permute-done | bytes 262176 | tf_op jit(solution)/shard_map/ppermute | solution.py:437
  42.0 0.8 %finish.3 = f32[256,512]{1,0:T(8,128)} custom-call(s32[1,128]{1,0:T(1,128)S(1)} %get-tuple-element.61.refs_0_, f32[128,512]{1,0:T(8,128)S(1)} %invert.2.refs_1_, f32[128,512]{1,0:T(8,128)S(1)} %collective-permute-done.10.refs_2_, bf16[2,512,512]{2,1,0:T(8,128)(2,1)S(1)} %copy-done.2, f32[256,512]{1,0:T(8,128)} %finish.2.refs_4_), custom_call_target="tpu_custom_call", output_to_operand_aliasing={{}: (4, {})} | custom-call | flops 1 | bytes 1 | tf_op jit(solution)/shard_map/finish/pallas_call | solution.py:401
  (5 shorter events, 0.0 us)
Async XLA Ops:
  2.2 9.7 %collective-permute-start.3 = (f32[3,16,8,256]{3,2,1,0:T(8,128)}, f32[3,16,8,256]{3,2,1,0:T(8,128)S(1)}, u32[]{:S(2)}, u32[]{:S(2)}) collective-permute-start(f32[3,16,8,256]{3,2,1,0:T(8,128)} %get-tuple-element.65.refs_1_), channel_id=1, source_target_pairs={{0,4},{4,0},{8,12},{12,8},{1,5},{5,1},{9,13},{13,9},{2,6},{6,2},{1... | collective-permute-start | bytes 1179656 | tf_op jit(solution)/shard_map/ppermute | solution.py:428
  2.7 13.3 %collective-permute-start.2 = (f32[3,9,8,256]{3,2,1,0:T(8,128)}, f32[3,9,8,256]{3,2,1,0:T(8,128)S(1)}, u32[]{:S(2)}, u32[]{:S(2)}) collective-permute-start(f32[3,9,8,256]{3,2,1,0:T(8,128)} %get-tuple-element.64), channel_id=1, source_target_pairs={{0,3},{1,2},{2,1},{3,0},{4,7},{5,6},{6,5},{7,4},{8,11},{9,10},{10,... | collective-permute-start | bytes 663560 | tf_op jit(solution)/shard_map/ppermute | solution.py:434
  7.4 11.5 %collective-permute-start.4 = (f32[3,9,8,256]{3,2,1,0:T(8,128)}, f32[3,9,8,256]{3,2,1,0:T(8,128)S(1)}, u32[]{:S(2)}, u32[]{:S(2)}) collective-permute-start(f32[3,9,8,256]{3,2,1,0:T(8,128)} %get-tuple-element.64), channel_id=1, source_target_pairs={{0,12},{4,8},{8,4},{12,0},{1,13},{5,9},{9,5},{13,1},{2,14},{6,10},... | collective-permute-start | bytes 663560 | tf_op jit(solution)/shard_map/ppermute | solution.py:431
  8.6 10.2 %collective-permute-start.5 = (f32[3,7,8,256]{3,2,1,0:T(8,128)}, f32[3,7,8,256]{3,2,1,0:T(8,128)S(1)}, u32[]{:S(2)}, u32[]{:S(2)}) collective-permute-start(f32[3,7,8,256]{3,2,1,0:T(8,128)} %get-tuple-element.63), channel_id=1, source_target_pairs={{0,12},{4,8},{8,4},{12,0},{1,13},{5,9},{9,5},{13,1},{2,14},{6,10},... | collective-permute-start | bytes 516104 | tf_op jit(solution)/shard_map/ppermute | solution.py:431
  9.1 12.1 %collective-permute-start.1 = (f32[3,7,8,256]{3,2,1,0:T(8,128)}, f32[3,7,8,256]{3,2,1,0:T(8,128)S(1)}, u32[]{:S(2)}, u32[]{:S(2)}) collective-permute-start(f32[3,7,8,256]{3,2,1,0:T(8,128)} %get-tuple-element.63), channel_id=1, source_target_pairs={{0,3},{1,2},{2,1},{3,0},{4,7},{5,6},{6,5},{7,4},{8,11},{9,10},{10,... | collective-permute-start | bytes 516104 | tf_op jit(solution)/shard_map/ppermute | solution.py:434
  9.2 0.7 %copy-start.4 = (s32[4,1,256,2]{2,3,1,0:T(2,128)S(1)}, s32[4,1,256,2]{2,3,1,0:T(2,128)}, u32[]{:S(2)}) copy-start(s32[4,1,256,2]{2,3,1,0:T(2,128)} %param.14) | copy-start | bytes 24580
  9.9 0.7 %copy-start.5 = (s32[4,4]{1,0:T(4,128)S(1)}, s32[4,4]{1,0:T(4,128)}, u32[]{:S(2)}) copy-start(s32[4,4]{1,0:T(4,128)} %refs_0_.1) | copy-start | bytes 196
  10.6 0.7 %copy-start.6 = (s32[4]{0:T(128)S(1)}, s32[4]{0:T(128)}, u32[]{:S(2)}) copy-start(s32[4]{0:T(128)} %refs_1_.3) | copy-start | bytes 52
  11.9 1.0 %copy-start = (bf16[2,256,512]{2,1,0:T(8,128)(2,1)S(1)}, bf16[2,256,512]{2,1,0:T(8,128)(2,1)}, u32[]{:S(2)}) copy-start(bf16[2,256,512]{2,1,0:T(8,128)(2,1)} %constant.7.clone.refs_3_.refs_1_.refs_2_) | copy-start | bytes 1572868
  12.9 1.0 %copy-start.3 = (f32[3,16,8,256]{3,2,1,0:T(8,128)S(1)}, f32[3,16,8,256]{3,2,1,0:T(8,128)}, u32[]{:S(2)}) copy-start(f32[3,16,8,256]{3,2,1,0:T(8,128)} %get-tuple-element.65.refs_1_) | copy-start | bytes 1179652
  13.9 4.9 %copy-start.1 = (bf16[2,256,512]{2,1,0:T(8,128)(2,1)S(1)}, bf16[2,256,512]{2,1,0:T(8,128)(2,1)}, u32[]{:S(2)}) copy-start(bf16[2,256,512]{2,1,0:T(8,128)(2,1)} %constant.7.clone.refs_3_.refs_1_.refs_2_) | copy-start | bytes 1572868
  16.0 7.8 %collective-permute-start.9 = (f32[3,9,8,256]{3,2,1,0:T(8,128)S(1)}, f32[3,9,8,256]{3,2,1,0:T(8,128)S(1)}, u32[]{:S(2)}, u32[]{:S(2)}) collective-permute-start(f32[3,9,8,256]{3,2,1,0:T(8,128)S(1)} %collective-permute-done.2.refs_0_), channel_id=1, source_target_pairs={{0,4},{4,0},{8,12},{12,8},{1,5},{5,1},{9,13},{13,9},{2,6},{6,2},{1... | collective-permute-start | bytes 663560 | tf_op jit(solution)/shard_map/ppermute | solution.py:428
  16.8 12.9 %collective-permute-start.7 = (f32[3,9,8,256]{3,2,1,0:T(8,128)S(1)}, f32[3,9,8,256]{3,2,1,0:T(8,128)S(1)}, u32[]{:S(2)}, u32[]{:S(2)}) collective-permute-start(f32[3,9,8,256]{3,2,1,0:T(8,128)S(1)} %collective-permute-done.2.refs_0_), channel_id=1, source_target_pairs={{0,12},{4,8},{8,4},{12,0},{1,13},{5,9},{9,5},{13,1},{2,14},{6,10},... | collective-permute-start | bytes 663560 | tf_op jit(solution)/shard_map/ppermute | solution.py:431
  21.2 3.0 %collective-permute-start.8 = (f32[3,7,8,256]{3,2,1,0:T(8,128)S(1)}, f32[3,7,8,256]{3,2,1,0:T(8,128)S(1)}, u32[]{:S(2)}, u32[]{:S(2)}) collective-permute-start(f32[3,7,8,256]{3,2,1,0:T(8,128)S(1)} %collective-permute-done.1.refs_1_), channel_id=1, source_target_pairs={{0,4},{4,0},{8,12},{12,8},{1,5},{5,1},{9,13},{13,9},{2,6},{6,2},{1... | collective-permute-start | bytes 516104 | tf_op jit(solution)/shard_map/ppermute | solution.py:428
  21.2 9.2 %collective-permute-start.6 = (f32[3,7,8,256]{3,2,1,0:T(8,128)S(1)}, f32[3,7,8,256]{3,2,1,0:T(8,128)S(1)}, u32[]{:S(2)}, u32[]{:S(2)}) collective-permute-start(f32[3,7,8,256]{3,2,1,0:T(8,128)S(1)} %collective-permute-done.1.refs_1_), channel_id=1, source_target_pairs={{0,12},{4,8},{8,4},{12,0},{1,13},{5,9},{9,5},{13,1},{2,14},{6,10},... | collective-permute-start | bytes 516104 | tf_op jit(solution)/shard_map/ppermute | solution.py:431
  25.0 13.8 %collective-permute-start.11 = (f32[128,512]{1,0:T(8,128)S(1)}, f32[128,512]{1,0:T(8,128)S(1)}, u32[]{:S(2)}, u32[]{:S(2)}) collective-permute-start(f32[128,512]{1,0:T(8,128)S(1)} %get-tuple-element.101), channel_id=1, source_target_pairs={{0,1},{1,0},{2,3},{3,2},{4,5},{5,4},{6,7},{7,6},{8,9},{9,8},{10,11... | collective-permute-start | bytes 786440 | tf_op jit(solution)/shard_map/ppermute | solution.py:437
  30.4 1.4 %copy-start.2 = (bf16[2,512,512]{2,1,0:T(8,128)(2,1)S(1)}, bf16[2,512,512]{2,1,0:T(8,128)(2,1)}, u32[]{:S(2)}) copy-start(bf16[2,512,512]{2,1,0:T(8,128)(2,1)} %constant.8.clone.table_ref.refs_3_) | copy-start | bytes 3145732
  32.2 9.7 %collective-permute-start.10 = (f32[128,512]{1,0:T(8,128)S(1)}, f32[128,512]{1,0:T(8,128)S(1)}, u32[]{:S(2)}, u32[]{:S(2)}) collective-permute-start(f32[128,512]{1,0:T(8,128)S(1)} %invert.3), channel_id=1, source_target_pairs={{0,1},{1,0},{2,3},{3,2},{4,5},{5,4},{6,7},{7,6},{8,9},{9,8},{10,11... | collective-permute-start | bytes 786440 | tf_op jit(solution)/shard_map/ppermute | solution.py:437

commit v7 on v6

--- a/solution.py
+++ b/solution.py
@@ -300,32 +300,25 @@
     fill_spectra(sibling_ref, 1, 0, table_ref, spectra_ref)
     clear_last(spectra_ref)
     copy.wait()
+    for out_ref in out_refs:
+        out_ref[...] = jnp.zeros(out_ref.shape, F32)
     for half in range(2):
         turns = half_turns(rounds, half)
         some = out_refs[half * len(out_refs) // 2 : (half + 1) * len(out_refs) // 2]
         add_pairs(index_ref, all_pairs, turns, lambda part: part < 2, blocks, spectra_ref, None, some)
 
 
-def first_far_kernel(blocks, rounds, all_pairs, index_hbm, first_ref, last_ref, table_ref, *refs):
-    spectra_ref, *out_refs, index_ref, sem = refs[len(refs) // 2 - 1 :]
-    copy = index_copy(index_hbm, index_ref, sem)
-    fill_spectra(first_ref, 2, 0, table_ref, spectra_ref)
-    fill_spectra(last_ref, 2, first_ref.shape[1], table_ref, spectra_ref)
-    copy.wait()
-    for half in range(2):
-        turns = half_turns(rounds, half)
-        some = out_refs[half * len(out_refs) // 2 : (half + 1) * len(out_refs) // 2]
-        add_pairs(index_ref, all_pairs, turns, lambda part: part == 2, blocks, spectra_ref, None, some)
-
-
-def more_kernel(rounds, all_pairs, places, jobs, has_base, *refs):
+def more_kernel(all_pairs, places, jobs, with_inverse, has_base, *refs):
     count = len(places)
     index_hbm, trace_refs, refs = refs[0], refs[1 : 1 + count], refs[1 + count :]
     if count:
         table_ref, refs = refs[0], refs[1:]
+    if with_inverse:
+        inverse_ref, refs = refs[0], refs[1:]
     *refs, index_ref, sem = refs
     arrays = len(refs) // 2 - 1 if has_base else len(refs) - 2
-    base_refs, (spectra_ref, *out_refs) = refs[1 : 1 + arrays] if has_base else None, refs[-1 - arrays :]
+    base_refs = refs[1 : 1 + arrays] if has_base else None
+    spectra_ref, *out_refs = refs[-1 - arrays :]
     copy = index_copy(index_hbm, index_ref, sem)
     for (part, pair), traces_ref in zip(places, trace_refs, strict=True):
         fill_spectra(traces_ref, part, pair, table_ref, spectra_ref)
@@ -333,14 +326,15 @@
         for out_ref in out_refs:
             out_ref[...] = jnp.zeros(out_ref.shape, F32)
     copy.wait()
-    for half, parts, blocks, first, last in jobs:
+    for turns, parts, blocks, first, last in jobs:
 
         def wanted(part, parts=parts):
             return (part >= parts[0]) & (part <= parts[-1])
 
-        turns = half_turns(rounds, half)
         base = base_refs[first:last] if has_base else None
         add_pairs(index_ref, all_pairs, turns, wanted, blocks, spectra_ref, base, out_refs[first:last])
+    if with_inverse:
+        out_refs[-1][...] = split_dot(out_refs[-1][...], inverse_ref)
 
 
 def call_kernel(kernel, name, operands, specs, updated, out_shapes, scratch, flops):
@@ -367,17 +361,13 @@
     )(*operands)
 
 
-def invert_kernel(cross_ref, table_ref, out_ref):
-    out_ref[...] = split_dot(cross_ref[...], table_ref)
-
-
-def finish_kernel(turns, invert, order_ref, kept_ref, swapped_ref, table_ref, *refs):
-    out_hbm, result_ref, sems = refs[-3:]
-    rows = kept_ref.shape[0] // len(turns)
+def finish_kernel(turns, invert, terms, order_ref, table_ref, *refs):
+    term_refs, (out_hbm, result_ref, sems) = refs[:terms], refs[-3:]
+    rows = result_ref.shape[0] // len(turns)
     lane = lax.broadcasted_iota(jnp.int32, (1, LANES), 1)
     order = order_ref[...].astype(F32)
     targets = [jnp.sum(jnp.where(lane == turn, order, 0.0)).astype(jnp.int32) for turn in turns]
-    total = kept_ref[...] + swapped_ref[...]
+    total = sum(ref[...] for ref in term_refs)
     result_ref[...] = split_dot(total, table_ref) if invert else total
     copies = [
         pltpu.make_async_copy(
@@ -393,21 +383,21 @@
         copy.wait()
 
 
-def finish(order, kept, swapped, table, turns, invert, result):
-    rows, lags = kept.shape
+def finish(order, terms, table, turns, invert, result):
+    rows, lags = terms[0].shape
     vmem = pl.BlockSpec(memory_space=pltpu.VMEM)
     hbm = pl.BlockSpec(memory_space=pltpu.HBM)
-    operands = [order, kept, swapped, table] + ([] if result is None else [result])
+    operands = [order, table, *terms] + ([] if result is None else [result])
     return pl.pallas_call(
-        lambda *refs: finish_kernel(turns, invert, *refs),
+        lambda *refs: finish_kernel(turns, invert, len(terms), *refs),
         out_shape=jax.ShapeDtypeStruct((2 * rows, lags), F32),
-        in_specs=[vmem] * 4 + [hbm] * (len(operands) - 4),
+        in_specs=[vmem] * (2 + len(terms)) + ([] if result is None else [hbm]),
         out_specs=hbm,
         scratch_shapes=[
             pltpu.VMEM((rows, lags), F32),
             pltpu.SemaphoreType.DMA((len(turns),)),
         ],
-        input_output_aliases={} if result is None else {4: 0},
+        input_output_aliases={} if result is None else {2 + len(terms): 0},
         compiler_params=pltpu.CompilerParams(vmem_limit_bytes=VMEM_BYTES),
         cost_estimate=pl.CostEstimate(flops=1, bytes_accessed=1, transcendentals=0),
         name="finish",
@@ -440,8 +430,7 @@
         groups = np.arange(length).reshape(2, length // 2).tolist()
         value = value.reshape(rounds // 2, all_pairs // 2, 2 * samples)
         kept = lax.psum_scatter(value, "station", scatter_dimension=1, axis_index_groups=groups, tiled=True)
-        kept = kept.reshape(-1, 2 * samples)
-        return kept, jnp.zeros_like(kept)
+        return [kept.reshape(-1, 2 * samples)]
 
     def invert(cross, table):
         return call_kernel(invert_kernel, "invert", [cross, table], {}, [], [half_shape], [], 1)[0]
@@ -470,11 +459,14 @@
             flops,
         )
 
-    def more_sums(name, traces, places, jobs, spectra, base):
+    early_turns, late_turns = half_turns(rounds, 0), half_turns(rounds, 1)
+
+    def more_sums(name, traces, places, jobs, spectra, base, with_inverse=False):
+        tables = [forward] * bool(traces) + [inverse] * with_inverse
         return call_kernel(
-            lambda *refs: more_kernel(rounds, all_pairs, places, jobs, bool(base), *refs),
+            lambda *refs: more_kernel(all_pairs, places, jobs, with_inverse, bool(base), *refs),
             name,
-            [index, *traces, forward] if traces else [index],
+            [index, *traces, *tables],
             anywhere,
             [spectra, *base],
             [] if base else [half_shape] * outs,
@@ -501,53 +493,52 @@
     mirror_first, *partial = lax.optimization_barrier((mirror_first, *partial))
     far_first, near_first = to_across(mirror_first), to_sibling(mirror_first)
     (other,) = add_spectra([mirror_first], [(0, 0)], [], 1)
-    other, *partial = lax.optimization_barrier((other, *partial))
-    _, *partial = call_kernel(
-        lambda *refs: first_far_kernel(blocks, rounds, all_pairs, *refs),
-        "first_far",
-        [index, *across, forward],
-        anywhere,
-        [spectra, *partial],
-        [],
-        scratch,
-        1,
-    )
-    mirror_last, other, *partial = lax.optimization_barrier((mirror_last, other, *partial))
+    early, late = partial[:outs], partial[outs:]
+    later = mirror_first.shape[1]
+    other, spectra = lax.optimization_barrier((other, spectra))
+    (spectra,) = add_spectra(across, [(2, 0), (2, later)], [spectra], 1)
+    mirror_last, other, spectra = lax.optimization_barrier((mirror_last, other, spectra))
     far_last, near_last = to_across(mirror_last), to_sibling(mirror_last)
-    early, late = partial[:outs], partial[outs:]
-    later = piece_spots(events // 2)[1][0]
     sent = blocks[1:] if swap else blocks
     *early_kept, early_sent = early
+
+    def add_sent(name, traces, places, turns, parts, spectra, value, **options):
+        return more_sums(name, traces, places, [(turns, parts, sent, 0, 1)], spectra, [value], **options)
+
+    traces, places = [mirror_last, near_first, near_last], [(0, later), (1, 0), (1, later)]
+    other, early_sent = add_sent("near_sums", traces, places, early_turns, (0, 1), other, early_sent)
+    early_sent, spectra, *late = lax.optimization_barrier((early_sent, spectra, *late))
+    jobs = [(late_turns, (2,), blocks, 0, outs)]
+    spectra, *late = more_sums("across_sums", [], [], jobs, spectra, late)
     *late_kept, late_sent = late
-
-    def add_sent(name, traces, places, half, parts, spectra, value):
-        return more_sums(name, traces, places, [(half, parts, sent, 0, 1)], spectra, [value])
-
-    other, early_sent = add_sent("own_sums", [mirror_last], [(0, later)], 0, (0,), other, early_sent)
-    (other,) = add_spectra([near_first], [(1, 0)], [other], 1)
-    other, early_sent = add_sent("sibling_sums", [near_last], [(1, later)], 0, (1,), other, early_sent)
-    if not swap:
-        other, late_sent = add_sent("near_sums", [far_first], [(2, 0)], 1, (0, 1), other, late_sent)
-        other, late_sent = add_sent("across_sums", [far_last], [(2, later)], 1, (2,), other, late_sent)
-        other, early_sent = add_sent("across_sums", [], [], 0, (2,), other, early_sent)
+    other, late_sent = add_sent("near_sums", [far_first], [(2, 0)], late_turns, (0, 1), other, late_sent)
+    traces, places = [far_last], [(2, later)]
+    if swap:
+        early_received = swap_stations(early_sent)
+        other, late_sent = add_sent(
+            "across_sums", traces, places, late_turns, (2,), other, late_sent, with_inverse=True
+        )
+        late_received = swap_stations(late_sent)
+        jobs = [(early_turns, (0, 1), blocks[:1], 0, 1), (late_turns, (0, 1, 2), blocks[:1], 1, 2)]
+        kept = early_kept + late_kept
+        other, early_kept, late_kept = more_sums("kept_sums", [], [], jobs, other, kept, with_inverse=True)
+
+        def with_across(spectra, other, kept):
+            jobs = [(early_turns, (2,), blocks, 0, 2)]
+            _, *more = more_sums("across_sums", [], [], jobs, spectra, [])
+            _, more_kept, more_sent = more_sums("across_sums", [], [], jobs, other, more)
+            return kept + more_kept + swap_stations(more_sent)
+
+        many = order[0, rounds] > len(late_turns)
+        early_kept = lax.cond(many, with_across, lambda _, __, kept: kept, spectra, other, early_kept)
+        early, late = [early_kept, early_received], [late_kept, late_received]
+    else:
+        other, late_sent = add_sent("across_sums", traces, places, late_turns, (2,), other, late_sent)
+        spectra, early_sent = add_sent("across_sums", [], [], early_turns, (2,), spectra, early_sent)
+        other, early_sent = add_sent("across_sums", [], [], early_turns, (2,), other, early_sent)
         early, late = spread(early_sent), spread(late_sent)
-    else:
-        early_received = swap_stations(early_sent)
-        other, late_sent = add_sent("near_sums", [far_first], [(2, 0)], 1, (0, 1), other, late_sent)
-        other, late_sent = add_sent("across_sums", [far_last], [(2, later)], 1, (2,), other, late_sent)
-        late_received = swap_stations(invert(late_sent, inverse))
-        jobs = [(0, (0, 1), blocks[:1], 0, 1), (1, (0, 2), blocks[:1], 1, 2)]
-        other, early_kept, late_kept = more_sums("kept_sums", [], [], jobs, other, early_kept + late_kept)
-
-        def with_across(spectra, kept):
-            jobs = [(0, (2,), blocks, 0, 2)]
-            _, more_kept, more_sent = more_sums("across_sums", [], [], jobs, spectra, [])
-            return kept + more_kept + swap_stations(more_sent)
-
-        early_kept = lax.cond(order[0, rounds] > rounds // 2, with_across, lambda _, kept: kept, other, early_kept)
-        early, late = (early_kept, early_received), (invert(late_kept, inverse), late_received)
-    result = finish(order, *early, inverse, half_turns(rounds, 0), True, None)
-    result = finish(order, *late, inverse, half_turns(rounds, 1), not swap, result)
+    result = finish(order, early, inverse, early_turns, True, None)
+    result = finish(order, late, inverse, late_turns, not swap, result)
     return result.reshape(rounds, 1, all_pairs // length, 2 * samples)
 
 

time: 43.1 us -> 42.9 us (level)
  Pallas kernels: 16.8 us -> 16 us
    pallas_call x11 -> x8, Pallas kernels: 12.1 us -> 11.3 us  [call_kernel(): pl.pallas_call(kernel, out_shape=shapes, in_specs=in_specs, out_specs=out...]
    ppermute x3, starting transfers between devices: 1.37 us -> 0.79 us  [to_sibling(): return lax.ppermute(value, 'cluster', [(i, i ^ 1) for i in range(clusters)])]
    ppermute x2, starting transfers between devices: 7.57 us -> 8.13 us  [swap_stations(): return lax.ppermute(value, 'station', [(i, i ^ 1) for i in range(length)])]
  transfers between devices with their start and end apart: 11 -> 11, of which waited for: 1 -> 1; matrix products, arithmetic and copies ran while one was open for 1% -> 1% of each run, Pallas kernels for 32% -> 30%
where the time goes in v7:
time: 42.9 us; the launch traced here: 42.6 us
  starting transfers between devices  18.5 us (43%)
  Pallas kernels  16 us (37%)
  local copies, waits for them, and re-layouts  4.76 us (11%)
  waiting for transfers between devices  2.51 us (6%)
  between operations  0.85 us (2%)
    pallas_call x8, Pallas kernels, call_kernel(): pl.pallas_call(kernel, out_shape=shapes, in_specs=in_specs, out_specs=out...  11.3 us
    ppermute x2, starting transfers between devices, swap_stations(): return lax.ppermute(value, 'station', [(i, i ^ 1) for i in range(length)])  8.13 us
    ppermute x4, starting transfers between devices, to_across(): lax.ppermute(value, 'cluster', [(i, (i + 1 if i % 2 else i - 1) % cluster...  4.79 us
    ppermute x2, starting transfers between devices, to_mirror(): lax.ppermute(value, 'station', [(i, length - 1 - i) for i in range(length)])  4.77 us
    unnamed x14, local copies, waits for them, and re-layouts  4.18 us
    ppermute x2, waiting for transfers between devices, swap_stations(): return lax.ppermute(value, 'station', [(i, i ^ 1) for i in range(length)])  2.48 us
    pallas_call x1, Pallas kernels, prepare(): pl.pallas_call(prepare_kernel, out_shape=[jax.ShapeDtypeStruct(shape, F32...  2.15 us
    pallas_call x2, Pallas kernels, finish(): pl.pallas_call(lambda *refs: finish_kernel(turns, invert, len(terms), *re...  1.94 us
  transfers between devices with their start and end apart: 11, of which 1 were waited for; matrix products, arithmetic and copies ran while one was open for 1% of the time, Pallas kernels for 30%

profile of v7, /device:TPU:0, one launch (start us, length us, event | category | flops | bytes accessed | tf_op | source)
XLA Modules:
  0.0 42.6 jit_solution(6961370544277307051)
XLA Ops:
  0.0 2.1 %prepare.1 = (f32[3,16,8,256]{3,2,1,0:T(8,128)}, f32[3,9,8,256]{3,2,1,0:T(8,128)}, f32[3,7,8,256]{3,2,1,0:T(8,128)}) custom-call(f32[16,2,3,4,256]{4,3,2,1,0:T(4,128)} %bitcast.18, s32[4,32]{1,0:T(4,128)} %bitcast.19, f32[16]{0:T(128)} %weight_hbm.1), custom_call_target="tpu_custom_call" | custom-call | tf_op jit(solution)/shard_map/prepare/pallas_call | solution.py:124
  2.2 0.5 %collective-permute-start.3 = (f32[3,16,8,256]{3,2,1,0:T(8,128)}, f32[3,16,8,256]{3,2,1,0:T(8,128)S(1)}, u32[]{:S(2)}, u32[]{:S(2)}) collective-permute-start(f32[3,16,8,256]{3,2,1,0:T(8,128)} %get-tuple-element.65.refs_1_), channel_id=1, source_target_pairs={{0,4},{4,0},{8,12},{12,8},{1,5},{5,1},{9,13},{13,9},{2,6},{6,2},{1... | collective-permute-start | bytes 1179656 | tf_op jit(solution)/shard_map/ppermute | solution.py:418
  2.7 4.7 %collective-permute-start.2 = (f32[3,9,8,256]{3,2,1,0:T(8,128)}, f32[3,9,8,256]{3,2,1,0:T(8,128)S(1)}, u32[]{:S(2)}, u32[]{:S(2)}) collective-permute-start(f32[3,9,8,256]{3,2,1,0:T(8,128)} %get-tuple-element.64), channel_id=1, source_target_pairs={{0,3},{1,2},{2,1},{3,0},{4,7},{5,6},{6,5},{7,4},{8,11},{9,10},{10,... | collective-permute-start | bytes 663560 | tf_op jit(solution)/shard_map/ppermute | solution.py:424
  7.4 1.3 %collective-permute-start.4 = (f32[3,9,8,256]{3,2,1,0:T(8,128)}, f32[3,9,8,256]{3,2,1,0:T(8,128)S(1)}, u32[]{:S(2)}, u32[]{:S(2)}) collective-permute-start(f32[3,9,8,256]{3,2,1,0:T(8,128)} %get-tuple-element.64), channel_id=1, source_target_pairs={{0,12},{4,8},{8,4},{12,0},{1,13},{5,9},{9,5},{13,1},{2,14},{6,10},... | collective-permute-start | bytes 663560 | tf_op jit(solution)/shard_map/ppermute | solution.py:421
  8.6 0.5 %collective-permute-start.5 = (f32[3,7,8,256]{3,2,1,0:T(8,128)}, f32[3,7,8,256]{3,2,1,0:T(8,128)S(1)}, u32[]{:S(2)}, u32[]{:S(2)}) collective-permute-start(f32[3,7,8,256]{3,2,1,0:T(8,128)} %get-tuple-element.63), channel_id=1, source_target_pairs={{0,12},{4,8},{8,4},{12,0},{1,13},{5,9},{9,5},{13,1},{2,14},{6,10},... | collective-permute-start | bytes 516104 | tf_op jit(solution)/shard_map/ppermute | solution.py:421
  9.1 0.1 collective-permute-start.1
  9.2 0.0 copy-start.4
  9.2 0.7 %copy-done.4 = s32[4,1,256,2]{2,3,1,0:T(2,128)S(1)} copy-done((s32[4,1,256,2]{2,3,1,0:T(2,128)S(1)}, s32[4,1,256,2]{2,3,1,0:T(2,128)}, u32[]{:S(2)}) %copy-start.4) | copy-done | bytes 8216
  9.9 0.0 copy-start.5
  9.9 0.7 %copy-done.5 = s32[4,4]{1,0:T(4,128)S(1)} copy-done((s32[4,4]{1,0:T(4,128)S(1)}, s32[4,4]{1,0:T(4,128)}, u32[]{:S(2)}) %copy-start.5) | copy-done | bytes 88
  10.6 0.0 copy-start.6
  10.6 0.7 %copy-done.6 = s32[4]{0:T(128)S(1)} copy-done((s32[4]{0:T(128)S(1)}, s32[4]{0:T(128)}, u32[]{:S(2)}) %copy-start.6) | copy-done | bytes 40
  11.2 0.6 %pair_index.1 = (s32[24,128]{1,0:T(8,128)S(1)}, s32[1,128]{1,0:T(1,128)S(1)}) custom-call(s32[4,4]{1,0:T(4,128)S(1)} %copy-done.5, s32[4]{0:T(128)S(1)} %copy-done.6, s32[4,1,2,256]{3,2,1,0:T(2,128)S(1)} %bitcast.10), custom_call_target="tpu_custom_call" | custom-call | tf_op jit(solution)/shard_map/pair_index/pallas_call | solution.py:178
  11.8 0.0 collective-permute-done.3.refs_2_
  11.9 0.0 copy-start
  11.9 1.0 %copy-done = bf16[2,256,512]{2,1,0:T(8,128)(2,1)S(1)} copy-done((bf16[2,256,512]{2,1,0:T(8,128)(2,1)S(1)}, bf16[2,256,512]{2,1,0:T(8,128)(2,1)}, u32[]{:S(2)}) %copy-start) | copy-done | bytes 524312
  12.9 0.0 copy-start.3
  12.9 1.0 %copy-done.3 = f32[3,16,8,256]{3,2,1,0:T(8,128)S(1)} copy-done((f32[3,16,8,256]{3,2,1,0:T(8,128)S(1)}, f32[3,16,8,256]{3,2,1,0:T(8,128)}, u32[]{:S(2)}) %copy-start.3) | copy-done | bytes 393240
  13.9 2.8 %first_near.1 = (f32[3,17,2,6,8,128]{5,4,3,2,1,0:T(8,128)S(1)}, f32[128,512]{1,0:T(8,128)S(1)}, f32[128,512]{1,0:T(8,128)S(1)}, f32[128,512]{1,0:T(8,128)S(1)}, f32[128,512]{1,0:T(8,128)S(1)}) custom-call(s32[3072]{0:T(1024)S(1)} %bitcast.11, f32[3,16,8,256]{3,2,1,0:T(8,128)S(1)} %copy-done.3, f32[3,16,8,256]{3,2,1,0:T(8,128)S(1)} %collective-permute-done.3.refs_2_, ...), custom_call_target="tpu_custom_call" | custom-call | flops 1 | tf_op jit(solution)/shard_map/first_near/pallas_call | solution.py:351
  16.7 0.0 collective-permute-done.2.refs_0_
  16.7 0.1 collective-permute-start.8
  16.8 1.7 %collective-permute-start.7 = (f32[3,9,8,256]{3,2,1,0:T(8,128)S(1)}, f32[3,9,8,256]{3,2,1,0:T(8,128)S(1)}, u32[]{:S(2)}, u32[]{:S(2)}) collective-permute-start(f32[3,9,8,256]{3,2,1,0:T(8,128)S(1)} %collective-permute-done.2.refs_0_), channel_id=1, source_target_pairs={{0,12},{4,8},{8,4},{12,0},{1,13},{5,9},{9,5},{13,1},{2,14},{6,10},... | collective-permute-start | bytes 663560 | tf_op jit(solution)/shard_map/ppermute | solution.py:421
  18.5 0.3 add_spectra.2.refs_5_
  18.9 0.0 collective-permute-done.5.refs_1_
  18.9 0.0 collective-permute-done.4.refs_0_
  18.9 0.0 copy-done.1
  18.9 0.5 %add_spectra.3.refs_1_ = f32[3,17,2,6,8,128]{5,4,3,2,1,0:T(8,128)S(1)} custom-call(f32[3,9,8,256]{3,2,1,0:T(8,128)S(1)} %collective-permute-done.4.refs_0_, f32[3,7,8,256]{3,2,1,0:T(8,128)S(1)} %collective-permute-done.5.refs_1_, bf16[2,256,512]{2,1,0:T(8,128)(2,1)S(1)} %copy-done.1, ...), custom_call_target="tpu_custom_call", output_to_operand_aliasing={{}: (3, {})} | custom-call | flops 1 | tf_op jit(solution)/shard_map/add_spectra/pallas_call | solution.py:351
  19.4 0.0 collective-permute-done.1.refs_1_
  19.4 0.1 collective-permute-start.9
  19.5 1.4 %collective-permute-start.6 = (f32[3,7,8,256]{3,2,1,0:T(8,128)S(1)}, f32[3,7,8,256]{3,2,1,0:T(8,128)S(1)}, u32[]{:S(2)}, u32[]{:S(2)}) collective-permute-start(f32[3,7,8,256]{3,2,1,0:T(8,128)S(1)} %collective-permute-done.1.refs_1_), channel_id=1, source_target_pairs={{0,12},{4,8},{8,4},{12,0},{1,13},{5,9},{9,5},{13,1},{2,14},{6,10},... | collective-permute-start | bytes 516104 | tf_op jit(solution)/shard_map/ppermute | solution.py:421
  20.9 0.0 collective-permute-done.9.refs_3_
  20.9 0.0 collective-permute-done.8.refs_2_
  20.9 1.4 %near_sums.2 = (f32[3,17,2,6,8,128]{5,4,3,2,1,0:T(8,128)S(1)}, f32[128,512]{1,0:T(8,128)S(1)}) custom-call(s32[3072]{0:T(1024)S(1)} %bitcast.12, f32[3,7,8,256]{3,2,1,0:T(8,128)S(1)} %collective-permute-done.1.refs_1_, f32[3,9,8,256]{3,2,1,0:T(8,128)S(1)} %collective-permute-done.8.refs_2_, ...), custom_call_target="tpu_custom_call", output_to_operand_aliasing={{0}: (5, {}), {1}: (6, {})} | custom-call | flops 1 | tf_op jit(solution)/shard_map/near_sums/pallas_call | solution.py:351
  22.3 6.2 %collective-permute-start.11 = (f32[128,512]{1,0:T(8,128)S(1)}, f32[128,512]{1,0:T(8,128)S(1)}, u32[]{:S(2)}, u32[]{:S(2)}) collective-permute-start(f32[128,512]{1,0:T(8,128)S(1)} %get-tuple-element.96), channel_id=1, source_target_pairs={{0,1},{1,0},{2,3},{3,2},{4,5},{5,4},{6,7},{7,6},{8,9},{9,8},{10,11... | collective-permute-start | bytes 786440 | tf_op jit(solution)/shard_map/ppermute | solution.py:427
  28.5 1.4 %across_sums.6 = (f32[3,17,2,6,8,128]{5,4,3,2,1,0:T(8,128)S(1)}, f32[128,512]{1,0:T(8,128)S(1)}, f32[128,512]{1,0:T(8,128)S(1)}) custom-call(s32[3072]{0:T(1024)S(1)} %bitcast.13, f32[3,17,2,6,8,128]{5,4,3,2,1,0:T(8,128)S(1)} %add_spectra.3.refs_1_, ...), custom_call_target="tpu_custom_call", output_to_operand_aliasing={{0}: (1, {}), {1}: (2, {}), {2}: (3, {})} | custom-call | flops 1 | tf_op jit(solution)/shard_map/across_sums/pallas_call | solution.py:351
  29.9 0.0 copy-start.2
  29.9 0.0 collective-permute-done.7.refs_1_
  29.9 1.1 %near_sums.3 = (f32[3,17,2,6,8,128]{5,4,3,2,1,0:T(8,128)S(1)}, f32[128,512]{1,0:T(8,128)S(1)}) custom-call(s32[3072]{0:T(1024)S(1)} %bitcast.14, f32[3,9,8,256]{3,2,1,0:T(8,128)S(1)} %collective-permute-done.7.refs_1_, bf16[2,256,512]{2,1,0:T(8,128)(2,1)S(1)} %copy-done.1, ...), custom_call_target="tpu_custom_call", output_to_operand_aliasing={{0}: (3, {}), {1}: (4, {})} | custom-call | flops 1 | tf_op jit(solution)/shard_map/near_sums/pallas_call | solution.py:351
  31.0 0.0 collective-permute-done.6.refs_1_
  31.0 0.1 copy-done.2
  31.1 1.4 %across_sums.7 = (f32[3,17,2,6,8,128]{5,4,3,2,1,0:T(8,128)S(1)}, f32[128,512]{1,0:T(8,128)S(1)}) custom-call(s32[3072]{0:T(1024)S(1)} %bitcast.15, f32[3,7,8,256]{3,2,1,0:T(8,128)S(1)} %collective-permute-done.6.refs_1_, bf16[2,256,512]{2,1,0:T(8,128)(2,1)S(1)} %copy-done.1, ...), custom_call_target="tpu_custom_call", output_to_operand_aliasing={{0}: (4, {}), {1}: (5, {})} | custom-call | flops 1 | tf_op jit(solution)/shard_map/across_sums/pallas_call | solution.py:351
  32.6 1.9 %collective-permute-start.10 = (f32[128,512]{1,0:T(8,128)S(1)}, f32[128,512]{1,0:T(8,128)S(1)}, u32[]{:S(2)}, u32[]{:S(2)}) collective-permute-start(f32[128,512]{1,0:T(8,128)S(1)} %get-tuple-element.92), channel_id=1, source_target_pairs={{0,1},{1,0},{2,3},{3,2},{4,5},{5,4},{6,7},{7,6},{8,9},{9,8},{10,11... | collective-permute-start | bytes 786440 | tf_op jit(solution)/shard_map/ppermute | solution.py:427
  34.5 0.6 %slice.3 = s32[1,1]{1,0:T(1,128)} slice(s32[1,128]{1,0:T(1,128)S(1)} %get-tuple-element.61.refs_0_), slice={[0:1], [4:5]} | slice | bytes 8 | tf_op jit(solution)/shard_map/slice | solution.py:532
  35.7 2.4 %kept_sums.1 = (f32[3,17,2,6,8,128]{5,4,3,2,1,0:T(8,128)S(1)}, f32[128,512]{1,0:T(8,128)S(1)}, f32[128,512]{1,0:T(8,128)S(1)}) custom-call(s32[3072]{0:T(1024)S(1)} %bitcast.16, bf16[2,512,512]{2,1,0:T(8,128)(2,1)S(1)} %copy-done.2, ...), custom_call_target="tpu_custom_call", output_to_operand_aliasing={{0}: (2, {}), {1}: (3, {}), {2}: (4, {})} | custom-call | flops 1 | tf_op jit(solution)/shard_map/kept_sums/pallas_call | solution.py:351
  38.1 0.0 collective-permute-done.11.refs_3_
  38.1 1.1 %finish.2.refs_4_ = f32[256,512]{1,0:T(8,128)} custom-call(s32[1,128]{1,0:T(1,128)S(1)} %get-tuple-element.61.refs_0_, bf16[2,512,512]{2,1,0:T(8,128)(2,1)S(1)} %copy-done.2, f32[128,512]{1,0:T(8,128)S(1)} %get-tuple-element.97.refs_2_, f32[128,512]{1,0:T(8,128)S(1)} %collective-permute-done.11.refs_3_), custom_call_target="tpu_custom_call" | custom-call | flops 1 | bytes 1 | tf_op jit(solution)/shard_map/finish/pallas_call | solution.py:391
  39.2 2.5 %collective-permute-done.10.refs_3_ = f32[128,512]{1,0:T(8,128)S(1)} collective-permute-done((f32[128,512]{1,0:T(8,128)S(1)}, f32[128,512]{1,0:T(8,128)S(1)}, u32[]{:S(2)}, u32[]{:S(2)}) %collective-permute-start.10) | collective-permute-done | bytes 262176 | tf_op jit(solution)/shard_map/ppermute | solution.py:427
  41.7 0.8 %finish.3 = f32[256,512]{1,0:T(8,128)} custom-call(s32[1,128]{1,0:T(1,128)S(1)} %get-tuple-element.61.refs_0_, bf16[2,512,512]{2,1,0:T(8,128)(2,1)S(1)} %copy-done.2, f32[128,512]{1,0:T(8,128)S(1)} %get-tuple-element.91.refs_2_, f32[128,512]{1,0:T(8,128)S(1)} %collective-permute-done.10.refs_3_, ...), custom_call_target="tpu_custom_call", output_to_operand_aliasing={{}: (4, {})} | custom-call | flops 1 | bytes 1 | tf_op jit(solution)/shard_map/finish/pallas_call | solution.py:391
  (2 shorter events, 0.0 us)
Async XLA Ops:
  2.2 9.7 %collective-permute-start.3 = (f32[3,16,8,256]{3,2,1,0:T(8,128)}, f32[3,16,8,256]{3,2,1,0:T(8,128)S(1)}, u32[]{:S(2)}, u32[]{:S(2)}) collective-permute-start(f32[3,16,8,256]{3,2,1,0:T(8,128)} %get-tuple-element.65.refs_1_), channel_id=1, source_target_pairs={{0,4},{4,0},{8,12},{12,8},{1,5},{5,1},{9,13},{13,9},{2,6},{6,2},{1... | collective-permute-start | bytes 1179656 | tf_op jit(solution)/shard_map/ppermute | solution.py:418
  2.7 14.0 %collective-permute-start.2 = (f32[3,9,8,256]{3,2,1,0:T(8,128)}, f32[3,9,8,256]{3,2,1,0:T(8,128)S(1)}, u32[]{:S(2)}, u32[]{:S(2)}) collective-permute-start(f32[3,9,8,256]{3,2,1,0:T(8,128)} %get-tuple-element.64), channel_id=1, source_target_pairs={{0,3},{1,2},{2,1},{3,0},{4,7},{5,6},{6,5},{7,4},{8,11},{9,10},{10,... | collective-permute-start | bytes 663560 | tf_op jit(solution)/shard_map/ppermute | solution.py:424
  7.4 11.5 %collective-permute-start.4 = (f32[3,9,8,256]{3,2,1,0:T(8,128)}, f32[3,9,8,256]{3,2,1,0:T(8,128)S(1)}, u32[]{:S(2)}, u32[]{:S(2)}) collective-permute-start(f32[3,9,8,256]{3,2,1,0:T(8,128)} %get-tuple-element.64), channel_id=1, source_target_pairs={{0,12},{4,8},{8,4},{12,0},{1,13},{5,9},{9,5},{13,1},{2,14},{6,10},... | collective-permute-start | bytes 663560 | tf_op jit(solution)/shard_map/ppermute | solution.py:421
  8.6 10.3 %collective-permute-start.5 = (f32[3,7,8,256]{3,2,1,0:T(8,128)}, f32[3,7,8,256]{3,2,1,0:T(8,128)S(1)}, u32[]{:S(2)}, u32[]{:S(2)}) collective-permute-start(f32[3,7,8,256]{3,2,1,0:T(8,128)} %get-tuple-element.63), channel_id=1, source_target_pairs={{0,12},{4,8},{8,4},{12,0},{1,13},{5,9},{9,5},{13,1},{2,14},{6,10},... | collective-permute-start | bytes 516104 | tf_op jit(solution)/shard_map/ppermute | solution.py:421
  9.1 10.3 %collective-permute-start.1 = (f32[3,7,8,256]{3,2,1,0:T(8,128)}, f32[3,7,8,256]{3,2,1,0:T(8,128)S(1)}, u32[]{:S(2)}, u32[]{:S(2)}) collective-permute-start(f32[3,7,8,256]{3,2,1,0:T(8,128)} %get-tuple-element.63), channel_id=1, source_target_pairs={{0,3},{1,2},{2,1},{3,0},{4,7},{5,6},{6,5},{7,4},{8,11},{9,10},{10,... | collective-permute-start | bytes 516104 | tf_op jit(solution)/shard_map/ppermute | solution.py:424
  9.2 0.7 %copy-start.4 = (s32[4,1,256,2]{2,3,1,0:T(2,128)S(1)}, s32[4,1,256,2]{2,3,1,0:T(2,128)}, u32[]{:S(2)}) copy-start(s32[4,1,256,2]{2,3,1,0:T(2,128)} %param.14) | copy-start | bytes 24580
  9.9 0.7 %copy-start.5 = (s32[4,4]{1,0:T(4,128)S(1)}, s32[4,4]{1,0:T(4,128)}, u32[]{:S(2)}) copy-start(s32[4,4]{1,0:T(4,128)} %refs_0_.1) | copy-start | bytes 196
  10.6 0.7 %copy-start.6 = (s32[4]{0:T(128)S(1)}, s32[4]{0:T(128)}, u32[]{:S(2)}) copy-start(s32[4]{0:T(128)} %refs_1_.5) | copy-start | bytes 52
  11.9 1.0 %copy-start = (bf16[2,256,512]{2,1,0:T(8,128)(2,1)S(1)}, bf16[2,256,512]{2,1,0:T(8,128)(2,1)}, u32[]{:S(2)}) copy-start(bf16[2,256,512]{2,1,0:T(8,128)(2,1)} %constant.7.clone.refs_3_.refs_1_.refs_2_.refs_4_) | copy-start | bytes 1572868
  12.9 1.0 %copy-start.3 = (f32[3,16,8,256]{3,2,1,0:T(8,128)S(1)}, f32[3,16,8,256]{3,2,1,0:T(8,128)}, u32[]{:S(2)}) copy-start(f32[3,16,8,256]{3,2,1,0:T(8,128)} %get-tuple-element.65.refs_1_) | copy-start | bytes 1179652
  13.9 5.0 %copy-start.1 = (bf16[2,256,512]{2,1,0:T(8,128)(2,1)S(1)}, bf16[2,256,512]{2,1,0:T(8,128)(2,1)}, u32[]{:S(2)}) copy-start(bf16[2,256,512]{2,1,0:T(8,128)(2,1)} %constant.7.clone.refs_3_.refs_1_.refs_2_.refs_4_) | copy-start | bytes 1572868
  16.7 4.2 %collective-permute-start.8 = (f32[3,9,8,256]{3,2,1,0:T(8,128)S(1)}, f32[3,9,8,256]{3,2,1,0:T(8,128)S(1)}, u32[]{:S(2)}, u32[]{:S(2)}) collective-permute-start(f32[3,9,8,256]{3,2,1,0:T(8,128)S(1)} %collective-permute-done.2.refs_0_), channel_id=1, source_target_pairs={{0,4},{4,0},{8,12},{12,8},{1,5},{5,1},{9,13},{13,9},{2,6},{6,2},{1... | collective-permute-start | bytes 663560 | tf_op jit(solution)/shard_map/ppermute | solution.py:418
  16.8 13.1 %collective-permute-start.7 = (f32[3,9,8,256]{3,2,1,0:T(8,128)S(1)}, f32[3,9,8,256]{3,2,1,0:T(8,128)S(1)}, u32[]{:S(2)}, u32[]{:S(2)}) collective-permute-start(f32[3,9,8,256]{3,2,1,0:T(8,128)S(1)} %collective-permute-done.2.refs_0_), channel_id=1, source_target_pairs={{0,12},{4,8},{8,4},{12,0},{1,13},{5,9},{9,5},{13,1},{2,14},{6,10},... | collective-permute-start | bytes 663560 | tf_op jit(solution)/shard_map/ppermute | solution.py:421
  19.4 1.5 %collective-permute-start.9 = (f32[3,7,8,256]{3,2,1,0:T(8,128)S(1)}, f32[3,7,8,256]{3,2,1,0:T(8,128)S(1)}, u32[]{:S(2)}, u32[]{:S(2)}) collective-permute-start(f32[3,7,8,256]{3,2,1,0:T(8,128)S(1)} %collective-permute-done.1.refs_1_), channel_id=1, source_target_pairs={{0,4},{4,0},{8,12},{12,8},{1,5},{5,1},{9,13},{13,9},{2,6},{6,2},{1... | collective-permute-start | bytes 516104 | tf_op jit(solution)/shard_map/ppermute | solution.py:418
  19.5 11.5 %collective-permute-start.6 = (f32[3,7,8,256]{3,2,1,0:T(8,128)S(1)}, f32[3,7,8,256]{3,2,1,0:T(8,128)S(1)}, u32[]{:S(2)}, u32[]{:S(2)}) collective-permute-start(f32[3,7,8,256]{3,2,1,0:T(8,128)S(1)} %collective-permute-done.1.refs_1_), channel_id=1, source_target_pairs={{0,12},{4,8},{8,4},{12,0},{1,13},{5,9},{9,5},{13,1},{2,14},{6,10},... | collective-permute-start | bytes 516104 | tf_op jit(solution)/shard_map/ppermute | solution.py:421
  22.3 15.8 %collective-permute-start.11 = (f32[128,512]{1,0:T(8,128)S(1)}, f32[128,512]{1,0:T(8,128)S(1)}, u32[]{:S(2)}, u32[]{:S(2)}) collective-permute-start(f32[128,512]{1,0:T(8,128)S(1)} %get-tuple-element.96), channel_id=1, source_target_pairs={{0,1},{1,0},{2,3},{3,2},{4,5},{5,4},{6,7},{7,6},{8,9},{9,8},{10,11... | collective-permute-start | bytes 786440 | tf_op jit(solution)/shard_map/ppermute | solution.py:427
  29.9 1.2 %copy-start.2 = (bf16[2,512,512]{2,1,0:T(8,128)(2,1)S(1)}, bf16[2,512,512]{2,1,0:T(8,128)(2,1)}, u32[]{:S(2)}) copy-start(bf16[2,512,512]{2,1,0:T(8,128)(2,1)} %constant.8.clone.refs_3_.refs_1_) | copy-start | bytes 3145732
  32.6 9.2 %collective-permute-start.10 = (f32[128,512]{1,0:T(8,128)S(1)}, f32[128,512]{1,0:T(8,128)S(1)}, u32[]{:S(2)}, u32[]{:S(2)}) collective-permute-start(f32[128,512]{1,0:T(8,128)S(1)} %get-tuple-element.92), channel_id=1, source_target_pairs={{0,1},{1,0},{2,3},{3,2},{4,5},{5,4},{6,7},{7,6},{8,9},{9,8},{10,11... | collective-permute-start | bytes 786440 | tf_op jit(solution)/shard_map/ppermute | solution.py:427

commit v8 on v7

--- a/solution.py
+++ b/solution.py
@@ -523,14 +523,20 @@
         kept = early_kept + late_kept
         other, early_kept, late_kept = more_sums("kept_sums", [], [], jobs, other, kept, with_inverse=True)
 
-        def with_across(spectra, other, kept):
-            jobs = [(early_turns, (2,), blocks, 0, 2)]
-            _, *more = more_sums("across_sums", [], [], jobs, spectra, [])
-            _, more_kept, more_sent = more_sums("across_sums", [], [], jobs, other, more)
-            return kept + more_kept + swap_stations(more_sent)
-
-        many = order[0, rounds] > len(late_turns)
-        early_kept = lax.cond(many, with_across, lambda _, __, kept: kept, spectra, other, early_kept)
+        def with_across(count):
+            def add(spectra, other, kept):
+                jobs = [(early_turns, (2,), blocks, 0, 2)]
+                _, *more = more_sums("across_sums", [], [], jobs, spectra, [])
+                _, more_kept, more_sent = more_sums("across_sums", [], [], jobs, other, more)
+                split = (len(early_turns) - count) * all_pairs // length
+                received = jnp.pad(swap_stations(more_sent[split:]), ((split, 0), (0, 0)))
+                return kept + more_kept + received
+
+            return add
+
+        short = jnp.clip(order[0, rounds] - len(late_turns), 0, len(early_turns))
+        choices = [lambda _, __, kept: kept] + [with_across(count + 1) for count in range(len(early_turns))]
+        early_kept = lax.switch(short, choices, spectra, other, early_kept)
         early, late = [early_kept, early_received], [late_kept, late_received]
     else:
         other, late_sent = add_sent("across_sums", traces, places, late_turns, (2,), other, late_sent)

time: 42.9 us -> 42.8 us (level)
  transfers between devices with their start and end apart: 11 -> 11, of which waited for: 1 -> 2; matrix products, arithmetic and copies ran while one was open for 1% -> 1% of each run, Pallas kernels for 30% -> 31%
where the time goes in v8:
time: 42.8 us; the launch traced here: 42.4 us
  starting transfers between devices  18.1 us (42%)
  Pallas kernels  16 us (37%)
  local copies, waits for them, and re-layouts  4.76 us (11%)
  waiting for transfers between devices  2.71 us (6%)
  between operations  0.84 us (2%)
    pallas_call x8, Pallas kernels, call_kernel(): pl.pallas_call(kernel, out_shape=shapes, in_specs=in_specs, out_specs=out...  11.3 us
    ppermute x2, starting transfers between devices, swap_stations(): return lax.ppermute(value, 'station', [(i, i ^ 1) for i in range(length)])  8.12 us
    ppermute x2, starting transfers between devices, to_mirror(): lax.ppermute(value, 'station', [(i, length - 1 - i) for i in range(length)])  4.77 us
    ppermute x4, starting transfers between devices, to_across(): lax.ppermute(value, 'cluster', [(i, (i + 1 if i % 2 else i - 1) % cluster...  4.48 us
    unnamed x14, local copies, waits for them, and re-layouts  4.18 us
    ppermute x2, waiting for transfers between devices, swap_stations(): return lax.ppermute(value, 'station', [(i, i ^ 1) for i in range(length)])  2.36 us
    pallas_call x1, Pallas kernels, prepare(): pl.pallas_call(prepare_kernel, out_shape=[jax.ShapeDtypeStruct(shape, F32...  2.15 us
    pallas_call x2, Pallas kernels, finish(): pl.pallas_call(lambda *refs: finish_kernel(turns, invert, len(terms), *re...  1.94 us
  transfers between devices with their start and end apart: 11, of which 2 were waited for; matrix products, arithmetic and copies ran while one was open for 1% of the time, Pallas kernels for 31%

profile of v8, /device:TPU:0, one launch (start us, length us, event | category | flops | bytes accessed | tf_op | source)
XLA Modules:
  0.0 42.4 jit_solution(1239641367051107089)
XLA Ops:
  0.0 2.1 %prepare.1 = (f32[3,16,8,256]{3,2,1,0:T(8,128)}, f32[3,9,8,256]{3,2,1,0:T(8,128)}, f32[3,7,8,256]{3,2,1,0:T(8,128)}) custom-call(f32[16,2,3,4,256]{4,3,2,1,0:T(4,128)} %bitcast.19, s32[4,32]{1,0:T(4,128)} %bitcast.20, f32[16]{0:T(128)} %weight_hbm.1), custom_call_target="tpu_custom_call" | custom-call | tf_op jit(solution)/shard_map/prepare/pallas_call | solution.py:124
  2.2 0.5 %collective-permute-start.4 = (f32[3,16,8,256]{3,2,1,0:T(8,128)}, f32[3,16,8,256]{3,2,1,0:T(8,128)S(1)}, u32[]{:S(2)}, u32[]{:S(2)}) collective-permute-start(f32[3,16,8,256]{3,2,1,0:T(8,128)} %get-tuple-element.82.refs_1_), channel_id=1, source_target_pairs={{0,4},{4,0},{8,12},{12,8},{1,5},{5,1},{9,13},{13,9},{2,6},{6,2},{1... | collective-permute-start | bytes 1179656 | tf_op jit(solution)/shard_map/ppermute | solution.py:418
  2.7 4.7 %collective-permute-start.3 = (f32[3,9,8,256]{3,2,1,0:T(8,128)}, f32[3,9,8,256]{3,2,1,0:T(8,128)S(1)}, u32[]{:S(2)}, u32[]{:S(2)}) collective-permute-start(f32[3,9,8,256]{3,2,1,0:T(8,128)} %get-tuple-element.81), channel_id=1, source_target_pairs={{0,3},{1,2},{2,1},{3,0},{4,7},{5,6},{6,5},{7,4},{8,11},{9,10},{10,... | collective-permute-start | bytes 663560 | tf_op jit(solution)/shard_map/ppermute | solution.py:424
  7.4 1.3 %collective-permute-start.5 = (f32[3,9,8,256]{3,2,1,0:T(8,128)}, f32[3,9,8,256]{3,2,1,0:T(8,128)S(1)}, u32[]{:S(2)}, u32[]{:S(2)}) collective-permute-start(f32[3,9,8,256]{3,2,1,0:T(8,128)} %get-tuple-element.81), channel_id=1, source_target_pairs={{0,12},{4,8},{8,4},{12,0},{1,13},{5,9},{9,5},{13,1},{2,14},{6,10},... | collective-permute-start | bytes 663560 | tf_op jit(solution)/shard_map/ppermute | solution.py:421
  8.6 0.5 %collective-permute-start.6 = (f32[3,7,8,256]{3,2,1,0:T(8,128)}, f32[3,7,8,256]{3,2,1,0:T(8,128)S(1)}, u32[]{:S(2)}, u32[]{:S(2)}) collective-permute-start(f32[3,7,8,256]{3,2,1,0:T(8,128)} %get-tuple-element.80), channel_id=1, source_target_pairs={{0,12},{4,8},{8,4},{12,0},{1,13},{5,9},{9,5},{13,1},{2,14},{6,10},... | collective-permute-start | bytes 516104 | tf_op jit(solution)/shard_map/ppermute | solution.py:421
  9.1 0.1 collective-permute-start.2
  9.2 0.0 copy-start.4
  9.2 0.7 %copy-done.4 = s32[4,1,256,2]{2,3,1,0:T(2,128)S(1)} copy-done((s32[4,1,256,2]{2,3,1,0:T(2,128)S(1)}, s32[4,1,256,2]{2,3,1,0:T(2,128)}, u32[]{:S(2)}) %copy-start.4) | copy-done | bytes 8216
  9.9 0.0 copy-start.5
  9.9 0.7 %copy-done.5 = s32[4,4]{1,0:T(4,128)S(1)} copy-done((s32[4,4]{1,0:T(4,128)S(1)}, s32[4,4]{1,0:T(4,128)}, u32[]{:S(2)}) %copy-start.5) | copy-done | bytes 88
  10.6 0.0 copy-start.6
  10.6 0.7 %copy-done.6 = s32[4]{0:T(128)S(1)} copy-done((s32[4]{0:T(128)S(1)}, s32[4]{0:T(128)}, u32[]{:S(2)}) %copy-start.6) | copy-done | bytes 40
  11.2 0.6 %pair_index.1 = (s32[24,128]{1,0:T(8,128)S(1)}, s32[1,128]{1,0:T(1,128)S(1)}) custom-call(s32[4,4]{1,0:T(4,128)S(1)} %copy-done.5, s32[4]{0:T(128)S(1)} %copy-done.6, s32[4,1,2,256]{3,2,1,0:T(2,128)S(1)} %bitcast.10), custom_call_target="tpu_custom_call" | custom-call | tf_op jit(solution)/shard_map/pair_index/pallas_call | solution.py:178
  11.8 0.0 collective-permute-done.4.refs_2_
  11.9 0.0 copy-start
  11.9 1.0 %copy-done = bf16[2,256,512]{2,1,0:T(8,128)(2,1)S(1)} copy-done((bf16[2,256,512]{2,1,0:T(8,128)(2,1)S(1)}, bf16[2,256,512]{2,1,0:T(8,128)(2,1)}, u32[]{:S(2)}) %copy-start) | copy-done | bytes 524312
  12.9 0.0 copy-start.3
  12.9 1.0 %copy-done.3 = f32[3,16,8,256]{3,2,1,0:T(8,128)S(1)} copy-done((f32[3,16,8,256]{3,2,1,0:T(8,128)S(1)}, f32[3,16,8,256]{3,2,1,0:T(8,128)}, u32[]{:S(2)}) %copy-start.3) | copy-done | bytes 393240
  13.9 2.8 %first_near.1 = (f32[3,17,2,6,8,128]{5,4,3,2,1,0:T(8,128)S(1)}, f32[128,512]{1,0:T(8,128)S(1)}, f32[128,512]{1,0:T(8,128)S(1)}, f32[128,512]{1,0:T(8,128)S(1)}, f32[128,512]{1,0:T(8,128)S(1)}) custom-call(s32[3072]{0:T(1024)S(1)} %bitcast.11, f32[3,16,8,256]{3,2,1,0:T(8,128)S(1)} %copy-done.3, f32[3,16,8,256]{3,2,1,0:T(8,128)S(1)} %collective-permute-done.4.refs_2_, ...), custom_call_target="tpu_custom_call" | custom-call | flops 1 | tf_op jit(solution)/shard_map/first_near/pallas_call | solution.py:351
  16.7 0.0 collective-permute-done.3.refs_0_
  16.7 0.1 collective-permute-start.9
  16.8 1.3 %collective-permute-start.8 = (f32[3,9,8,256]{3,2,1,0:T(8,128)S(1)}, f32[3,9,8,256]{3,2,1,0:T(8,128)S(1)}, u32[]{:S(2)}, u32[]{:S(2)}) collective-permute-start(f32[3,9,8,256]{3,2,1,0:T(8,128)S(1)} %collective-permute-done.3.refs_0_), channel_id=1, source_target_pairs={{0,12},{4,8},{8,4},{12,0},{1,13},{5,9},{9,5},{13,1},{2,14},{6,10},... | collective-permute-start | bytes 663560 | tf_op jit(solution)/shard_map/ppermute | solution.py:421
  18.0 0.3 add_spectra.2.refs_5_
  18.4 0.3 collective-permute-done.6.refs_1_
  18.7 0.0 collective-permute-done.5.refs_0_
  18.7 0.0 copy-done.1
  18.7 0.5 %add_spectra.3.refs_1_ = f32[3,17,2,6,8,128]{5,4,3,2,1,0:T(8,128)S(1)} custom-call(f32[3,9,8,256]{3,2,1,0:T(8,128)S(1)} %collective-permute-done.5.refs_0_, f32[3,7,8,256]{3,2,1,0:T(8,128)S(1)} %collective-permute-done.6.refs_1_, bf16[2,256,512]{2,1,0:T(8,128)(2,1)S(1)} %copy-done.1, ...), custom_call_target="tpu_custom_call", output_to_operand_aliasing={{}: (3, {})} | custom-call | flops 1 | tf_op jit(solution)/shard_map/add_spectra/pallas_call | solution.py:351
  19.2 0.0 collective-permute-done.2.refs_1_
  19.2 0.2 collective-permute-start.10
  19.4 1.5 %collective-permute-start.7 = (f32[3,7,8,256]{3,2,1,0:T(8,128)S(1)}, f32[3,7,8,256]{3,2,1,0:T(8,128)S(1)}, u32[]{:S(2)}, u32[]{:S(2)}) collective-permute-start(f32[3,7,8,256]{3,2,1,0:T(8,128)S(1)} %collective-permute-done.2.refs_1_), channel_id=1, source_target_pairs={{0,12},{4,8},{8,4},{12,0},{1,13},{5,9},{9,5},{13,1},{2,14},{6,10},... | collective-permute-start | bytes 516104 | tf_op jit(solution)/shard_map/ppermute | solution.py:421
  20.9 0.0 collective-permute-done.10.refs_3_
  20.9 0.0 collective-permute-done.9.refs_2_
  20.9 1.4 %near_sums.2 = (f32[3,17,2,6,8,128]{5,4,3,2,1,0:T(8,128)S(1)}, f32[128,512]{1,0:T(8,128)S(1)}) custom-call(s32[3072]{0:T(1024)S(1)} %bitcast.12, f32[3,7,8,256]{3,2,1,0:T(8,128)S(1)} %collective-permute-done.2.refs_1_, f32[3,9,8,256]{3,2,1,0:T(8,128)S(1)} %collective-permute-done.9.refs_2_, ...), custom_call_target="tpu_custom_call", output_to_operand_aliasing={{0}: (5, {}), {1}: (6, {})} | custom-call | flops 1 | tf_op jit(solution)/shard_map/near_sums/pallas_call | solution.py:351
  22.3 6.2 %collective-permute-start.12 = (f32[128,512]{1,0:T(8,128)S(1)}, f32[128,512]{1,0:T(8,128)S(1)}, u32[]{:S(2)}, u32[]{:S(2)}) collective-permute-start(f32[128,512]{1,0:T(8,128)S(1)} %get-tuple-element.113), channel_id=1, source_target_pairs={{0,1},{1,0},{2,3},{3,2},{4,5},{5,4},{6,7},{7,6},{8,9},{9,8},{10,11... | collective-permute-start | bytes 786440 | tf_op jit(solution)/shard_map/ppermute | solution.py:427
  28.5 1.4 %across_sums.10 = (f32[3,17,2,6,8,128]{5,4,3,2,1,0:T(8,128)S(1)}, f32[128,512]{1,0:T(8,128)S(1)}, f32[128,512]{1,0:T(8,128)S(1)}) custom-call(s32[3072]{0:T(1024)S(1)} %bitcast.13, f32[3,17,2,6,8,128]{5,4,3,2,1,0:T(8,128)S(1)} %add_spectra.3.refs_1_, ...), custom_call_target="tpu_custom_call", output_to_operand_aliasing={{0}: (1, {}), {1}: (2, {}), {2}: (3, {})} | custom-call | flops 1 | tf_op jit(solution)/shard_map/across_sums/pallas_call | solution.py:351
  29.9 0.0 copy-start.2
  29.9 0.0 collective-permute-done.8.refs_1_
  29.9 1.1 %near_sums.3 = (f32[3,17,2,6,8,128]{5,4,3,2,1,0:T(8,128)S(1)}, f32[128,512]{1,0:T(8,128)S(1)}) custom-call(s32[3072]{0:T(1024)S(1)} %bitcast.14, f32[3,9,8,256]{3,2,1,0:T(8,128)S(1)} %collective-permute-done.8.refs_1_, bf16[2,256,512]{2,1,0:T(8,128)(2,1)S(1)} %copy-done.1, ...), custom_call_target="tpu_custom_call", output_to_operand_aliasing={{0}: (3, {}), {1}: (4, {})} | custom-call | flops 1 | tf_op jit(solution)/shard_map/near_sums/pallas_call | solution.py:351
  31.0 0.0 collective-permute-done.7.refs_1_
  31.0 0.1 copy-done.2
  31.1 1.5 %across_sums.11 = (f32[3,17,2,6,8,128]{5,4,3,2,1,0:T(8,128)S(1)}, f32[128,512]{1,0:T(8,128)S(1)}) custom-call(s32[3072]{0:T(1024)S(1)} %bitcast.15, f32[3,7,8,256]{3,2,1,0:T(8,128)S(1)} %collective-permute-done.7.refs_1_, bf16[2,256,512]{2,1,0:T(8,128)(2,1)S(1)} %copy-done.1, ...), custom_call_target="tpu_custom_call", output_to_operand_aliasing={{0}: (4, {}), {1}: (5, {})} | custom-call | flops 1 | tf_op jit(solution)/shard_map/across_sums/pallas_call | solution.py:351
  32.6 1.9 %collective-permute-start.11 = (f32[128,512]{1,0:T(8,128)S(1)}, f32[128,512]{1,0:T(8,128)S(1)}, u32[]{:S(2)}, u32[]{:S(2)}) collective-permute-start(f32[128,512]{1,0:T(8,128)S(1)} %get-tuple-element.109), channel_id=1, source_target_pairs={{0,1},{1,0},{2,3},{3,2},{4,5},{5,4},{6,7},{7,6},{8,9},{9,8},{10,11... | collective-permute-start | bytes 786440 | tf_op jit(solution)/shard_map/ppermute | solution.py:427
  34.5 0.6 %slice.6 = s32[1,1]{1,0:T(1,128)} slice(s32[1,128]{1,0:T(1,128)S(1)} %get-tuple-element.78.refs_0_), slice={[0:1], [4:5]} | slice | bytes 8 | tf_op jit(solution)/shard_map/slice | solution.py:537
  35.7 2.4 %kept_sums.1 = (f32[3,17,2,6,8,128]{5,4,3,2,1,0:T(8,128)S(1)}, f32[128,512]{1,0:T(8,128)S(1)}, f32[128,512]{1,0:T(8,128)S(1)}) custom-call(s32[3072]{0:T(1024)S(1)} %bitcast.16, bf16[2,512,512]{2,1,0:T(8,128)(2,1)S(1)} %copy-done.2, ...), custom_call_target="tpu_custom_call", output_to_operand_aliasing={{0}: (2, {}), {1}: (3, {}), {2}: (4, {})} | custom-call | flops 1 | tf_op jit(solution)/shard_map/kept_sums/pallas_call | solution.py:351
  38.1 0.0 collective-permute-done.12.refs_3_
  38.1 1.1 %finish.2.refs_4_ = f32[256,512]{1,0:T(8,128)} custom-call(s32[1,128]{1,0:T(1,128)S(1)} %get-tuple-element.78.refs_0_, bf16[2,512,512]{2,1,0:T(8,128)(2,1)S(1)} %copy-done.2, f32[128,512]{1,0:T(8,128)S(1)} %get-tuple-element.114.refs_2_, f32[128,512]{1,0:T(8,128)S(1)} %collective-permute-done.12.refs_3_), custom_call_target="tpu_custom_call" | custom-call | flops 1 | bytes 1 | tf_op jit(solution)/shard_map/finish/pallas_call | solution.py:391
  39.2 2.4 %collective-permute-done.11.refs_3_ = f32[128,512]{1,0:T(8,128)S(1)} collective-permute-done((f32[128,512]{1,0:T(8,128)S(1)}, f32[128,512]{1,0:T(8,128)S(1)}, u32[]{:S(2)}, u32[]{:S(2)}) %collective-permute-start.11) | collective-permute-done | bytes 262176 | tf_op jit(solution)/shard_map/ppermute | solution.py:427
  41.6 0.8 %finish.3 = f32[256,512]{1,0:T(8,128)} custom-call(s32[1,128]{1,0:T(1,128)S(1)} %get-tuple-element.78.refs_0_, bf16[2,512,512]{2,1,0:T(8,128)(2,1)S(1)} %copy-done.2, f32[128,512]{1,0:T(8,128)S(1)} %get-tuple-element.108.refs_2_, f32[128,512]{1,0:T(8,128)S(1)} %collective-permute-done.11.refs_3_, ...), custom_call_target="tpu_custom_call", output_to_operand_aliasing={{}: (4, {})} | custom-call | flops 1 | bytes 1 | tf_op jit(solution)/shard_map/finish/pallas_call | solution.py:391
  (2 shorter events, 0.0 us)
Async XLA Ops:
  2.2 9.7 %collective-permute-start.4 = (f32[3,16,8,256]{3,2,1,0:T(8,128)}, f32[3,16,8,256]{3,2,1,0:T(8,128)S(1)}, u32[]{:S(2)}, u32[]{:S(2)}) collective-permute-start(f32[3,16,8,256]{3,2,1,0:T(8,128)} %get-tuple-element.82.refs_1_), channel_id=1, source_target_pairs={{0,4},{4,0},{8,12},{12,8},{1,5},{5,1},{9,13},{13,9},{2,6},{6,2},{1... | collective-permute-start | bytes 1179656 | tf_op jit(solution)/shard_map/ppermute | solution.py:418
  2.7 14.0 %collective-permute-start.3 = (f32[3,9,8,256]{3,2,1,0:T(8,128)}, f32[3,9,8,256]{3,2,1,0:T(8,128)S(1)}, u32[]{:S(2)}, u32[]{:S(2)}) collective-permute-start(f32[3,9,8,256]{3,2,1,0:T(8,128)} %get-tuple-element.81), channel_id=1, source_target_pairs={{0,3},{1,2},{2,1},{3,0},{4,7},{5,6},{6,5},{7,4},{8,11},{9,10},{10,... | collective-permute-start | bytes 663560 | tf_op jit(solution)/shard_map/ppermute | solution.py:424
  7.4 11.4 %collective-permute-start.5 = (f32[3,9,8,256]{3,2,1,0:T(8,128)}, f32[3,9,8,256]{3,2,1,0:T(8,128)S(1)}, u32[]{:S(2)}, u32[]{:S(2)}) collective-permute-start(f32[3,9,8,256]{3,2,1,0:T(8,128)} %get-tuple-element.81), channel_id=1, source_target_pairs={{0,12},{4,8},{8,4},{12,0},{1,13},{5,9},{9,5},{13,1},{2,14},{6,10},... | collective-permute-start | bytes 663560 | tf_op jit(solution)/shard_map/ppermute | solution.py:421
  8.6 10.1 %collective-permute-start.6 = (f32[3,7,8,256]{3,2,1,0:T(8,128)}, f32[3,7,8,256]{3,2,1,0:T(8,128)S(1)}, u32[]{:S(2)}, u32[]{:S(2)}) collective-permute-start(f32[3,7,8,256]{3,2,1,0:T(8,128)} %get-tuple-element.80), channel_id=1, source_target_pairs={{0,12},{4,8},{8,4},{12,0},{1,13},{5,9},{9,5},{13,1},{2,14},{6,10},... | collective-permute-start | bytes 516104 | tf_op jit(solution)/shard_map/ppermute | solution.py:421
  9.1 10.1 %collective-permute-start.2 = (f32[3,7,8,256]{3,2,1,0:T(8,128)}, f32[3,7,8,256]{3,2,1,0:T(8,128)S(1)}, u32[]{:S(2)}, u32[]{:S(2)}) collective-permute-start(f32[3,7,8,256]{3,2,1,0:T(8,128)} %get-tuple-element.80), channel_id=1, source_target_pairs={{0,3},{1,2},{2,1},{3,0},{4,7},{5,6},{6,5},{7,4},{8,11},{9,10},{10,... | collective-permute-start | bytes 516104 | tf_op jit(solution)/shard_map/ppermute | solution.py:424
  9.2 0.7 %copy-start.4 = (s32[4,1,256,2]{2,3,1,0:T(2,128)S(1)}, s32[4,1,256,2]{2,3,1,0:T(2,128)}, u32[]{:S(2)}) copy-start(s32[4,1,256,2]{2,3,1,0:T(2,128)} %param.15) | copy-start | bytes 24580
  9.9 0.7 %copy-start.5 = (s32[4,4]{1,0:T(4,128)S(1)}, s32[4,4]{1,0:T(4,128)}, u32[]{:S(2)}) copy-start(s32[4,4]{1,0:T(4,128)} %refs_0_.1) | copy-start | bytes 196
  10.6 0.7 %copy-start.6 = (s32[4]{0:T(128)S(1)}, s32[4]{0:T(128)}, u32[]{:S(2)}) copy-start(s32[4]{0:T(128)} %refs_1_.5) | copy-start | bytes 52
  11.9 1.0 %copy-start = (bf16[2,256,512]{2,1,0:T(8,128)(2,1)S(1)}, bf16[2,256,512]{2,1,0:T(8,128)(2,1)}, u32[]{:S(2)}) copy-start(bf16[2,256,512]{2,1,0:T(8,128)(2,1)} %constant.19.clone.refs_3_.refs_1_.refs_2_.refs_4_) | copy-start | bytes 1572868
  12.9 1.0 %copy-start.3 = (f32[3,16,8,256]{3,2,1,0:T(8,128)S(1)}, f32[3,16,8,256]{3,2,1,0:T(8,128)}, u32[]{:S(2)}) copy-start(f32[3,16,8,256]{3,2,1,0:T(8,128)} %get-tuple-element.82.refs_1_) | copy-start | bytes 1179652
  13.9 4.8 %copy-start.1 = (bf16[2,256,512]{2,1,0:T(8,128)(2,1)S(1)}, bf16[2,256,512]{2,1,0:T(8,128)(2,1)}, u32[]{:S(2)}) copy-start(bf16[2,256,512]{2,1,0:T(8,128)(2,1)} %constant.19.clone.refs_3_.refs_1_.refs_2_.refs_4_) | copy-start | bytes 1572868
  16.7 4.2 %collective-permute-start.9 = (f32[3,9,8,256]{3,2,1,0:T(8,128)S(1)}, f32[3,9,8,256]{3,2,1,0:T(8,128)S(1)}, u32[]{:S(2)}, u32[]{:S(2)}) collective-permute-start(f32[3,9,8,256]{3,2,1,0:T(8,128)S(1)} %collective-permute-done.3.refs_0_), channel_id=1, source_target_pairs={{0,4},{4,0},{8,12},{12,8},{1,5},{5,1},{9,13},{13,9},{2,6},{6,2},{1... | collective-permute-start | bytes 663560 | tf_op jit(solution)/shard_map/ppermute | solution.py:418
  16.8 13.1 %collective-permute-start.8 = (f32[3,9,8,256]{3,2,1,0:T(8,128)S(1)}, f32[3,9,8,256]{3,2,1,0:T(8,128)S(1)}, u32[]{:S(2)}, u32[]{:S(2)}) collective-permute-start(f32[3,9,8,256]{3,2,1,0:T(8,128)S(1)} %collective-permute-done.3.refs_0_), channel_id=1, source_target_pairs={{0,12},{4,8},{8,4},{12,0},{1,13},{5,9},{9,5},{13,1},{2,14},{6,10},... | collective-permute-start | bytes 663560 | tf_op jit(solution)/shard_map/ppermute | solution.py:421
  19.2 1.7 %collective-permute-start.10 = (f32[3,7,8,256]{3,2,1,0:T(8,128)S(1)}, f32[3,7,8,256]{3,2,1,0:T(8,128)S(1)}, u32[]{:S(2)}, u32[]{:S(2)}) collective-permute-start(f32[3,7,8,256]{3,2,1,0:T(8,128)S(1)} %collective-permute-done.2.refs_1_), channel_id=1, source_target_pairs={{0,4},{4,0},{8,12},{12,8},{1,5},{5,1},{9,13},{13,9},{2,6},{6,2},{1... | collective-permute-start | bytes 516104 | tf_op jit(solution)/shard_map/ppermute | solution.py:418
  19.4 11.6 %collective-permute-start.7 = (f32[3,7,8,256]{3,2,1,0:T(8,128)S(1)}, f32[3,7,8,256]{3,2,1,0:T(8,128)S(1)}, u32[]{:S(2)}, u32[]{:S(2)}) collective-permute-start(f32[3,7,8,256]{3,2,1,0:T(8,128)S(1)} %collective-permute-done.2.refs_1_), channel_id=1, source_target_pairs={{0,12},{4,8},{8,4},{12,0},{1,13},{5,9},{9,5},{13,1},{2,14},{6,10},... | collective-permute-start | bytes 516104 | tf_op jit(solution)/shard_map/ppermute | solution.py:421
  22.3 15.8 %collective-permute-start.12 = (f32[128,512]{1,0:T(8,128)S(1)}, f32[128,512]{1,0:T(8,128)S(1)}, u32[]{:S(2)}, u32[]{:S(2)}) collective-permute-start(f32[128,512]{1,0:T(8,128)S(1)} %get-tuple-element.113), channel_id=1, source_target_pairs={{0,1},{1,0},{2,3},{3,2},{4,5},{5,4},{6,7},{7,6},{8,9},{9,8},{10,11... | collective-permute-start | bytes 786440 | tf_op jit(solution)/shard_map/ppermute | solution.py:427
  29.9 1.2 %copy-start.2 = (bf16[2,512,512]{2,1,0:T(8,128)(2,1)S(1)}, bf16[2,512,512]{2,1,0:T(8,128)(2,1)}, u32[]{:S(2)}) copy-start(bf16[2,512,512]{2,1,0:T(8,128)(2,1)} %constant.20.clone.refs_3_.refs_1_) | copy-start | bytes 3145732
  32.6 9.0 %collective-permute-start.11 = (f32[128,512]{1,0:T(8,128)S(1)}, f32[128,512]{1,0:T(8,128)S(1)}, u32[]{:S(2)}, u32[]{:S(2)}) collective-permute-start(f32[128,512]{1,0:T(8,128)S(1)} %get-tuple-element.109), channel_id=1, source_target_pairs={{0,1},{1,0},{2,3},{3,2},{4,5},{5,4},{6,7},{7,6},{8,9},{9,8},{10,11... | collective-permute-start | bytes 786440 | tf_op jit(solution)/shard_map/ppermute | solution.py:427
